TPU v7x, 32 devices: a whole 2x2x4 slice. The times are simulated.
32 devices in a mesh: layers: 2 (over y), gr: 4 (over z), gc: 4 (over x, core).
Axes of the slice: x: 2, y: 2, z: 4, core: 2. Of those that a mesh axis runs over, the one named last changes fastest.
Arguments:
- acts: bfloat16 [1536, 8192], P('layers', 'gc'), parts along dimension 0, may hold values from -6 to 6
- grads: bfloat16 [1536, 28672], P(('layers', 'gc'), 'gr'), parts along dimension 0, may hold values from -6 to 6
- act_basis: bfloat16 [16384, 8192], P(('layers', 'gc'), 'gr'), parts along dimension 0, may hold values from -0.0625 to 0.0625
- grad_basis: bfloat16 [57344, 14336], P(('layers', 'gr'), 'gc'), parts along dimension 0, may hold values from -0.03125 to 0.03125
Outputs:
- correction: bfloat16 [16384, 14336], P(('layers', 'gr'), 'gc'), parts along dimension 0
There are 2 independent parts, one for each index of `layers`. A program takes and returns all parts, laid end to end along the dimension named above; each array names one. Nothing has to cross between parts.
All inputs are finite; a program needn't handle non-finite values.
Results may differ from a plain program's by a relative error of at most 0.0034.
Values may be sent and summed in bfloat16 or wider, within the bound.
No kernel may reach another device: no remote copies, remote signals or barrier semaphores. Data moves between devices by JAX's collectives and lax.ppermute only.
A program may use at most 192 MiB of HBM per device.

v0:
```python
import jax
import jax.numpy as jnp
from jax import lax
from jax.sharding import PartitionSpec as P


def token_product(left, right):
    return lax.dot_general(
        left, right, (((0,), (0,)), ((), ())), preferred_element_type=jnp.float32
    )


def shards(acts, grads, act_basis, grad_basis):
    token_count = acts.shape[0]
    grad_partial = jnp.dot(
        lax.all_gather(grads, "gc", axis=0, tiled=True),
        grad_basis,
        preferred_element_type=jnp.float32,
    )
    rows = acts
    act_share = lax.psum_scatter(
        jnp.dot(rows, act_basis, preferred_element_type=jnp.float32),
        "gc",
        scatter_dimension=0,
        tiled=True,
    )
    act_sq = (act_share * act_share).astype(jnp.bfloat16)
    grad_share = lax.psum_scatter(grad_partial, "gr", scatter_dimension=0, tiled=True)
    grad_sq = (grad_share * grad_share).astype(jnp.bfloat16)
    grad_all = lax.all_gather(grad_sq, "gr", axis=0, tiled=True)
    rows = grad_all
    total = token_product(lax.all_gather(act_sq, "gc", axis=0, tiled=True), rows)
    return (total / token_count).astype(jnp.bfloat16)


def solution(mesh):
    in_specs = (
        P("layers", "gc"),
        P(("layers", "gc"), "gr"),
        P(("layers", "gc"), "gr"),
        P(("layers", "gr"), "gc"),
    )
    out_specs = P(("layers", "gr"), "gc")
    return jax.shard_map(shards, mesh=mesh, in_specs=in_specs, out_specs=out_specs, check_vma=False)
```

profile of v0, /device:TPU:0, one launch (start us, length us, event | category | flops | bytes accessed | tf_op | source)
XLA Modules:
  0.0 494.1 jit_solution(14808227758963334825)
XLA Ops:
  6.5 0.0 copy-start
  6.5 0.0 all-gather.6.cloned.1.call-start
  6.5 0.7 all-gather.6.cloned.1.call-update
  7.3 0.0 reduce-scatter.3.cloned.1.call-start
  7.3 1.1 copy-done
  8.4 10.7 %fusion = f32[768,2048]{1,0:T(8,128)} fusion(bf16[768,2048]{1,0:T(8,128)(2,1)S(1)} %copy-done, bf16[2048,2048]{1,0:T(8,128)(2,1)} %param.6), kind=kOutput, calls=%fused_computation.3 | convolution fusion | flops 6442450944 | bytes 17825792 | tf_op jit(solution)/shard_map/dot_general | solution.py:22
  19.1 0.0 reduce-scatter.3.cloned.1.call-update
  19.1 0.0 reduce-scatter.5.cloned.1.call-start
  19.2 65.7 %all-gather.6.cloned.1.call-done = bf16[768,7168]{1,0:T(8,128)(2,1)} async-done(((bf16[192,7168]{1,0:T(8,128)(2,1)}), bf16[768,7168]{1,0:T(8,128)(2,1)}) %all-gather.6.cloned.1.call-update) | async-done | bytes 11010064 | tf_op jit(solution)/shard_map/all_gather | solution.py:16
  84.8 48.2 %fusion.1 = f32[768,3584]{1,0:T(8,128)} fusion(bf16[768,7168]{1,0:T(8,128)(2,1)} %all-gather.6.cloned.1.call-done, bf16[7168,3584]{1,0:T(8,128)(2,1)} %param.7), kind=kOutput, calls=%fused_computation.4 | convolution fusion | flops 39460012032 | bytes 73400320 | tf_op jit(solution)/shard_map/dot_general | solution.py:15
  133.1 0.0 reduce-scatter.5.cloned.1.call-update
  133.1 0.0 all-gather.4.cloned.1.call-start
  133.1 12.6 %reduce-scatter.3.cloned.1.call-done = f32[192,2048]{1,0:T(8,128)} async-done(((f32[768,2048]{1,0:T(8,128)}), f32[192,2048]{1,0:T(8,128)}) %reduce-scatter.3.cloned.1.call-update) | async-done | bytes 1572880 | tf_op jit(solution)/shard_map/reduce_scatter | solution.py:21
  145.7 2.5 multiply_convert_fusion.2
  148.3 0.0 all-gather.4.cloned.1.call-update
  148.3 0.2 all-gather.8.cloned.1.call-start
  148.5 186.2 %reduce-scatter.5.cloned.1.call-done = f32[192,3584]{1,0:T(8,128)} async-done(((f32[768,3584]{1,0:T(8,128)}), f32[192,3584]{1,0:T(8,128)}) %reduce-scatter.5.cloned.1.call-update) | async-done | bytes 2752528 | tf_op jit(solution)/shard_map/reduce_scatter | solution.py:28
  334.7 3.0 multiply_convert_fusion.1
  337.7 0.0 all-gather.8.cloned.1.call-update
  337.8 28.1 %all-gather.4.cloned.1.call-done = bf16[768,2048]{1,0:T(8,128)(2,1)} async-done(((bf16[192,2048]{1,0:T(8,128)(2,1)}), bf16[768,2048]{1,0:T(8,128)(2,1)}) %all-gather.4.cloned.1.call-update) | async-done | bytes 3145744 | tf_op jit(solution)/shard_map/all_gather | solution.py:32
  365.8 103.9 %all-gather.8.cloned.1.call-done = bf16[768,3584]{1,0:T(8,128)(2,1)} async-done(((bf16[192,3584]{1,0:T(8,128)(2,1)}), bf16[768,3584]{1,0:T(8,128)(2,1)}) %all-gather.8.cloned.1.call-update) | async-done | bytes 5505040 | tf_op jit(solution)/shard_map/all_gather | solution.py:30
  469.7 0.0 copy-start.1
  469.7 17.9 %multiply_convert_fusion = bf16[2048,3584]{1,0:T(8,128)(2,1)} fusion(bf16[768,2048]{1,0:T(8,128)(2,1)} %all-gather.4.cloned.1.call-done, bf16[768,3584]{1,0:T(8,128)(2,1)} %all-gather.8.cloned.1.call-done), kind=kOutput, calls=%fused_computation | convolution fusion | flops 11288969216 | bytes 23330816 | tf_op jit(solution)/shard_map/dot_general | solution.py:8
  487.6 0.0 copy-done.1
Async XLA Ops:
  6.5 1.9 copy-start
  6.5 78.3 %all-gather.6.cloned.1.call-start = ((), (), s32[]{:S(2)}) async-start(), calls=%async_computation.4 | async-start | bytes 13762560 | tf_op jit(solution)/shard_map/all_gather | solution.py:16
  7.3 138.5 %reduce-scatter.3.cloned.1.call-start = ((), (), s32[]{:S(2)}) async-start(), calls=%async_computation.2 | async-start | bytes 7864320 | tf_op jit(solution)/shard_map/reduce_scatter | solution.py:21
  19.1 315.6 %reduce-scatter.5.cloned.1.call-start = ((), (), s32[]{:S(2)}) async-start(), calls=%async_computation.5 | async-start | bytes 13762560 | tf_op jit(solution)/shard_map/reduce_scatter | solution.py:28
  133.1 232.7 %all-gather.4.cloned.1.call-start = ((), (), s32[]{:S(2)}) async-start(), calls=%async_computation.3 | async-start | bytes 3932160 | tf_op jit(solution)/shard_map/all_gather | solution.py:32
  148.3 321.5 %all-gather.8.cloned.1.call-start = ((), (), s32[]{:S(2)}) async-start(), calls=%async_computation.6 | async-start | bytes 6881280 | tf_op jit(solution)/shard_map/all_gather | solution.py:30
  469.7 17.9 %copy-start.1 = (bf16[768,2048]{1,0:T(8,128)(2,1)S(1)}, bf16[768,2048]{1,0:T(8,128)(2,1)}, u32[]{:S(2)}) copy-start(bf16[768,2048]{1,0:T(8,128)(2,1)} %param.4) | copy-start | bytes 9437188
Sparse Core Ops, SparseCore 0:
  8.9 75.8 all-gather.5
  87.3 58.3 reduce-scatter.2
  148.2 186.4 reduce-scatter.4
  336.2 29.5 all-gather.3
  367.3 102.3 all-gather.7
where the time goes:
time: 494 us
  waiting for transfers between devices  397 us (80%)
  matrix products  76.8 us (16%)
  between operations  13.1 us (3%)
  other arithmetic  5.52 us (1%)
    reduce_scatter x1, waiting for transfers between devices, shards(): lax.psum_scatter(grad_partial, 'gr', scatter_dimension=0, tiled=True)  186 us
    all_gather x1, waiting for transfers between devices, shards(): grad_all = lax.all_gather(grad_sq, 'gr', axis=0, tiled=True)  104 us
    all_gather x1, waiting for transfers between devices, shards(): lax.all_gather(grads, 'gc', axis=0, tiled=True)  65.7 us
    dot_general x1, matrix products, shards(): jnp.dot(lax.all_gather(grads, 'gc', axis=0, tiled=True), grad_basis, pref...  48.2 us
    all_gather x1, waiting for transfers between devices, shards(): lax.all_gather(act_sq, 'gc', axis=0, tiled=True)  28.1 us
    dot_general x1, matrix products, token_product(): lax.dot_general(left, right, (((0,), (0,)), ((), ())), preferred_element_...  17.9 us
    reduce_scatter x1, waiting for transfers between devices, shards(): lax.psum_scatter(jnp.dot(rows, act_basis, preferred_element_type=jnp.floa...  12.6 us
    dot_general x1, matrix products, shards(): jnp.dot(rows, act_basis, preferred_element_type=jnp.float32)  10.7 us
  transfers between devices with their start and end apart: 5, of which 5 were waited for; matrix products, arithmetic and copies ran while one was open for 13% of the time, Pallas kernels for 0%

commit v1 on v0

v1 whole, which is shorter than its diff:
```python
import functools

import jax
import jax.numpy as jnp
from jax import lax
from jax.experimental import pallas as pl
from jax.experimental.pallas import tpu as pltpu
from jax.sharding import PartitionSpec as P

BF16 = jnp.bfloat16
F32 = jnp.float32
MIB = 2**20


def token_product(left, right):
    return lax.dot_general(
        left, right, (((0,), (0,)), ((), ())), preferred_element_type=F32
    )


def gathered(acts, grads, act_basis, grad_basis):
    token_count = acts.shape[0]
    grad_partial = jnp.dot(
        lax.all_gather(grads, "gc", axis=0, tiled=True),
        grad_basis,
        preferred_element_type=F32,
    )
    act_share = lax.psum_scatter(
        jnp.dot(acts, act_basis, preferred_element_type=F32),
        "gc",
        scatter_dimension=0,
        tiled=True,
    )
    act_sq = (act_share * act_share).astype(BF16)
    grad_share = lax.psum_scatter(grad_partial, "gr", scatter_dimension=0, tiled=True)
    grad_sq = (grad_share * grad_share).astype(BF16)
    grad_all = lax.all_gather(grad_sq, "gr", axis=0, tiled=True)
    total = token_product(lax.all_gather(act_sq, "gc", axis=0, tiled=True), grad_all)
    return (total / token_count).astype(BF16)


FREE = pl.CostEstimate(flops=10**7, bytes_accessed=10**5, transcendentals=0)
VMEM = pl.BlockSpec(memory_space=pltpu.VMEM)
ANYWHERE = pl.BlockSpec(memory_space=pl.ANY)


def ordered(array, *after):
    def body(*refs):
        pass

    return pl.pallas_call(
        body,
        in_specs=[ANYWHERE] * (1 + len(after)),
        out_specs=ANYWHERE,
        out_shape=jax.ShapeDtypeStruct(array.shape, array.dtype),
        input_output_aliases={0: 0},
        cost_estimate=FREE,
        name="ordered",
    )(array, *after)


def whole(body, out_shape, flags, arrays, after, name, limit=16):
    def run(flags_ref, *refs):
        body(flags_ref, *refs[:len(arrays)], *refs[len(arrays) + len(after):])

    return pl.pallas_call(
        run,
        in_specs=[pl.BlockSpec(memory_space=pltpu.SMEM)] + [VMEM] * len(arrays) + [ANYWHERE] * len(after),
        out_specs=[VMEM] * len(out_shape),
        out_shape=[pltpu.VMEM(shape, BF16) for shape in out_shape],
        compiler_params=pltpu.CompilerParams(vmem_limit_bytes=limit * MIB),
        name=name,
    )(flags, *arrays, *after)


def add_body(flags, left, right, out):
    out[...] = (left[...].astype(F32) + right[...].astype(F32)).astype(BF16)


def square_body(flags, left, right, out):
    t = left[...].astype(F32) + right[...].astype(F32)
    out[...] = (t * t).astype(BF16)


def square_or_term_body(flags, left, right, term, out):
    @pl.when(flags[0] == 0)
    def _():
        square_body(flags, left, right, out)

    @pl.when(flags[0] == 1)
    def _():
        out[...] = term[...]


def add_pieces_body(flags, keep, *refs):
    taken, out = refs[:-1], refs[-1]
    width = taken[0].shape[1]
    for i, piece in enumerate(taken):
        at = slice(i * width, (i + 1) * width)
        out[:, at] = (keep[:, at].astype(F32) + piece[...].astype(F32)).astype(BF16)


def square_pieces_body(flags, left, right, *outs):
    width = outs[0].shape[1]
    for i, out in enumerate(outs):
        at = slice(i * width, (i + 1) * width)
        t = left[:, at].astype(F32) + right[:, at].astype(F32)
        out[...] = (t * t).astype(BF16)


def stack_body(flags, *refs):
    n = len(refs) // 2
    own, other, out = refs[:n], refs[n:2 * n], refs[2 * n]
    block, width = own[0].shape[0] // 2, own[0].shape[1]
    for chip in range(2):
        @pl.when(flags[1] == chip)
        def _(chip=chip):
            for i in range(n):
                at = slice(i * width, (i + 1) * width)
                for to, which in ((0, chip), (2, 1 - chip)):
                    rows = slice(which * block, (which + 1) * block)
                    out[to * block:(to + 1) * block, at] = own[i][rows]
                    out[(to + 1) * block:(to + 2) * block, at] = other[i][rows]


def split(array, pieces, after):
    rows, columns = array.shape
    width = columns // pieces

    def body(array_ref, *refs):
        outs, sems = refs[len(after):-1], refs[-1]
        copies = [
            pltpu.make_async_copy(array_ref.at[:, pl.ds(i * width, width)], out, sems.at[i])
            for i, out in enumerate(outs)
        ]
        for copy in copies:
            copy.start()
        for copy in copies:
            copy.wait()

    return pl.pallas_call(
        body,
        in_specs=[ANYWHERE] * (1 + len(after)),
        out_specs=[VMEM] * pieces,
        out_shape=[pltpu.VMEM((rows, width), BF16)] * pieces,
        scratch_shapes=[pltpu.SemaphoreType.DMA((pieces,))],
        compiler_params=pltpu.CompilerParams(vmem_limit_bytes=16 * MIB),
        cost_estimate=FREE,
        name="split",
    )(array, *after)


def join(top, bottom, after):
    count, depth = top.shape
    width = depth // len(bottom)

    def body(top_ref, *refs):
        out, sems = refs[len(bottom) + len(after):]
        copies = [pltpu.make_async_copy(top_ref, out.at[pl.ds(0, count)], sems.at[0])]
        for i in range(len(bottom)):
            to = out.at[pl.ds(count, count), pl.ds(i * width, width)]
            copies.append(pltpu.make_async_copy(refs[i], to, sems.at[1 + i]))
        for copy in copies:
            copy.start()
        for copy in copies:
            copy.wait()

    return pl.pallas_call(
        body,
        in_specs=[ANYWHERE] * (1 + len(bottom) + len(after)),
        out_specs=VMEM,
        out_shape=pltpu.VMEM((2 * count, depth), BF16),
        scratch_shapes=[pltpu.SemaphoreType.DMA((1 + len(bottom),))],
        compiler_params=pltpu.CompilerParams(vmem_limit_bytes=16 * MIB),
        cost_estimate=FREE,
        name="join",
    )(top, *bottom, *after)


def project(rows, basis, first, widths, after):
    count, depth = rows.shape
    step = 256
    steps = sum(widths) // step

    def body(rows_ref, basis_ref, *refs):
        outs = refs[len(after):]
        j = pl.program_id(0)
        part = jnp.dot(rows_ref[...], basis_ref[...], preferred_element_type=F32).astype(BF16)
        at = 0
        for out, width in zip(outs, widths):
            for h in range(width // step):
                @pl.when(j == at)
                def _(out=out, h=h):
                    out[:, h * step:(h + 1) * step] = part
                at += 1

    return pl.pallas_call(
        body,
        grid=(steps,),
        in_specs=[VMEM, pl.BlockSpec((depth, step), lambda j: (0, first // step + j))] + [ANYWHERE] * len(after),
        out_specs=[pl.BlockSpec((count, w), lambda j: (0, 0)) for w in widths],
        out_shape=[pltpu.VMEM((count, w), BF16) for w in widths],
        compiler_params=pltpu.CompilerParams(vmem_limit_bytes=16 * MIB),
        cost_estimate=FREE,
        name="project_grads",
    )(rows, basis, *after)


def project_acts(flags, acts, basis, after):
    count, depth = acts.shape
    width = basis.shape[1]
    block = count // 4
    step = 512
    steps = width // step

    def body(flags_ref, acts_ref, basis_ref, *refs):
        keep, *gives = refs[len(after):]
        j = pl.program_id(0)
        part = jnp.dot(acts_ref[...], basis_ref[...], preferred_element_type=F32).astype(BF16)
        for own in range(2):
            @pl.when(flags_ref[2] == own)
            def _(own=own):
                for chip in range(2):
                    to = slice(chip * block, (chip + 1) * block)
                    mine, other = 2 * chip + own, 2 * chip + 1 - own
                    keep[to, :] = part[mine * block:(mine + 1) * block]
                    for i, give in enumerate(gives):
                        @pl.when(j == i)
                        def _(give=give, to=to, other=other):
                            give[to, :] = part[other * block:(other + 1) * block]

    out = pl.BlockSpec((count // 2, step), lambda j, c: (0, j))
    return pl.pallas_call(
        body,
        grid_spec=pltpu.PrefetchScalarGridSpec(
            num_scalar_prefetch=1,
            grid=(steps,),
            in_specs=[
                pl.BlockSpec((count, depth), lambda j, c: (0, 0)),
                pl.BlockSpec((depth, step), lambda j, c: (0, j)),
            ]
            + [ANYWHERE] * len(after),
            out_specs=[out] + [pl.BlockSpec((count // 2, step), lambda j, c: (0, 0))] * steps,
        ),
        out_shape=[pltpu.VMEM((count // 2, width), BF16)] + [pltpu.VMEM((count // 2, step), BF16)] * steps,
        compiler_params=pltpu.CompilerParams(vmem_limit_bytes=24 * MIB),
        cost_estimate=FREE,
        name="project_acts",
    )(flags, pltpu.with_memory_space_constraint(acts, pltpu.HBM), pltpu.with_memory_space_constraint(basis, pltpu.HBM), *after)


def correct(flags, act_sq, pieces, first, total_width, result, after):
    tokens, height = act_sq.shape
    half, step = pieces[0][0].shape
    flat = [a for piece in pieces for a in piece]
    extra = list(after) if result is None else [result, *after]

    def body(flags_ref, act_ref, *refs):
        ins = refs[:len(flat)]
        out, done, grad_sq = refs[len(flat) + len(extra):]
        j = pl.program_id(0)

        @pl.when(j == 0)
        def _():
            done[...] = jnp.zeros_like(done)

        for i in range(len(pieces)):
            for from_other in range(2):
                @pl.when((j == i) & (flags_ref[0] == from_other))
                def _(i=i, from_other=from_other):
                    grad_sq[:half] = ins[4 * i + from_other][...]
                    grad_sq[half:] = ins[4 * i + 2 + from_other][...]
        total = token_product(act_ref[...], grad_sq[...])
        out[...] = (total * (1.0 / tokens)).astype(BF16)

    return pl.pallas_call(
        body,
        grid_spec=pltpu.PrefetchScalarGridSpec(
            num_scalar_prefetch=1,
            grid=(len(pieces),),
            in_specs=[VMEM] * (1 + len(flat)) + [ANYWHERE] * len(extra),
            out_specs=[pl.BlockSpec((height, step), lambda j, o: (0, first // step + j)), VMEM],
            scratch_shapes=[pltpu.VMEM((tokens, step), BF16)],
        ),
        out_shape=[pltpu.HBM((height, total_width), BF16), pltpu.VMEM((16, 128), BF16)],
        input_output_aliases={} if result is None else {2 + len(flat): 0},
        compiler_params=pltpu.CompilerParams(vmem_limit_bytes=24 * MIB),
        cost_estimate=FREE,
        name="correct",
    )(flags, act_sq, *flat, *extra)


CORES = [(0, 1), (1, 0), (2, 3), (3, 2)]
CHIPS = [(0, 2), (2, 0), (1, 3), (3, 1)]
OUTER = [(0, 1), (1, 0), (2, 3), (3, 2)]
INNER = [(1, 2), (2, 1), (5, 6), (6, 5), (0, 4), (4, 0), (3, 7), (7, 3)]


def lined(acts, grads, act_basis, grad_basis):
    chunk = 512
    lag = 3
    width = grad_basis.shape[1]
    half = width // chunk
    count = 2 * half
    place = lax.axis_index("gr")
    chip, core = lax.axis_index("gc") // 2, lax.axis_index("gc") % 2
    is_outer = (place == 0) | (place == 3)
    flags = jnp.stack([is_outer.astype(jnp.int32), chip.astype(jnp.int32), core.astype(jnp.int32)])

    near = lax.ppermute(grads, "gc", CORES)
    far = lax.ppermute(grads, "gc", CHIPS)

    last = ()
    parts, payloads, received, sums, others = [], [], [], [], []

    def project_next(rows, n):
        nonlocal last
        first = len(parts) * chunk % width
        parts.extend(project(rows, grad_basis, first, [chunk] * n, last))
        last = (parts[-1],)

    def send(k):
        nonlocal last
        j = k - lag
        if k < lag:
            payload = parts[k]
        else:
            shape = sums[j].shape
            if k < count:
                (payload,) = whole(
                    square_or_term_body, [shape], flags, [sums[j], others[j], parts[k]], last, "square"
                )
            else:
                (payload,) = whole(square_body, [shape], flags, [sums[j], others[j]], last, "square")
            last = (payload,)
        payloads.append(payload)
        received.append(lax.ppermute(payload, "gr", OUTER))

    def add(k):
        nonlocal last
        sums.extend(whole(add_body, [parts[k].shape], flags, [parts[k], received[k]], last, "add"))
        last = (sums[-1],)
        others.append(lax.ppermute(sums[-1], ("layers", "gr"), INNER))

    result = None
    done = 0

    def correct_next(n):
        nonlocal last, result, done
        pieces = [
            (payloads[j + lag], received[j + lag], payloads[half + j + lag], received[half + j + lag])
            for j in range(done, done + n)
        ]
        result, token = correct(flags, act_sq, pieces, done * chunk, width, result, last)
        last = (token,)
        done += n

    def small(body, shapes, arrays, name):
        nonlocal last
        out = whole(body, shapes, flags, arrays, last, name, 24)
        last = (out[-1],)
        return out

    rows = join(pltpu.with_memory_space_constraint(grads, pltpu.HBM), [near], last)
    last = (rows,)
    project_next(rows, 1)
    send(0)
    project_next(rows, 2)
    send(1)
    send(2)
    add(0)
    project_next(rows, 2)
    add(1)
    send(3)
    project_next(rows, 1)
    add(2)
    send(4)
    project_next(rows, 1)
    add(3)
    send(5)
    add(4)
    far_pieces = split(far, far.shape[1] // 1024, last)
    last = (far_pieces[-1],)
    far_near = [lax.ppermute(piece, "gc", CORES) for piece in far_pieces]
    keep, *give = project_acts(flags, acts, act_basis, last)
    last = (keep,)
    taken = [lax.ppermute(piece, "gc", CORES) for piece in give]
    send(6)
    rows = join(far, far_near, last)
    last = (rows,)
    project_next(rows, 1)
    add(5)
    (act,) = small(add_pieces_body, [keep.shape], [keep, *taken], "add")
    act_far = lax.ppermute(act, "gc", CHIPS)
    send(7)
    project_next(rows, 2)
    add(6)
    send(8)
    add(7)
    project_next(rows, 2)
    send(9)
    add(8)
    project_next(rows, 1)
    send(10)
    add(9)
    project_next(rows, 1)
    send(11)
    add(10)
    own = small(square_pieces_body, [piece.shape for piece in give], [act, act_far], "square")
    other = [lax.ppermute(piece, "gc", CORES) for piece in own]
    send(12)
    add(11)
    (act_sq,) = small(stack_body, [(2 * act.shape[0], act.shape[1])], [*own, *other], "stack")
    send(13)
    correct_next(1)
    add(12)
    send(14)
    correct_next(2)
    add(13)
    send(15)
    correct_next(1)
    send(16)
    correct_next(1)
    correct_next(1)
    correct_next(1)
    return result


def solution(mesh):
    in_specs = (
        P("layers", "gc"),
        P(("layers", "gc"), "gr"),
        P(("layers", "gc"), "gr"),
        P(("layers", "gr"), "gc"),
    )
    out_specs = P(("layers", "gr"), "gc")
    sizes = (mesh.shape["layers"], mesh.shape["gr"], mesh.shape["gc"])
    shards = lined if sizes == (2, 4, 4) else gathered
    return jax.shard_map(shards, mesh=mesh, in_specs=in_specs, out_specs=out_specs, check_vma=False)
```

time: 494 us -> 208 us (0.42)
  waiting for transfers between devices: 397 us -> 28.1 us
  Pallas kernels: 0 us -> 130 us
  matrix products: 76.8 us -> 0 us
  starting transfers between devices: 0.35 us -> 46.3 us
  between operations: 13.1 us -> 0.49 us
  other arithmetic: 5.52 us -> 0.08 us
    reduce_scatter x2 -> x0, waiting for transfers between devices: 199 us -> none  [the longest x1 186 us: shards(): lax.psum_scatter(grad_partial, 'gr', scatter_dimension=0, tiled=True)]
    all_gather x3 -> x0, waiting for transfers between devices: 198 us -> none  [the longest x1 104 us: shards(): grad_all = lax.all_gather(grad_sq, 'gr', axis=0, tiled=True)]
    pallas_call x0 -> x51, Pallas kernels: none -> 130 us  [the longest x10 70.8 us: project(): pl.pallas_call(body, grid=(steps,), in_specs=[VMEM, pl.BlockSpec((depth,...]
    dot_general x3 -> x0, matrix products: 76.8 us -> none  [the longest x1 48.2 us: shards(): jnp.dot(lax.all_gather(grads, 'gc', axis=0, tiled=True), grad_basis, pref...]
    ppermute x0 -> x49, starting transfers between devices: none -> 46.3 us  [the longest x17 25.9 us: send(): received.append(lax.ppermute(payload, 'gr', OUTER))]
    ppermute x0 -> x49, waiting for transfers between devices: none -> 28.1 us  [the longest x14 16.7 us: add(): others.append(lax.ppermute(sums[-1], ('layers', 'gr'), INNER))]
    convert_element_type x2 -> x0, other arithmetic: 5.52 us -> none  [the longest x1 3 us: shards(): grad_sq = (grad_share * grad_share).astype(jnp.bfloat16)]
  transfers between devices with their start and end apart: 5 -> 49, of which waited for: 5 -> 12; matrix products, arithmetic and copies ran while one was open for 13% -> 0% of each run, Pallas kernels for 0% -> 61%
where the time goes in v1:
time: 208 us
  Pallas kernels  130 us (62%)
  starting transfers between devices  46.3 us (22%)
  waiting for transfers between devices  28.1 us (14%)
  local copies, waits for them, and re-layouts  2.57 us (1%)
    pallas_call x10, Pallas kernels, project(): pl.pallas_call(body, grid=(steps,), in_specs=[VMEM, pl.BlockSpec((depth,...  70.8 us
    ppermute x17, starting transfers between devices, send(): received.append(lax.ppermute(payload, 'gr', OUTER))  25.9 us
    pallas_call x6, Pallas kernels, correct(): pl.pallas_call(body, grid_spec=pltpu.PrefetchScalarGridSpec(num_scalar_pr...  24.9 us
    pallas_call x31, Pallas kernels, whole(): pl.pallas_call(run, in_specs=[pl.BlockSpec(memory_space=pltpu.SMEM)] + [V...  21.2 us
    ppermute x14, waiting for transfers between devices, add(): others.append(lax.ppermute(sums[-1], ('layers', 'gr'), INNER))  16.7 us
    ppermute x14, starting transfers between devices, add(): others.append(lax.ppermute(sums[-1], ('layers', 'gr'), INNER))  12.5 us
    pallas_call x1, Pallas kernels, project_acts(): pl.pallas_call(body, grid_spec=pltpu.PrefetchScalarGridSpec(num_scalar_pr...  10.8 us
    ppermute x17, waiting for transfers between devices, send(): received.append(lax.ppermute(payload, 'gr', OUTER))  8.94 us
  transfers between devices with their start and end apart: 49, of which 12 were waited for; matrix products, arithmetic and copies ran while one was open for 0% of the time, Pallas kernels for 61%

profile of v1, /device:TPU:0, one launch (start us, length us, event | category | flops | bytes accessed | tf_op | source)
XLA Modules:
  0.0 208.0 jit_solution(16162795482905065008)
XLA Ops:
  0.5 2.5 %collective-permute-start = (bf16[192,7168]{1,0:T(8,128)(2,1)}, bf16[192,7168]{1,0:T(8,128)(2,1)S(1)}, u32[]{:S(2)}, u32[]{:S(2)}) collective-permute-start(bf16[192,7168]{1,0:T(8,128)(2,1)} %top_ref.1), channel_id=1, source_target_pairs={{0,2},{2,0},{1,3},{3,1},{4,6},{6,4},{5,7},{7,5},{8,10},{10,8},{9,1... | collective-permute-start | bytes 8257544 | tf_op jit(solution)/shard_map/ppermute | solution.py:311
  2.9 2.4 %collective-permute-done.1.refs_0_ = bf16[192,7168]{1,0:T(8,128)(2,1)S(1)} collective-permute-done((bf16[192,7168]{1,0:T(8,128)(2,1)}, bf16[192,7168]{1,0:T(8,128)(2,1)S(1)}, u32[]{:S(2)}, u32[]{:S(2)}) %collective-permute-start.1) | collective-permute-done | bytes 2752544 | tf_op jit(solution)/shard_map/ppermute | solution.py:310
  5.4 1.8 join.2.rows_ref.refs_0_
  7.2 7.3 %project_grads.10.refs_0_ = bf16[384,512]{1,0:T(8,128)(2,1)S(1)} custom-call(bf16[384,7168]{1,0:T(8,128)(2,1)S(1)} %join.2.rows_ref.refs_0_, bf16[7168,3584]{1,0:T(8,128)(2,1)} %basis_ref.21, bf16[384,7168]{1,0:T(8,128)(2,1)S(1)} %join.2.rows_ref.refs_0_), custom_call_target="tpu_custom_call" | custom-call | flops 10000000 | bytes 100000 | tf_op jit(solution)/shard_map/project_grads/pallas_call | solution.py:197
  14.5 3.0 %collective-permute-start.2 = (bf16[384,512]{1,0:T(8,128)(2,1)S(1)}, bf16[384,512]{1,0:T(8,128)(2,1)}, u32[]{:S(2)}, u32[]{:S(2)}) collective-permute-start(bf16[384,512]{1,0:T(8,128)(2,1)S(1)} %project_grads.10.refs_0_), channel_id=1, source_target_pairs={{0,4},{4,0},{8,12},{12,8},{1,5},{5,1},{9,13},{13,9},{2,6},{6,2},{1... | collective-permute-start | bytes 1179656 | tf_op jit(solution)/shard_map/ppermute | solution.py:337
  17.5 9.8 %project_grads.11 = (bf16[384,512]{1,0:T(8,128)(2,1)}, bf16[384,512]{1,0:T(8,128)(2,1)S(1)}) custom-call(bf16[384,7168]{1,0:T(8,128)(2,1)S(1)} %join.2.rows_ref.refs_0_, bf16[7168,3584]{1,0:T(8,128)(2,1)} %basis_ref.21, bf16[384,512]{1,0:T(8,128)(2,1)S(1)} %project_grads.10.refs_0_), custom_call_target="tpu_custom_call" | custom-call | flops 10000000 | bytes 100000 | tf_op jit(solution)/shard_map/project_grads/pallas_call | solution.py:197
  27.4 1.1 add.25.refs_0_
  28.5 2.0 collective-permute-start.6
  30.5 1.6 collective-permute-start.5
  32.1 2.6 %copy-done.1 = bf16[384,7168]{1,0:T(8,128)(2,1)S(1)} copy-done((bf16[384,7168]{1,0:T(8,128)(2,1)S(1)}, bf16[384,7168]{1,0:T(8,128)(2,1)}, u32[]{:S(2)}) %copy-start.1) | copy-done | bytes 5505048
  34.7 9.2 %project_grads.12 = (bf16[384,512]{1,0:T(8,128)(2,1)S(1)}, bf16[384,512]{1,0:T(8,128)(2,1)S(1)}) custom-call(bf16[384,7168]{1,0:T(8,128)(2,1)S(1)} %copy-done.1, bf16[7168,3584]{1,0:T(8,128)(2,1)} %basis_ref.21, bf16[384,512]{1,0:T(8,128)(2,1)S(1)} %add.25.refs_0_), custom_call_target="tpu_custom_call" | custom-call | flops 10000000 | bytes 100000 | tf_op jit(solution)/shard_map/project_grads/pallas_call | solution.py:197
  43.9 1.2 add.26.refs_3_.refs_0_
  45.1 1.6 collective-permute-start.4
  47.3 1.7 collective-permute-start.9
  49.1 5.3 %project_grads.13.refs_2_.refs_0_ = bf16[384,512]{1,0:T(8,128)(2,1)S(1)} custom-call(bf16[384,7168]{1,0:T(8,128)(2,1)S(1)} %copy-done.2, bf16[7168,3584]{1,0:T(8,128)(2,1)} %basis_ref.21, bf16[384,512]{1,0:T(8,128)(2,1)S(1)} %square.15.refs_0_), custom_call_target="tpu_custom_call" | custom-call | flops 10000000 | bytes 100000 | tf_op jit(solution)/shard_map/project_grads/pallas_call | solution.py:197
  54.3 0.6 add.27.refs_3_.refs_0_
  56.1 1.8 collective-permute-start.7
  58.0 5.3 %project_grads.14.refs_2_.refs_0_ = bf16[384,512]{1,0:T(8,128)(2,1)S(1)} custom-call(bf16[384,7168]{1,0:T(8,128)(2,1)S(1)} %copy-done.2, bf16[7168,3584]{1,0:T(8,128)(2,1)} %basis_ref.21, bf16[384,512]{1,0:T(8,128)(2,1)S(1)} %square.16.refs_0_), custom_call_target="tpu_custom_call" | custom-call | flops 10000000 | bytes 100000 | tf_op jit(solution)/shard_map/project_grads/pallas_call | solution.py:197
  64.0 1.0 collective-permute-done.8.refs_1_
  67.6 5.3 %collective-permute-done.22.refs_1_ = bf16[384,512]{1,0:T(8,128)(2,1)S(1)} collective-permute-done((bf16[384,512]{1,0:T(8,128)(2,1)S(1)}, bf16[384,512]{1,0:T(8,128)(2,1)S(1)}, u32[]{:S(2)}, u32[]{:S(2)}) %collective-permute-start.22) | collective-permute-done | bytes 393248 | tf_op jit(solution)/shard_map/ppermute | solution.py:343
  74.0 10.8 %project_acts.1 = (bf16[384,2048]{1,0:T(8,128)(2,1)S(1)}, bf16[384,512]{1,0:T(8,128)(2,1)S(1)}, bf16[384,512]{1,0:T(8,128)(2,1)S(1)}, bf16[384,512]{1,0:T(8,128)(2,1)S(1)}, bf16[384,512]{1,0:T(8,128)(2,1)S(1)}) custom-call(s32[3]{0:T(128)S(1)} %pad_add_fusion.flags_ref, bf16[768,2048]{1,0:T(8,128)(2,1)} %acts_ref.1, bf16[2048,2048]{1,0:T(8,128)(2,1)} %basis_ref.16, ...), custom_call_target="tpu_custom_call" | custom-call | flops 10000000 | bytes 100000 | tf_op jit(solution)/shard_map/project_acts/pallas_call | solution.py:233
  86.0 0.8 square.18.refs_7_.refs_0_
  86.7 0.7 join.3.rows_ref.refs_0_
  87.4 1.3 collective-permute-start.24
  88.7 5.3 %project_grads.15.refs_2_.refs_0_ = bf16[384,512]{1,0:T(8,128)(2,1)S(1)} custom-call(bf16[384,7168]{1,0:T(8,128)(2,1)S(1)} %join.3.rows_ref.refs_0_, bf16[7168,3584]{1,0:T(8,128)(2,1)} %basis_ref.21, bf16[384,7168]{1,0:T(8,128)(2,1)S(1)} %join.3.rows_ref.refs_0_), custom_call_target="tpu_custom_call" | custom-call | flops 10000000 | bytes 100000 | tf_op jit(solution)/shard_map/project_grads/pallas_call | solution.py:197
  94.7 1.7 collective-permute-start.27
  96.4 0.9 add.31.refs_3_.refs_0_
  97.3 1.6 collective-permute-start.23
  99.7 1.4 collective-permute-start.25
  101.0 9.1 %project_grads.16 = (bf16[384,512]{1,0:T(8,128)(2,1)S(1)}, bf16[384,512]{1,0:T(8,128)(2,1)S(1)}) custom-call(bf16[384,7168]{1,0:T(8,128)(2,1)S(1)} %join.3.rows_ref.refs_0_, bf16[7168,3584]{1,0:T(8,128)(2,1)} %basis_ref.21, bf16[384,512]{1,0:T(8,128)(2,1)S(1)} %square.19.refs_0_), custom_call_target="tpu_custom_call" | custom-call | flops 10000000 | bytes 100000 | tf_op jit(solution)/shard_map/project_grads/pallas_call | solution.py:197
  110.8 1.6 collective-permute-start.30
  112.9 0.7 collective-permute-start.29
  114.7 0.9 collective-permute-start.28
  115.6 9.1 %project_grads.17 = (bf16[384,512]{1,0:T(8,128)(2,1)S(1)}, bf16[384,512]{1,0:T(8,128)(2,1)S(1)}) custom-call(bf16[384,7168]{1,0:T(8,128)(2,1)S(1)} %join.3.rows_ref.refs_0_, bf16[7168,3584]{1,0:T(8,128)(2,1)} %basis_ref.21, bf16[384,512]{1,0:T(8,128)(2,1)S(1)} %add.33.refs_0_), custom_call_target="tpu_custom_call" | custom-call | flops 10000000 | bytes 100000 | tf_op jit(solution)/shard_map/project_grads/pallas_call | solution.py:197
  125.3 2.7 %collective-permute-start.33 = (bf16[384,512]{1,0:T(8,128)(2,1)S(1)}, bf16[384,512]{1,0:T(8,128)(2,1)S(1)}, u32[]{:S(2)}, u32[]{:S(2)}) collective-permute-start(bf16[384,512]{1,0:T(8,128)(2,1)S(1)} %square.21.refs_2_.refs_0_), channel_id=1, source_target_pairs={{0,4},{4,0},{8,12},{12,8},{1,5},{5,1},{9,13},{13,9},{2,6},{6,2},{1... | collective-permute-start | bytes 1179656 | tf_op jit(solution)/shard_map/ppermute | solution.py:337
  128.7 5.3 %project_grads.18.refs_3_.refs_2_.refs_0_ = bf16[384,512]{1,0:T(8,128)(2,1)S(1)} custom-call(bf16[384,7168]{1,0:T(8,128)(2,1)S(1)} %join.3.rows_ref.refs_0_, bf16[7168,3584]{1,0:T(8,128)(2,1)} %basis_ref.21, bf16[384,512]{1,0:T(8,128)(2,1)S(1)} %add.34.refs_0_), custom_call_target="tpu_custom_call" | custom-call | flops 10000000 | bytes 100000 | tf_op jit(solution)/shard_map/project_grads/pallas_call | solution.py:197
  134.6 1.7 collective-permute-start.31
  136.9 5.3 %project_grads.19.refs_3_.refs_2_.refs_0_ = bf16[384,512]{1,0:T(8,128)(2,1)S(1)} custom-call(bf16[384,7168]{1,0:T(8,128)(2,1)S(1)} %join.3.rows_ref.refs_0_, bf16[7168,3584]{1,0:T(8,128)(2,1)} %basis_ref.21, bf16[384,512]{1,0:T(8,128)(2,1)S(1)} %add.35.refs_0_), custom_call_target="tpu_custom_call" | custom-call | flops 10000000 | bytes 100000 | tf_op jit(solution)/shard_map/project_grads/pallas_call | solution.py:197
  142.2 0.8 collective-permute-start.39
  143.6 2.3 %collective-permute-start.38 = (bf16[384,512]{1,0:T(8,128)(2,1)S(1)}, bf16[384,512]{1,0:T(8,128)(2,1)S(1)}, u32[]{:S(2)}, u32[]{:S(2)}) collective-permute-start(bf16[384,512]{1,0:T(8,128)(2,1)S(1)} %square.23.refs_2_), channel_id=1, source_target_pairs={{0,4},{4,0},{8,12},{12,8},{1,5},{5,1},{9,13},{13,9},{2,6},{6,2},{1... | collective-permute-start | bytes 1179656 | tf_op jit(solution)/shard_map/ppermute | solution.py:337
  146.5 1.0 square.24
  148.1 2.6 %collective-permute-done.39.refs_1_ = bf16[384,512]{1,0:T(8,128)(2,1)S(1)} collective-permute-done((bf16[384,512]{1,0:T(8,128)(2,1)S(1)}, bf16[384,512]{1,0:T(8,128)(2,1)S(1)}, u32[]{:S(2)}, u32[]{:S(2)}) %collective-permute-start.39) | collective-permute-done | bytes 393248 | tf_op jit(solution)/shard_map/ppermute | solution.py:343
  150.7 1.2 collective-permute-done.38.refs_1_.refs_3_
  151.9 1.4 collective-permute-start.40
  153.9 1.7 collective-permute-start.42
  156.7 0.8 stack.22.refs_3_.act_ref
  157.5 6.5 %collective-permute-done.40.refs_1_ = bf16[384,512]{1,0:T(8,128)(2,1)S(1)} collective-permute-done((bf16[384,512]{1,0:T(8,128)(2,1)S(1)}, bf16[384,512]{1,0:T(8,128)(2,1)S(1)}, u32[]{:S(2)}, u32[]{:S(2)}) %collective-permute-start.40) | collective-permute-done | bytes 393248 | tf_op jit(solution)/shard_map/ppermute | solution.py:343
  164.6 1.8 collective-permute-start.41
  166.4 4.0 %correct.6 = (bf16[2048,3584]{1,0:T(8,128)(2,1)}, bf16[16,128]{1,0:T(8,128)(2,1)S(1)}) custom-call(s32[3]{0:T(128)S(1)} %pad_add_fusion.flags_ref, bf16[768,2048]{1,0:T(8,128)(2,1)S(1)} %stack.22.refs_3_.act_ref, bf16[384,512]{1,0:T(8,128)(2,1)S(1)} %square.15.refs_0_, bf16[384,512]{1,0:T(8,128)(2,1)S(1)} %collective-permute-done.9.refs_1_, ...), custom_call_target="tpu_custom_call" | custom-call | flops 10000000 | bytes 100000 | tf_op jit(solution)/shard_map/correct/pallas_call | solution.py:276
  171.0 0.8 collective-permute-start.45
  172.4 0.7 square.27.refs_9_.refs_2_
  173.1 5.8 %correct.7 = (bf16[2048,3584]{1,0:T(8,128)(2,1)}, bf16[16,128]{1,0:T(8,128)(2,1)S(1)}) custom-call(s32[3]{0:T(128)S(1)} %pad_add_fusion.flags_ref, bf16[768,2048]{1,0:T(8,128)(2,1)S(1)} %stack.22.refs_3_.act_ref, bf16[384,512]{1,0:T(8,128)(2,1)S(1)} %square.16.refs_0_, ...), custom_call_target="tpu_custom_call", output_to_operand_aliasing={{0}: (10, {})} | custom-call | flops 10000000 | bytes 100000 | tf_op jit(solution)/shard_map/correct/pallas_call | solution.py:276
  179.5 0.8 collective-permute-start.44
  180.3 1.8 collective-permute-start.48
  182.1 0.7 square.28.refs_5_.refs_2_
  183.0 3.8 %correct.8 = (bf16[2048,3584]{1,0:T(8,128)(2,1)}, bf16[16,128]{1,0:T(8,128)(2,1)S(1)}) custom-call(s32[3]{0:T(128)S(1)} %pad_add_fusion.flags_ref, bf16[768,2048]{1,0:T(8,128)(2,1)S(1)} %stack.22.refs_3_.act_ref, bf16[384,512]{1,0:T(8,128)(2,1)S(1)} %square.18.refs_7_.refs_0_, ...), custom_call_target="tpu_custom_call", output_to_operand_aliasing={{0}: (6, {})} | custom-call | flops 10000000 | bytes 100000 | tf_op jit(solution)/shard_map/correct/pallas_call | solution.py:276
  186.8 0.7 collective-permute-done.44.refs_1_
  187.5 0.7 square.29.refs_5_.refs_2_
  188.2 1.2 collective-permute-start.46
  189.4 3.0 %collective-permute-done.48.refs_3_ = bf16[384,512]{1,0:T(8,128)(2,1)S(1)} collective-permute-done((bf16[384,512]{1,0:T(8,128)(2,1)S(1)}, bf16[384,512]{1,0:T(8,128)(2,1)S(1)}, u32[]{:S(2)}, u32[]{:S(2)}) %collective-permute-start.48) | collective-permute-done | bytes 393248 | tf_op jit(solution)/shard_map/ppermute | solution.py:337
  192.3 3.8 %correct.9 = (bf16[2048,3584]{1,0:T(8,128)(2,1)}, bf16[16,128]{1,0:T(8,128)(2,1)S(1)}) custom-call(s32[3]{0:T(128)S(1)} %pad_add_fusion.flags_ref, bf16[768,2048]{1,0:T(8,128)(2,1)S(1)} %stack.22.refs_3_.act_ref, bf16[384,512]{1,0:T(8,128)(2,1)S(1)} %square.19.refs_0_, ...), custom_call_target="tpu_custom_call", output_to_operand_aliasing={{0}: (6, {})} | custom-call | flops 10000000 | bytes 100000 | tf_op jit(solution)/shard_map/correct/pallas_call | solution.py:276
  196.1 3.9 %collective-permute-done.47.refs_3_ = bf16[384,512]{1,0:T(8,128)(2,1)S(1)} collective-permute-done((bf16[384,512]{1,0:T(8,128)(2,1)S(1)}, bf16[384,512]{1,0:T(8,128)(2,1)S(1)}, u32[]{:S(2)}, u32[]{:S(2)}) %collective-permute-start.47) | collective-permute-done | bytes 393248 | tf_op jit(solution)/shard_map/ppermute | solution.py:337
  200.0 3.8 %correct.10 = (bf16[2048,3584]{1,0:T(8,128)(2,1)}, bf16[16,128]{1,0:T(8,128)(2,1)S(1)}) custom-call(s32[3]{0:T(128)S(1)} %pad_add_fusion.flags_ref, bf16[768,2048]{1,0:T(8,128)(2,1)S(1)} %stack.22.refs_3_.act_ref, bf16[384,512]{1,0:T(8,128)(2,1)S(1)} %square.20.refs_2_.refs_0_, ...), custom_call_target="tpu_custom_call", output_to_operand_aliasing={{0}: (6, {})} | custom-call | flops 10000000 | bytes 100000 | tf_op jit(solution)/shard_map/correct/pallas_call | solution.py:276
  204.2 3.8 %correct.11 = (bf16[2048,3584]{1,0:T(8,128)(2,1)}, bf16[16,128]{1,0:T(8,128)(2,1)}) custom-call(s32[3]{0:T(128)S(1)} %pad_add_fusion.flags_ref, bf16[768,2048]{1,0:T(8,128)(2,1)S(1)} %stack.22.refs_3_.act_ref, bf16[384,512]{1,0:T(8,128)(2,1)S(1)} %square.21.refs_2_.refs_0_, ...), custom_call_target="tpu_custom_call", output_to_operand_aliasing={{0}: (6, {})} | custom-call | flops 10000000 | bytes 100000 | tf_op jit(solution)/shard_map/correct/pallas_call | solution.py:276
  (92 shorter events, 20.8 us)
Async XLA Ops:
  0.0 5.4 %collective-permute-start.1 = (bf16[192,7168]{1,0:T(8,128)(2,1)}, bf16[192,7168]{1,0:T(8,128)(2,1)S(1)}, u32[]{:S(2)}, u32[]{:S(2)}) collective-permute-start(bf16[192,7168]{1,0:T(8,128)(2,1)} %top_ref.1), channel_id=1, source_target_pairs={{0,1},{1,0},{2,3},{3,2},{4,5},{5,4},{6,7},{7,6},{8,9},{9,8},{10,11... | collective-permute-start | bytes 8257544 | tf_op jit(solution)/shard_map/ppermute | solution.py:310
  0.5 65.8 %collective-permute-start = (bf16[192,7168]{1,0:T(8,128)(2,1)}, bf16[192,7168]{1,0:T(8,128)(2,1)S(1)}, u32[]{:S(2)}, u32[]{:S(2)}) collective-permute-start(bf16[192,7168]{1,0:T(8,128)(2,1)} %top_ref.1), channel_id=1, source_target_pairs={{0,2},{2,0},{1,3},{3,1},{4,6},{6,4},{5,7},{7,5},{8,10},{10,8},{9,1... | collective-permute-start | bytes 8257544 | tf_op jit(solution)/shard_map/ppermute | solution.py:311
  7.2 10.3 %copy-start = (bf16[384,7168]{1,0:T(8,128)(2,1)}, bf16[384,7168]{1,0:T(8,128)(2,1)S(1)}, u32[]{:S(2)}) copy-start(bf16[384,7168]{1,0:T(8,128)(2,1)S(1)} %join.2.rows_ref.refs_0_) | copy-start | bytes 16515076
  14.5 12.9 %collective-permute-start.2 = (bf16[384,512]{1,0:T(8,128)(2,1)S(1)}, bf16[384,512]{1,0:T(8,128)(2,1)}, u32[]{:S(2)}, u32[]{:S(2)}) collective-permute-start(bf16[384,512]{1,0:T(8,128)(2,1)S(1)} %project_grads.10.refs_0_), channel_id=1, source_target_pairs={{0,4},{4,0},{8,12},{12,8},{1,5},{5,1},{9,13},{13,9},{2,6},{6,2},{1... | collective-permute-start | bytes 1179656 | tf_op jit(solution)/shard_map/ppermute | solution.py:337
  27.3 16.6 %collective-permute-start.3 = (bf16[384,512]{1,0:T(8,128)(2,1)}, bf16[384,512]{1,0:T(8,128)(2,1)}, u32[]{:S(2)}, u32[]{:S(2)}) collective-permute-start(bf16[384,512]{1,0:T(8,128)(2,1)} %get-tuple-element.42.refs_0_), channel_id=1, source_target_pairs={{0,4},{4,0},{8,12},{12,8},{1,5},{5,1},{9,13},{13,9},{2,6},{6,2},{1... | collective-permute-start | bytes 1179656 | tf_op jit(solution)/shard_map/ppermute | solution.py:337
  28.5 18.2 %collective-permute-start.6 = (bf16[384,512]{1,0:T(8,128)(2,1)S(1)}, bf16[384,512]{1,0:T(8,128)(2,1)S(1)}, u32[]{:S(2)}, u32[]{:S(2)}) collective-permute-start(bf16[384,512]{1,0:T(8,128)(2,1)S(1)} %add.25.refs_0_), channel_id=1, source_target_pairs={{4,8},{8,4},{20,24},{24,20},{0,16},{16,0},{12,28},{28,12},{5,9},{9... | collective-permute-start | bytes 1179656 | tf_op jit(solution)/shard_map/ppermute | solution.py:343
  30.5 23.8 %collective-permute-start.5 = (bf16[384,512]{1,0:T(8,128)(2,1)S(1)}, bf16[384,512]{1,0:T(8,128)(2,1)S(1)}, u32[]{:S(2)}, u32[]{:S(2)}) collective-permute-start(bf16[384,512]{1,0:T(8,128)(2,1)S(1)} %get-tuple-element.40.refs_2_.refs_0_), channel_id=1, source_target_pairs={{0,4},{4,0},{8,12},{12,8},{1,5},{5,1},{9,13},{13,9},{2,6},{6,2},{1... | collective-permute-start | bytes 1179656 | tf_op jit(solution)/shard_map/ppermute | solution.py:337
  32.1 2.6 %copy-start.1 = (bf16[384,7168]{1,0:T(8,128)(2,1)S(1)}, bf16[384,7168]{1,0:T(8,128)(2,1)}, u32[]{:S(2)}) copy-start(bf16[384,7168]{1,0:T(8,128)(2,1)} %copy-done) | copy-start | bytes 16515076
  34.7 14.4 %copy-start.2 = (bf16[384,7168]{1,0:T(8,128)(2,1)S(1)}, bf16[384,7168]{1,0:T(8,128)(2,1)}, u32[]{:S(2)}) copy-start(bf16[384,7168]{1,0:T(8,128)(2,1)} %copy-done) | copy-start | bytes 16515076
  45.1 10.4 %collective-permute-start.4 = (bf16[384,512]{1,0:T(8,128)(2,1)S(1)}, bf16[384,512]{1,0:T(8,128)(2,1)S(1)}, u32[]{:S(2)}, u32[]{:S(2)}) collective-permute-start(bf16[384,512]{1,0:T(8,128)(2,1)S(1)} %add.26.refs_3_.refs_0_), channel_id=1, source_target_pairs={{4,8},{8,4},{20,24},{24,20},{0,16},{16,0},{12,28},{28,12},{5,9},{9... | collective-permute-start | bytes 1179656 | tf_op jit(solution)/shard_map/ppermute | solution.py:343
  47.3 15.9 %collective-permute-start.9 = (bf16[384,512]{1,0:T(8,128)(2,1)S(1)}, bf16[384,512]{1,0:T(8,128)(2,1)S(1)}, u32[]{:S(2)}, u32[]{:S(2)}) collective-permute-start(bf16[384,512]{1,0:T(8,128)(2,1)S(1)} %square.15.refs_0_), channel_id=1, source_target_pairs={{0,4},{4,0},{8,12},{12,8},{1,5},{5,1},{9,13},{13,9},{2,6},{6,2},{1... | collective-permute-start | bytes 1179656 | tf_op jit(solution)/shard_map/ppermute | solution.py:337
  55.0 10.0 %collective-permute-start.8 = (bf16[384,512]{1,0:T(8,128)(2,1)S(1)}, bf16[384,512]{1,0:T(8,128)(2,1)S(1)}, u32[]{:S(2)}, u32[]{:S(2)}) collective-permute-start(bf16[384,512]{1,0:T(8,128)(2,1)S(1)} %add.27.refs_3_.refs_0_), channel_id=1, source_target_pairs={{4,8},{8,4},{20,24},{24,20},{0,16},{16,0},{12,28},{28,12},{5,9},{9... | collective-permute-start | bytes 1179656 | tf_op jit(solution)/shard_map/ppermute | solution.py:343
  56.1 9.4 %collective-permute-start.7 = (bf16[384,512]{1,0:T(8,128)(2,1)S(1)}, bf16[384,512]{1,0:T(8,128)(2,1)S(1)}, u32[]{:S(2)}, u32[]{:S(2)}) collective-permute-start(bf16[384,512]{1,0:T(8,128)(2,1)S(1)} %square.16.refs_0_), channel_id=1, source_target_pairs={{0,4},{4,0},{8,12},{12,8},{1,5},{5,1},{9,13},{13,9},{2,6},{6,2},{1... | collective-permute-start | bytes 1179656 | tf_op jit(solution)/shard_map/ppermute | solution.py:337
  63.9 9.1 %collective-permute-start.22 = (bf16[384,512]{1,0:T(8,128)(2,1)S(1)}, bf16[384,512]{1,0:T(8,128)(2,1)S(1)}, u32[]{:S(2)}, u32[]{:S(2)}) collective-permute-start(bf16[384,512]{1,0:T(8,128)(2,1)S(1)} %add.28.refs_3_.refs_0_), channel_id=1, source_target_pairs={{4,8},{8,4},{20,24},{24,20},{0,16},{16,0},{12,28},{28,12},{5,9},{9... | collective-permute-start | bytes 1179656 | tf_op jit(solution)/shard_map/ppermute | solution.py:343
  66.5 6.4 %collective-permute-start.15 = (bf16[192,1024]{1,0:T(8,128)(2,1)S(1)}, bf16[192,1024]{1,0:T(8,128)(2,1)S(1)}, u32[]{:S(2)}, u32[]{:S(2)}) collective-permute-start(bf16[192,1024]{1,0:T(8,128)(2,1)S(1)} %get-tuple-element.50), channel_id=1, source_target_pairs={{0,1},{1,0},{2,3},{3,2},{4,5},{5,4},{6,7},{7,6},{8,9},{9,8},{10,11... | collective-permute-start | bytes 1179656 | tf_op jit(solution)/shard_map/ppermute | solution.py:384
  66.6 6.9 %collective-permute-start.16 = (bf16[192,1024]{1,0:T(8,128)(2,1)S(1)}, bf16[192,1024]{1,0:T(8,128)(2,1)S(1)}, u32[]{:S(2)}, u32[]{:S(2)}) collective-permute-start(bf16[192,1024]{1,0:T(8,128)(2,1)S(1)} %get-tuple-element.51), channel_id=1, source_target_pairs={{0,1},{1,0},{2,3},{3,2},{4,5},{5,4},{6,7},{7,6},{8,9},{9,8},{10,11... | collective-permute-start | bytes 1179656 | tf_op jit(solution)/shard_map/ppermute | solution.py:384
  67.1 6.4 %collective-permute-start.17 = (bf16[192,1024]{1,0:T(8,128)(2,1)S(1)}, bf16[192,1024]{1,0:T(8,128)(2,1)S(1)}, u32[]{:S(2)}, u32[]{:S(2)}) collective-permute-start(bf16[192,1024]{1,0:T(8,128)(2,1)S(1)} %get-tuple-element.52), channel_id=1, source_target_pairs={{0,1},{1,0},{2,3},{3,2},{4,5},{5,4},{6,7},{7,6},{8,9},{9,8},{10,11... | collective-permute-start | bytes 1179656 | tf_op jit(solution)/shard_map/ppermute | solution.py:384
  67.2 17.7 %collective-permute-start.18 = (bf16[192,1024]{1,0:T(8,128)(2,1)S(1)}, bf16[192,1024]{1,0:T(8,128)(2,1)S(1)}, u32[]{:S(2)}, u32[]{:S(2)}) collective-permute-start(bf16[192,1024]{1,0:T(8,128)(2,1)S(1)} %get-tuple-element.53), channel_id=1, source_target_pairs={{0,1},{1,0},{2,3},{3,2},{4,5},{5,4},{6,7},{7,6},{8,9},{9,8},{10,11... | collective-permute-start | bytes 1179656 | tf_op jit(solution)/shard_map/ppermute | solution.py:384
  73.0 12.1 %collective-permute-start.19 = (bf16[192,1024]{1,0:T(8,128)(2,1)S(1)}, bf16[192,1024]{1,0:T(8,128)(2,1)S(1)}, u32[]{:S(2)}, u32[]{:S(2)}) collective-permute-start(bf16[192,1024]{1,0:T(8,128)(2,1)S(1)} %get-tuple-element.54), channel_id=1, source_target_pairs={{0,1},{1,0},{2,3},{3,2},{4,5},{5,4},{6,7},{7,6},{8,9},{9,8},{10,11... | collective-permute-start | bytes 1179656 | tf_op jit(solution)/shard_map/ppermute | solution.py:384
  73.0 12.5 %collective-permute-start.20 = (bf16[192,1024]{1,0:T(8,128)(2,1)S(1)}, bf16[192,1024]{1,0:T(8,128)(2,1)S(1)}, u32[]{:S(2)}, u32[]{:S(2)}) collective-permute-start(bf16[192,1024]{1,0:T(8,128)(2,1)S(1)} %get-tuple-element.55), channel_id=1, source_target_pairs={{0,1},{1,0},{2,3},{3,2},{4,5},{5,4},{6,7},{7,6},{8,9},{9,8},{10,11... | collective-permute-start | bytes 1179656 | tf_op jit(solution)/shard_map/ppermute | solution.py:384
  73.5 12.1 %collective-permute-start.21 = (bf16[192,1024]{1,0:T(8,128)(2,1)S(1)}, bf16[192,1024]{1,0:T(8,128)(2,1)S(1)}, u32[]{:S(2)}, u32[]{:S(2)}) collective-permute-start(bf16[192,1024]{1,0:T(8,128)(2,1)S(1)} %get-tuple-element.44.refs_0_), channel_id=1, source_target_pairs={{0,1},{1,0},{2,3},{3,2},{4,5},{5,4},{6,7},{7,6},{8,9},{9,8},{10,11... | collective-permute-start | bytes 1179656 | tf_op jit(solution)/shard_map/ppermute | solution.py:384
  73.5 13.9 %collective-permute-start.14 = (bf16[384,512]{1,0:T(8,128)(2,1)S(1)}, bf16[384,512]{1,0:T(8,128)(2,1)S(1)}, u32[]{:S(2)}, u32[]{:S(2)}) collective-permute-start(bf16[384,512]{1,0:T(8,128)(2,1)S(1)} %square.17.refs_2_.refs_4_), channel_id=1, source_target_pairs={{0,4},{4,0},{8,12},{12,8},{1,5},{5,1},{9,13},{13,9},{2,6},{6,2},{1... | collective-permute-start | bytes 1179656 | tf_op jit(solution)/shard_map/ppermute | solution.py:337
  84.9 9.8 %collective-permute-start.10 = (bf16[384,512]{1,0:T(8,128)(2,1)S(1)}, bf16[384,512]{1,0:T(8,128)(2,1)S(1)}, u32[]{:S(2)}, u32[]{:S(2)}) collective-permute-start(bf16[384,512]{1,0:T(8,128)(2,1)S(1)} %get-tuple-element.46), channel_id=1, source_target_pairs={{0,1},{1,0},{2,3},{3,2},{4,5},{5,4},{6,7},{7,6},{8,9},{9,8},{10,11... | collective-permute-start | bytes 1179656 | tf_op jit(solution)/shard_map/ppermute | solution.py:387
  85.1 11.3 %collective-permute-start.11 = (bf16[384,512]{1,0:T(8,128)(2,1)S(1)}, bf16[384,512]{1,0:T(8,128)(2,1)S(1)}, u32[]{:S(2)}, u32[]{:S(2)}) collective-permute-start(bf16[384,512]{1,0:T(8,128)(2,1)S(1)} %get-tuple-element.47), channel_id=1, source_target_pairs={{0,1},{1,0},{2,3},{3,2},{4,5},{5,4},{6,7},{7,6},{8,9},{9,8},{10,11... | collective-permute-start | bytes 1179656 | tf_op jit(solution)/shard_map/ppermute | solution.py:387
  85.5 10.9 %collective-permute-start.12 = (bf16[384,512]{1,0:T(8,128)(2,1)S(1)}, bf16[384,512]{1,0:T(8,128)(2,1)S(1)}, u32[]{:S(2)}, u32[]{:S(2)}) collective-permute-start(bf16[384,512]{1,0:T(8,128)(2,1)S(1)} %get-tuple-element.48), channel_id=1, source_target_pairs={{0,1},{1,0},{2,3},{3,2},{4,5},{5,4},{6,7},{7,6},{8,9},{9,8},{10,11... | collective-permute-start | bytes 1179656 | tf_op jit(solution)/shard_map/ppermute | solution.py:387
  85.6 10.8 %collective-permute-start.13 = (bf16[384,512]{1,0:T(8,128)(2,1)S(1)}, bf16[384,512]{1,0:T(8,128)(2,1)S(1)}, u32[]{:S(2)}, u32[]{:S(2)}) collective-permute-start(bf16[384,512]{1,0:T(8,128)(2,1)S(1)} %get-tuple-element.49), channel_id=1, source_target_pairs={{0,1},{1,0},{2,3},{3,2},{4,5},{5,4},{6,7},{7,6},{8,9},{9,8},{10,11... | collective-permute-start | bytes 1179656 | tf_op jit(solution)/shard_map/ppermute | solution.py:387
  87.4 11.6 %collective-permute-start.24 = (bf16[384,512]{1,0:T(8,128)(2,1)S(1)}, bf16[384,512]{1,0:T(8,128)(2,1)S(1)}, u32[]{:S(2)}, u32[]{:S(2)}) collective-permute-start(bf16[384,512]{1,0:T(8,128)(2,1)S(1)} %add.29.refs_0_), channel_id=1, source_target_pairs={{4,8},{8,4},{20,24},{24,20},{0,16},{16,0},{12,28},{28,12},{5,9},{9... | collective-permute-start | bytes 1179656 | tf_op jit(solution)/shard_map/ppermute | solution.py:343
  94.7 15.4 %collective-permute-start.27 = (bf16[384,512]{1,0:T(8,128)(2,1)S(1)}, bf16[384,512]{1,0:T(8,128)(2,1)S(1)}, u32[]{:S(2)}, u32[]{:S(2)}) collective-permute-start(bf16[384,512]{1,0:T(8,128)(2,1)S(1)} %square.18.refs_7_.refs_0_), channel_id=1, source_target_pairs={{0,4},{4,0},{8,12},{12,8},{1,5},{5,1},{9,13},{13,9},{2,6},{6,2},{1... | collective-permute-start | bytes 1179656 | tf_op jit(solution)/shard_map/ppermute | solution.py:337
  97.3 49.2 %collective-permute-start.23 = (bf16[384,2048]{1,0:T(8,128)(2,1)S(1)}, bf16[384,2048]{1,0:T(8,128)(2,1)S(1)}, u32[]{:S(2)}, u32[]{:S(2)}) collective-permute-start(bf16[384,2048]{1,0:T(8,128)(2,1)S(1)} %add.31.refs_3_.refs_0_), channel_id=1, source_target_pairs={{0,2},{2,0},{1,3},{3,1},{4,6},{6,4},{5,7},{7,5},{8,10},{10,8},{9,1... | collective-permute-start | bytes 4718600 | tf_op jit(solution)/shard_map/ppermute | solution.py:394
  98.9 13.5 %collective-permute-start.26 = (bf16[384,512]{1,0:T(8,128)(2,1)S(1)}, bf16[384,512]{1,0:T(8,128)(2,1)S(1)}, u32[]{:S(2)}, u32[]{:S(2)}) collective-permute-start(bf16[384,512]{1,0:T(8,128)(2,1)S(1)} %add.30.refs_5_.refs_0_), channel_id=1, source_target_pairs={{4,8},{8,4},{20,24},{24,20},{0,16},{16,0},{12,28},{28,12},{5,9},{9... | collective-permute-start | bytes 1179656 | tf_op jit(solution)/shard_map/ppermute | solution.py:343
  99.7 14.4 %collective-permute-start.25 = (bf16[384,512]{1,0:T(8,128)(2,1)S(1)}, bf16[384,512]{1,0:T(8,128)(2,1)S(1)}, u32[]{:S(2)}, u32[]{:S(2)}) collective-permute-start(bf16[384,512]{1,0:T(8,128)(2,1)S(1)} %square.19.refs_0_), channel_id=1, source_target_pairs={{0,4},{4,0},{8,12},{12,8},{1,5},{5,1},{9,13},{13,9},{2,6},{6,2},{1... | collective-permute-start | bytes 1179656 | tf_op jit(solution)/shard_map/ppermute | solution.py:337
  110.8 13.9 %collective-permute-start.30 = (bf16[384,512]{1,0:T(8,128)(2,1)S(1)}, bf16[384,512]{1,0:T(8,128)(2,1)S(1)}, u32[]{:S(2)}, u32[]{:S(2)}) collective-permute-start(bf16[384,512]{1,0:T(8,128)(2,1)S(1)} %add.32.refs_3_.refs_0_), channel_id=1, source_target_pairs={{4,8},{8,4},{20,24},{24,20},{0,16},{16,0},{12,28},{28,12},{5,9},{9... | collective-permute-start | bytes 1179656 | tf_op jit(solution)/shard_map/ppermute | solution.py:343
  112.9 15.0 %collective-permute-start.29 = (bf16[384,512]{1,0:T(8,128)(2,1)S(1)}, bf16[384,512]{1,0:T(8,128)(2,1)S(1)}, u32[]{:S(2)}, u32[]{:S(2)}) collective-permute-start(bf16[384,512]{1,0:T(8,128)(2,1)S(1)} %square.20.refs_2_.refs_0_), channel_id=1, source_target_pairs={{0,4},{4,0},{8,12},{12,8},{1,5},{5,1},{9,13},{13,9},{2,6},{6,2},{1... | collective-permute-start | bytes 1179656 | tf_op jit(solution)/shard_map/ppermute | solution.py:337
  114.7 19.3 %collective-permute-start.28 = (bf16[384,512]{1,0:T(8,128)(2,1)S(1)}, bf16[384,512]{1,0:T(8,128)(2,1)S(1)}, u32[]{:S(2)}, u32[]{:S(2)}) collective-permute-start(bf16[384,512]{1,0:T(8,128)(2,1)S(1)} %add.33.refs_0_), channel_id=1, source_target_pairs={{4,8},{8,4},{20,24},{24,20},{0,16},{16,0},{12,28},{28,12},{5,9},{9... | collective-permute-start | bytes 1179656 | tf_op jit(solution)/shard_map/ppermute | solution.py:343
  125.3 11.0 %collective-permute-start.33 = (bf16[384,512]{1,0:T(8,128)(2,1)S(1)}, bf16[384,512]{1,0:T(8,128)(2,1)S(1)}, u32[]{:S(2)}, u32[]{:S(2)}) collective-permute-start(bf16[384,512]{1,0:T(8,128)(2,1)S(1)} %square.21.refs_2_.refs_0_), channel_id=1, source_target_pairs={{0,4},{4,0},{8,12},{12,8},{1,5},{5,1},{9,13},{13,9},{2,6},{6,2},{1... | collective-permute-start | bytes 1179656 | tf_op jit(solution)/shard_map/ppermute | solution.py:337
  128.6 14.4 %collective-permute-start.32 = (bf16[384,512]{1,0:T(8,128)(2,1)S(1)}, bf16[384,512]{1,0:T(8,128)(2,1)S(1)}, u32[]{:S(2)}, u32[]{:S(2)}) collective-permute-start(bf16[384,512]{1,0:T(8,128)(2,1)S(1)} %add.34.refs_0_), channel_id=1, source_target_pairs={{4,8},{8,4},{20,24},{24,20},{0,16},{16,0},{12,28},{28,12},{5,9},{9... | collective-permute-start | bytes 1179656 | tf_op jit(solution)/shard_map/ppermute | solution.py:343
  134.6 11.3 %collective-permute-start.31 = (bf16[384,512]{1,0:T(8,128)(2,1)S(1)}, bf16[384,512]{1,0:T(8,128)(2,1)S(1)}, u32[]{:S(2)}, u32[]{:S(2)}) collective-permute-start(bf16[384,512]{1,0:T(8,128)(2,1)S(1)} %square.22.refs_2_), channel_id=1, source_target_pairs={{0,4},{4,0},{8,12},{12,8},{1,5},{5,1},{9,13},{13,9},{2,6},{6,2},{1... | collective-permute-start | bytes 1179656 | tf_op jit(solution)/shard_map/ppermute | solution.py:337
  142.2 8.5 %collective-permute-start.39 = (bf16[384,512]{1,0:T(8,128)(2,1)S(1)}, bf16[384,512]{1,0:T(8,128)(2,1)S(1)}, u32[]{:S(2)}, u32[]{:S(2)}) collective-permute-start(bf16[384,512]{1,0:T(8,128)(2,1)S(1)} %add.35.refs_0_), channel_id=1, source_target_pairs={{4,8},{8,4},{20,24},{24,20},{0,16},{16,0},{12,28},{28,12},{5,9},{9... | collective-permute-start | bytes 1179656 | tf_op jit(solution)/shard_map/ppermute | solution.py:343
  143.6 8.4 %collective-permute-start.38 = (bf16[384,512]{1,0:T(8,128)(2,1)S(1)}, bf16[384,512]{1,0:T(8,128)(2,1)S(1)}, u32[]{:S(2)}, u32[]{:S(2)}) collective-permute-start(bf16[384,512]{1,0:T(8,128)(2,1)S(1)} %square.23.refs_2_), channel_id=1, source_target_pairs={{0,4},{4,0},{8,12},{12,8},{1,5},{5,1},{9,13},{13,9},{2,6},{6,2},{1... | collective-permute-start | bytes 1179656 | tf_op jit(solution)/shard_map/ppermute | solution.py:337
  147.5 6.4 %collective-permute-start.34 = (bf16[384,512]{1,0:T(8,128)(2,1)S(1)}, bf16[384,512]{1,0:T(8,128)(2,1)S(1)}, u32[]{:S(2)}, u32[]{:S(2)}) collective-permute-start(bf16[384,512]{1,0:T(8,128)(2,1)S(1)} %get-tuple-element.60.refs_0_), channel_id=1, source_target_pairs={{0,1},{1,0},{2,3},{3,2},{4,5},{5,4},{6,7},{7,6},{8,9},{9,8},{10,11... | collective-permute-start | bytes 1179656 | tf_op jit(solution)/shard_map/ppermute | solution.py:410
  147.6 8.7 %collective-permute-start.35 = (bf16[384,512]{1,0:T(8,128)(2,1)S(1)}, bf16[384,512]{1,0:T(8,128)(2,1)S(1)}, u32[]{:S(2)}, u32[]{:S(2)}) collective-permute-start(bf16[384,512]{1,0:T(8,128)(2,1)S(1)} %get-tuple-element.61.refs_1_), channel_id=1, source_target_pairs={{0,1},{1,0},{2,3},{3,2},{4,5},{5,4},{6,7},{7,6},{8,9},{9,8},{10,11... | collective-permute-start | bytes 1179656 | tf_op jit(solution)/shard_map/ppermute | solution.py:410
  148.1 8.6 %collective-permute-start.36 = (bf16[384,512]{1,0:T(8,128)(2,1)S(1)}, bf16[384,512]{1,0:T(8,128)(2,1)S(1)}, u32[]{:S(2)}, u32[]{:S(2)}) collective-permute-start(bf16[384,512]{1,0:T(8,128)(2,1)S(1)} %get-tuple-element.62.refs_2_), channel_id=1, source_target_pairs={{0,1},{1,0},{2,3},{3,2},{4,5},{5,4},{6,7},{7,6},{8,9},{9,8},{10,11... | collective-permute-start | bytes 1179656 | tf_op jit(solution)/shard_map/ppermute | solution.py:410
  150.7 6.0 %collective-permute-start.37 = (bf16[384,512]{1,0:T(8,128)(2,1)S(1)}, bf16[384,512]{1,0:T(8,128)(2,1)S(1)}, u32[]{:S(2)}, u32[]{:S(2)}) collective-permute-start(bf16[384,512]{1,0:T(8,128)(2,1)S(1)} %get-tuple-element.63.refs_3_), channel_id=1, source_target_pairs={{0,1},{1,0},{2,3},{3,2},{4,5},{5,4},{6,7},{7,6},{8,9},{9,8},{10,11... | collective-permute-start | bytes 1179656 | tf_op jit(solution)/shard_map/ppermute | solution.py:410
  151.9 12.1 %collective-permute-start.40 = (bf16[384,512]{1,0:T(8,128)(2,1)S(1)}, bf16[384,512]{1,0:T(8,128)(2,1)S(1)}, u32[]{:S(2)}, u32[]{:S(2)}) collective-permute-start(bf16[384,512]{1,0:T(8,128)(2,1)S(1)} %add.36.refs_2_.refs_0_), channel_id=1, source_target_pairs={{4,8},{8,4},{20,24},{24,20},{0,16},{16,0},{12,28},{28,12},{5,9},{9... | collective-permute-start | bytes 1179656 | tf_op jit(solution)/shard_map/ppermute | solution.py:343
  153.9 16.5 %collective-permute-start.42 = (bf16[384,512]{1,0:T(8,128)(2,1)S(1)}, bf16[384,512]{1,0:T(8,128)(2,1)S(1)}, u32[]{:S(2)}, u32[]{:S(2)}) collective-permute-start(bf16[384,512]{1,0:T(8,128)(2,1)S(1)} %square.25.refs_2_.refs_6_), channel_id=1, source_target_pairs={{0,4},{4,0},{8,12},{12,8},{1,5},{5,1},{9,13},{13,9},{2,6},{6,2},{1... | collective-permute-start | bytes 1179656 | tf_op jit(solution)/shard_map/ppermute | solution.py:337
  156.3 16.2 %collective-permute-start.43 = (bf16[384,512]{1,0:T(8,128)(2,1)S(1)}, bf16[384,512]{1,0:T(8,128)(2,1)S(1)}, u32[]{:S(2)}, u32[]{:S(2)}) collective-permute-start(bf16[384,512]{1,0:T(8,128)(2,1)S(1)} %add.37.refs_8_.refs_0_), channel_id=1, source_target_pairs={{4,8},{8,4},{20,24},{24,20},{0,16},{16,0},{12,28},{28,12},{5,9},{9... | collective-permute-start | bytes 1179656 | tf_op jit(solution)/shard_map/ppermute | solution.py:343
  164.6 14.3 %collective-permute-start.41 = (bf16[384,512]{1,0:T(8,128)(2,1)S(1)}, bf16[384,512]{1,0:T(8,128)(2,1)S(1)}, u32[]{:S(2)}, u32[]{:S(2)}) collective-permute-start(bf16[384,512]{1,0:T(8,128)(2,1)S(1)} %square.26.refs_4_.refs_2_), channel_id=1, source_target_pairs={{0,4},{4,0},{8,12},{12,8},{1,5},{5,1},{9,13},{13,9},{2,6},{6,2},{1... | collective-permute-start | bytes 1179656 | tf_op jit(solution)/shard_map/ppermute | solution.py:337
  171.0 11.1 %collective-permute-start.45 = (bf16[384,512]{1,0:T(8,128)(2,1)S(1)}, bf16[384,512]{1,0:T(8,128)(2,1)S(1)}, u32[]{:S(2)}, u32[]{:S(2)}) collective-permute-start(bf16[384,512]{1,0:T(8,128)(2,1)S(1)} %add.38.refs_2_.refs_0_), channel_id=1, source_target_pairs={{4,8},{8,4},{20,24},{24,20},{0,16},{16,0},{12,28},{28,12},{5,9},{9... | collective-permute-start | bytes 1179656 | tf_op jit(solution)/shard_map/ppermute | solution.py:343
  179.5 8.0 %collective-permute-start.44 = (bf16[384,512]{1,0:T(8,128)(2,1)S(1)}, bf16[384,512]{1,0:T(8,128)(2,1)S(1)}, u32[]{:S(2)}, u32[]{:S(2)}) collective-permute-start(bf16[384,512]{1,0:T(8,128)(2,1)S(1)} %add.39.refs_2_.refs_0_), channel_id=1, source_target_pairs={{4,8},{8,4},{20,24},{24,20},{0,16},{16,0},{12,28},{28,12},{5,9},{9... | collective-permute-start | bytes 1179656 | tf_op jit(solution)/shard_map/ppermute | solution.py:343
  180.3 12.1 %collective-permute-start.48 = (bf16[384,512]{1,0:T(8,128)(2,1)S(1)}, bf16[384,512]{1,0:T(8,128)(2,1)S(1)}, u32[]{:S(2)}, u32[]{:S(2)}) collective-permute-start(bf16[384,512]{1,0:T(8,128)(2,1)S(1)} %square.27.refs_9_.refs_2_), channel_id=1, source_target_pairs={{0,4},{4,0},{8,12},{12,8},{1,5},{5,1},{9,13},{13,9},{2,6},{6,2},{1... | collective-permute-start | bytes 1179656 | tf_op jit(solution)/shard_map/ppermute | solution.py:337
  182.8 17.2 %collective-permute-start.47 = (bf16[384,512]{1,0:T(8,128)(2,1)S(1)}, bf16[384,512]{1,0:T(8,128)(2,1)S(1)}, u32[]{:S(2)}, u32[]{:S(2)}) collective-permute-start(bf16[384,512]{1,0:T(8,128)(2,1)S(1)} %square.28.refs_5_.refs_2_), channel_id=1, source_target_pairs={{0,4},{4,0},{8,12},{12,8},{1,5},{5,1},{9,13},{13,9},{2,6},{6,2},{1... | collective-permute-start | bytes 1179656 | tf_op jit(solution)/shard_map/ppermute | solution.py:337
  188.2 16.0 %collective-permute-start.46 = (bf16[384,512]{1,0:T(8,128)(2,1)S(1)}, bf16[384,512]{1,0:T(8,128)(2,1)S(1)}, u32[]{:S(2)}, u32[]{:S(2)}) collective-permute-start(bf16[384,512]{1,0:T(8,128)(2,1)S(1)} %square.29.refs_5_.refs_2_), channel_id=1, source_target_pairs={{0,4},{4,0},{8,12},{12,8},{1,5},{5,1},{9,13},{13,9},{2,6},{6,2},{1... | collective-permute-start | bytes 1179656 | tf_op jit(solution)/shard_map/ppermute | solution.py:337

commit v2 on v1

v2 whole, which is shorter than its diff:
```python
import functools

import jax
import jax.numpy as jnp
from jax import lax
from jax.experimental import pallas as pl
from jax.experimental.pallas import tpu as pltpu
from jax.sharding import PartitionSpec as P

BF16 = jnp.bfloat16
F32 = jnp.float32
MIB = 2**20


def token_product(left, right):
    return lax.dot_general(
        left, right, (((0,), (0,)), ((), ())), preferred_element_type=F32
    )


def gathered(acts, grads, act_basis, grad_basis):
    token_count = acts.shape[0]
    grad_partial = jnp.dot(
        lax.all_gather(grads, "gc", axis=0, tiled=True),
        grad_basis,
        preferred_element_type=F32,
    )
    act_share = lax.psum_scatter(
        jnp.dot(acts, act_basis, preferred_element_type=F32),
        "gc",
        scatter_dimension=0,
        tiled=True,
    )
    act_sq = (act_share * act_share).astype(BF16)
    grad_share = lax.psum_scatter(grad_partial, "gr", scatter_dimension=0, tiled=True)
    grad_sq = (grad_share * grad_share).astype(BF16)
    grad_all = lax.all_gather(grad_sq, "gr", axis=0, tiled=True)
    total = token_product(lax.all_gather(act_sq, "gc", axis=0, tiled=True), grad_all)
    return (total / token_count).astype(BF16)


FREE = pl.CostEstimate(flops=10**7, bytes_accessed=10**5, transcendentals=0)
VMEM = pl.BlockSpec(memory_space=pltpu.VMEM)
ANYWHERE = pl.BlockSpec(memory_space=pl.ANY)


def ordered(array, *after):
    def body(*refs):
        pass

    return pl.pallas_call(
        body,
        in_specs=[ANYWHERE] * (1 + len(after)),
        out_specs=ANYWHERE,
        out_shape=jax.ShapeDtypeStruct(array.shape, array.dtype),
        input_output_aliases={0: 0},
        compiler_params=pltpu.CompilerParams(vmem_limit_bytes=MIB),
        cost_estimate=FREE,
        name="ordered",
    )(array, *after)


def whole(body, out_shape, flags, arrays, after, name, limit=8):
    def run(flags_ref, *refs):
        body(flags_ref, *refs[:len(arrays)], *refs[len(arrays) + len(after):])

    return pl.pallas_call(
        run,
        in_specs=[pl.BlockSpec(memory_space=pltpu.SMEM)] + [VMEM] * len(arrays) + [ANYWHERE] * len(after),
        out_specs=[VMEM] * len(out_shape),
        out_shape=[pltpu.VMEM(shape, BF16) for shape in out_shape],
        compiler_params=pltpu.CompilerParams(vmem_limit_bytes=limit * MIB),
        name=name,
    )(flags, *arrays, *after)


def add_body(flags, left, right, out):
    out[...] = (left[...].astype(F32) + right[...].astype(F32)).astype(BF16)


def square_body(flags, left, right, out):
    t = left[...].astype(F32) + right[...].astype(F32)
    out[...] = (t * t).astype(BF16)


def square_or_term_body(flags, left, right, term, out):
    @pl.when(flags[0] == 0)
    def _():
        square_body(flags, left, right, out)

    @pl.when(flags[0] == 1)
    def _():
        out[...] = term[...]


def add_pieces_body(flags, *refs):
    n = len(refs) // 2
    width = refs[0].shape[1]
    for i in range(n):
        add_body(flags, refs[i], refs[n + i], refs[2 * n].at[:, i * width:(i + 1) * width])


def square_pieces_body(flags, left, right, *outs):
    width = outs[0].shape[1]
    for i, out in enumerate(outs):
        at = slice(i * width, (i + 1) * width)
        square_body(flags, left.at[:, at], right.at[:, at], out)


def stack_body(flags, *refs):
    n = len(refs) // 2
    own, other, out = refs[:n], refs[n:2 * n], refs[2 * n]
    block, width = own[0].shape[0] // 2, own[0].shape[1]
    for chip in range(2):
        @pl.when(flags[1] == chip)
        def _(chip=chip):
            for i in range(n):
                rows = []
                for which in (chip, 1 - chip):
                    at = slice(which * block, (which + 1) * block)
                    rows += [own[i][at], other[i][at]]
                out[i * width:(i + 1) * width, :] = jnp.concatenate(rows).T


def split(array, widths, after):
    rows = array.shape[0]

    def body(array_ref, *refs):
        outs, sems = refs[len(after):-1], refs[-1]
        at, copies = 0, []
        for i, out in enumerate(outs):
            copies.append(pltpu.make_async_copy(array_ref.at[:, pl.ds(at, widths[i])], out, sems.at[i]))
            at += widths[i]
        start(copies)
        wait(copies)

    return pl.pallas_call(
        body,
        in_specs=[ANYWHERE] * (1 + len(after)),
        out_specs=[VMEM] * len(widths),
        out_shape=[pltpu.VMEM((rows, width), BF16) for width in widths],
        scratch_shapes=[pltpu.SemaphoreType.DMA((len(widths),))],
        compiler_params=pltpu.CompilerParams(vmem_limit_bytes=2 * MIB),
        cost_estimate=FREE,
        name="split",
    )(array, *after)


def join(top, bottom, after):
    count = top[0].shape[0]
    depth = sum(piece.shape[1] for piece in top)
    n = len(top) + len(bottom)

    def body(*refs):
        out, sems = refs[n + len(after):]
        copies = []
        for first, row, pieces in ((0, 0, top), (len(top), count, bottom)):
            at = 0
            for i, piece in enumerate(pieces):
                width = piece.shape[1]
                to = out.at[pl.ds(row, count), pl.ds(at, width)]
                copies.append(pltpu.make_async_copy(refs[first + i], to, sems.at[first + i]))
                at += width
        start(copies)
        wait(copies)

    return pl.pallas_call(
        body,
        in_specs=[ANYWHERE] * (n + len(after)),
        out_specs=VMEM,
        out_shape=pltpu.VMEM((2 * count, depth), BF16),
        scratch_shapes=[pltpu.SemaphoreType.DMA((n,))],
        compiler_params=pltpu.CompilerParams(vmem_limit_bytes=2 * MIB),
        cost_estimate=FREE,
        name="join",
    )(*top, *bottom, *after)


def block_copies(basis_ref, first, out, sems):
    parts = sems.shape[0]
    rows = out.shape[0] // parts
    return [
        pltpu.make_async_copy(
            basis_ref.at[pl.ds(i * rows, rows), pl.ds(first, out.shape[1])], out.at[pl.ds(i * rows, rows)], sems.at[i]
        )
        for i in range(parts)
    ]


def start(copies):
    for copy in copies:
        copy.start()


def wait(copies):
    for copy in copies:
        copy.wait()


COPIES = 7


def fetch(basis, width, after):
    depth = basis.shape[0]

    def body(basis_ref, *refs):
        out, sems = refs[len(after):]
        copies = block_copies(basis_ref, 0, out, sems)
        start(copies)
        wait(copies)

    return pl.pallas_call(
        body,
        in_specs=[ANYWHERE] * (1 + len(after)),
        out_specs=VMEM,
        out_shape=pltpu.VMEM((depth, width), BF16),
        scratch_shapes=[pltpu.SemaphoreType.DMA((COPIES,))],
        compiler_params=pltpu.CompilerParams(vmem_limit_bytes=2 * MIB),
        cost_estimate=FREE,
        name="fetch",
    )(basis, *after)


def project(rows, basis, block, then, after):
    count, depth = rows.shape
    width = block.shape[1]
    fetches = then is not None
    step = depth // 2

    def body(rows_ref, basis_ref, block_ref, *refs):
        refs = refs[len(after):]
        if fetches:
            ahead = block_copies(basis_ref, then, refs[1], refs[2])
            start(ahead)

        def add(i, total):
            at = pl.ds(pl.multiple_of(i * step, step), step)
            return total + jnp.dot(rows_ref[:, at], block_ref[at, :], preferred_element_type=F32)

        refs[0][...] = lax.fori_loop(0, depth // step, add, jnp.zeros((count, width), F32)).astype(BF16)
        if fetches:
            wait(ahead)

    shapes = [pltpu.VMEM((count, width), BF16)] + [pltpu.VMEM((depth, width), BF16)] * fetches
    return pl.pallas_call(
        body,
        in_specs=[VMEM, ANYWHERE, VMEM] + [ANYWHERE] * len(after),
        out_specs=[VMEM] * len(shapes),
        out_shape=shapes,
        scratch_shapes=[pltpu.SemaphoreType.DMA((COPIES,))] * fetches,
        compiler_params=pltpu.CompilerParams(vmem_limit_bytes=8 * MIB),
        cost_estimate=FREE,
        name="project_grads",
    )(rows, basis, block, *after)


def project_acts(flags, acts, basis, first, width, given, after):
    count, depth = acts.shape
    tokens = count // 4
    step = 512
    steps = width // step

    def body(flags_ref, acts_ref, basis_ref, *refs):
        given_refs, outs = refs[:len(given)], refs[len(given) + len(after):]
        keeps, gives = outs[:steps], outs[steps:]
        j = pl.program_id(0)

        @pl.when(j == 0)
        def _():
            for old, new in zip(given_refs, gives):
                new[...] = old[...]

        part = jnp.dot(acts_ref[...], basis_ref[...], preferred_element_type=F32).astype(BF16)
        for own in range(2):
            for i in range(steps):
                @pl.when((flags_ref[2] == own) & (j == i))
                def _(own=own, i=i):
                    for chip in range(2):
                        to = slice(chip * tokens, (chip + 1) * tokens)
                        mine, other = 2 * chip + own, 2 * chip + 1 - own
                        keeps[i][to, :] = part[mine * tokens:(mine + 1) * tokens]
                        gives[len(given) + i][to, :] = part[other * tokens:(other + 1) * tokens]

    n = 2 * steps + len(given)
    return pl.pallas_call(
        body,
        grid_spec=pltpu.PrefetchScalarGridSpec(
            num_scalar_prefetch=1,
            grid=(steps,),
            in_specs=[
                VMEM,
                pl.BlockSpec((depth, step), lambda j, c: (0, first // step + j)),
            ]
            + [VMEM] * len(given)
            + [ANYWHERE] * len(after),
            out_specs=[VMEM] * n,
        ),
        out_shape=[pltpu.VMEM((count // 2, step), BF16)] * n,
        compiler_params=pltpu.CompilerParams(vmem_limit_bytes=12 * MIB),
        cost_estimate=FREE,
        name="project_acts",
    )(
        flags,
        acts,
        pltpu.with_memory_space_constraint(basis, pltpu.HBM),
        *given,
        *after,
    )


def correct(flags, act_sq, pieces, first, total_width, result, after):
    height, tokens = act_sq.shape
    half, chunk = pieces[0][0].shape
    flat = [a for piece in pieces for a in piece]
    width = chunk * len(pieces)
    extra = list(after) if result is None else [result, *after]
    rows = height // (4 * len(pieces))

    def body(flags_ref, act_ref, *refs):
        ins = refs[:len(flat)]
        out, done, grad_sq, held, sems = refs[len(flat) + len(extra):]
        done[...] = jnp.zeros_like(done)
        for from_other in range(2):
            @pl.when(flags_ref[0] == from_other)
            def _(from_other=from_other):
                for i in range(len(pieces)):
                    at = slice(i * chunk, (i + 1) * chunk)
                    grad_sq[:half, at] = ins[4 * i + from_other][...]
                    grad_sq[half:, at] = ins[4 * i + 2 + from_other][...]

        def copy(r):
            at = pl.ds(pl.multiple_of(r * rows, rows), rows)
            slot = lax.rem(r, 2)
            return pltpu.make_async_copy(held.at[slot], out.at[at, pl.ds(first, width)], sems.at[slot])

        @pl.loop(0, height // rows)
        def _(r):
            act = act_ref[pl.ds(pl.multiple_of(r * rows, rows), rows), :]
            total = jnp.dot(act, grad_sq[...], preferred_element_type=F32)

            @pl.when(r >= 2)
            def _():
                copy(r - 2).wait()

            held[lax.rem(r, 2)] = (total * (1.0 / tokens)).astype(BF16)
            copy(r).start()

        copy(height // rows - 2).wait()
        copy(height // rows - 1).wait()

    return pl.pallas_call(
        body,
        in_specs=[pl.BlockSpec(memory_space=pltpu.SMEM)] + [VMEM] * (1 + len(flat)) + [ANYWHERE] * len(extra),
        out_specs=[ANYWHERE, VMEM],
        out_shape=[pltpu.HBM((height, total_width), BF16), pltpu.VMEM((16, 128), BF16)],
        scratch_shapes=[
            pltpu.VMEM((tokens, width), BF16),
            pltpu.VMEM((2, rows, width), BF16),
            pltpu.SemaphoreType.DMA((2,)),
        ],
        input_output_aliases={} if result is None else {2 + len(flat): 0},
        compiler_params=pltpu.CompilerParams(vmem_limit_bytes=12 * MIB),
        cost_estimate=FREE,
        name="correct",
    )(flags, act_sq, *flat, *extra)


CORES = [(0, 1), (1, 0), (2, 3), (3, 2)]
CHIPS = [(0, 2), (2, 0), (1, 3), (3, 1)]
OUTER = [(0, 1), (1, 0), (2, 3), (3, 2)]
INNER = [(1, 2), (2, 1), (5, 6), (6, 5), (0, 4), (4, 0), (3, 7), (7, 3)]


def lined(acts, grads, act_basis, grad_basis):
    chunk = 512
    lag = 3
    width = grad_basis.shape[1]
    half = width // chunk
    count = 2 * half
    place = lax.axis_index("gr")
    chip, core = lax.axis_index("gc") // 2, lax.axis_index("gc") % 2
    is_outer = (place == 0) | (place == 3)
    flags = jnp.stack([is_outer.astype(jnp.int32), chip.astype(jnp.int32), core.astype(jnp.int32)])

    near = lax.ppermute(grads, "gc", CORES)
    last = (flags,)
    block = None
    parts, payloads, received, sums, others = [], [], [], [], []

    def project_next(rows):
        nonlocal last, block
        k = len(parts)
        then = (k + 1) % half * chunk if k + 1 < count else None
        part, *blocks = project(rows, grad_basis, block, then, last)
        block = blocks[0] if blocks else None
        parts.append(part)
        last = (part,)

    def send(k):
        nonlocal last
        j = k - lag
        if k < lag:
            payload = parts[k]
        else:
            shape = sums[j].shape
            if k < count:
                (payload,) = whole(
                    square_or_term_body, [shape], flags, [sums[j], others[j], parts[k]], last, "square"
                )
            else:
                (payload,) = whole(square_body, [shape], flags, [sums[j], others[j]], last, "square")
            last = (payload,)
        payloads.append(payload)
        received.append(lax.ppermute(payload, "gr", OUTER))

    def add(k):
        nonlocal last
        sums.extend(whole(add_body, [parts[k].shape], flags, [parts[k], received[k]], last, "add"))
        last = (sums[-1],)
        others.append(lax.ppermute(sums[-1], ("layers", "gr"), INNER))

    result = None
    done = 0

    def correct_next(n):
        nonlocal last, result, done
        pieces = [
            (payloads[j + lag], received[j + lag], payloads[half + j + lag], received[half + j + lag])
            for j in range(done, done + n)
        ]
        result, token = correct(flags, act_sq, pieces, done * chunk, width, result, last)
        last = (token,)
        done += n

    def small(body, shapes, arrays, name):
        nonlocal last
        out = whole(body, shapes, flags, arrays, last, name)
        last = (out[-1],)
        return out

    far = lax.ppermute(grads, "gc", CHIPS)
    columns = act_basis.shape[1]
    block = fetch(grad_basis, chunk, last)
    last = (block,)
    act_terms = list(project_acts(flags, acts, act_basis, 0, columns, [], last))
    keep, give = act_terms[:len(act_terms) // 2], act_terms[len(act_terms) // 2:]
    last = (keep[-1],)
    taken = [lax.ppermute(piece, "gc", CORES) for piece in give]
    rows = join([pltpu.with_memory_space_constraint(grads, pltpu.HBM)], [near], last)
    last = (rows,)
    project_next(rows)
    send(0)
    project_next(rows)
    send(1)
    (act,) = small(add_pieces_body, [(keep[0].shape[0], columns)], [*keep, *taken], "add")
    act_far = lax.ppermute(act, "gc", CHIPS)
    project_next(rows)
    send(2)
    add(0)
    project_next(rows)
    for k in (1, 2, 3):
        add(k)
        project_next(rows)
        send(k + 2)
    far_pieces = split(far, [far.shape[1] // 7] * 7, last)
    last = (far_pieces[-1],)
    far_near = [lax.ppermute(piece, "gc", CORES) for piece in far_pieces]
    add(4)
    send(6)
    rows = join([far], far_near, last)
    last = (rows,)
    project_next(rows)
    add(5)
    send(7)
    for k in range(6, 12):
        add(k)
        project_next(rows)
        send(k + 2)
        if k == 9:
            own = small(square_pieces_body, [(act.shape[0], columns // 2)] * 2, [act, act_far], "square")
            other = [lax.ppermute(piece, "gc", CORES) for piece in own]
    add(12)
    send(14)
    (act_sq,) = small(stack_body, [(columns, 2 * act.shape[0])], [*own, *other], "stack")
    correct_next(1)
    add(13)
    send(15)
    correct_next(2)
    send(16)
    correct_next(2)
    correct_next(1)
    correct_next(1)
    return result


def solution(mesh):
    in_specs = (
        P("layers", "gc"),
        P(("layers", "gc"), "gr"),
        P(("layers", "gc"), "gr"),
        P(("layers", "gr"), "gc"),
    )
    out_specs = P(("layers", "gr"), "gc")
    sizes = (mesh.shape["layers"], mesh.shape["gr"], mesh.shape["gc"])
    shards = lined if sizes == (2, 4, 4) else gathered
    return jax.shard_map(shards, mesh=mesh, in_specs=in_specs, out_specs=out_specs, check_vma=False)
```

time: 208 us -> 188 us (0.904)
  Pallas kernels: 130 us -> 115 us
  waiting for transfers between devices: 28.1 us -> 17.8 us
  starting transfers between devices: 46.3 us -> 54.1 us
    pallas_call x18 -> x22, Pallas kernels: 98.1 us -> 82 us  [the longest x14 48.5 us: project(): pl.pallas_call(body, in_specs=[VMEM, ANYWHERE, VMEM] + [ANYWHERE] * len(a...]
    ppermute x14, waiting for transfers between devices: 16.7 us -> 2.79 us  [add(): others.append(lax.ppermute(sums[-1], ('layers', 'gr'), INNER))]
    ppermute x14, starting transfers between devices: 12.5 us -> 22.2 us  [add(): others.append(lax.ppermute(sums[-1], ('layers', 'gr'), INNER))]
    ppermute x17, waiting for transfers between devices: 8.94 us -> 14.9 us  [send(): received.append(lax.ppermute(payload, 'gr', OUTER))]
    ppermute x1, waiting for transfers between devices: 2.45 us -> 0.01 us  [lined(): near = lax.ppermute(grads, 'gc', CORES)]
  transfers between devices with their start and end apart: 49 -> 47, of which waited for: 12 -> 12; matrix products, arithmetic and copies ran while one was open for 0% -> 0% of each run, Pallas kernels for 61% -> 58%
where the time goes in v2:
time: 188 us
  Pallas kernels  115 us (61%)
  starting transfers between devices  54.1 us (29%)
  waiting for transfers between devices  17.8 us (9%)
    pallas_call x14, Pallas kernels, project(): pl.pallas_call(body, in_specs=[VMEM, ANYWHERE, VMEM] + [ANYWHERE] * len(a...  48.5 us
    pallas_call x5, Pallas kernels, correct(): pl.pallas_call(body, in_specs=[pl.BlockSpec(memory_space=pltpu.SMEM)] + [...  26.5 us
    ppermute x17, starting transfers between devices, send(): received.append(lax.ppermute(payload, 'gr', OUTER))  25.1 us
    ppermute x14, starting transfers between devices, add(): others.append(lax.ppermute(sums[-1], ('layers', 'gr'), INNER))  22.2 us
    pallas_call x31, Pallas kernels, whole(): pl.pallas_call(run, in_specs=[pl.BlockSpec(memory_space=pltpu.SMEM)] + [V...  20.9 us
    ppermute x17, waiting for transfers between devices, send(): received.append(lax.ppermute(payload, 'gr', OUTER))  14.9 us
    pallas_call x1, Pallas kernels, project_acts(): pl.pallas_call(body, grid_spec=pltpu.PrefetchScalarGridSpec(num_scalar_pr...  9.88 us
  transfers between devices with their start and end apart: 47, of which 12 were waited for; matrix products, arithmetic and copies ran while one was open for 0% of the time, Pallas kernels for 58%

profile of v2, /device:TPU:0, one launch (start us, length us, event | category | flops | bytes accessed | tf_op | source)
XLA Modules:
  0.0 188.1 jit_solution(12211031095550432134)
XLA Ops:
  0.5 2.5 %collective-permute-start.6 = (bf16[192,7168]{1,0:T(8,128)(2,1)}, bf16[192,7168]{1,0:T(8,128)(2,1)}, u32[]{:S(2)}, u32[]{:S(2)}) collective-permute-start(bf16[192,7168]{1,0:T(8,128)(2,1)} %refs_0_.1), channel_id=1, source_target_pairs={{0,2},{2,0},{1,3},{3,1},{4,6},{6,4},{5,7},{7,5},{8,10},{10,8},{9,1... | collective-permute-start | bytes 8257544 | tf_op jit(solution)/shard_map/ppermute | solution.py:441
  3.0 3.4 %fetch.1.refs_0_.block_ref = bf16[7168,512]{1,0:T(8,128)(2,1)S(1)} custom-call(bf16[7168,3584]{1,0:T(8,128)(2,1)} %basis_ref.31, s32[3]{0:T(128)S(1)} %pad_add_fusion.refs_0_.flags_ref), custom_call_target="tpu_custom_call" | custom-call | flops 10000000 | bytes 100000 | tf_op jit(solution)/shard_map/fetch/pallas_call | solution.py:212
  7.1 9.9 %project_acts.1 = (bf16[384,512]{1,0:T(8,128)(2,1)S(1)}, bf16[384,512]{1,0:T(8,128)(2,1)S(1)}, bf16[384,512]{1,0:T(8,128)(2,1)S(1)}, bf16[384,512]{1,0:T(8,128)(...) custom-call(s32[3]{0:T(128)S(1)} %pad_add_fusion.refs_0_.flags_ref, ...), custom_call_target="tpu_custom_call" | custom-call | flops 10000000 | bytes 100000 | tf_op jit(solution)/shard_map/project_acts/pallas_call | solution.py:285
  18.1 1.8 join.2.rows_ref.refs_0_
  19.9 3.5 %project_grads.14 = (bf16[384,512]{1,0:T(8,128)(2,1)S(1)}, bf16[7168,512]{1,0:T(8,128)(2,1)S(1)}) custom-call(bf16[384,7168]{1,0:T(8,128)(2,1)S(1)} %join.2.rows_ref.refs_0_, bf16[7168,3584]{1,0:T(8,128)(2,1)} %basis_ref.31, bf16[7168,512]{1,0:T(8,128)(2,1)S(1)} %fetch.1.refs_0_.block_ref, bf16[384,7168]{1,0:T(8,128)(2,1)S(1)} %join.2.rows_ref.refs_0_), custom_call_target="tpu_custom_call" | custom-call | flops 10000000 | bytes 100000 | tf_op jit(solution)/shard_map/project_grads/pallas_call | solution.py:245
  23.4 1.6 collective-permute-start.8
  25.1 3.5 %project_grads.15 = (bf16[384,512]{1,0:T(8,128)(2,1)S(1)}, bf16[7168,512]{1,0:T(8,128)(2,1)S(1)}) custom-call(bf16[384,7168]{1,0:T(8,128)(2,1)S(1)} %join.2.rows_ref.refs_0_, bf16[7168,3584]{1,0:T(8,128)(2,1)} %basis_ref.31, bf16[7168,512]{1,0:T(8,128)(2,1)S(1)} %get-tuple-element.65.block_ref, bf16[384,512]{1,0:T(8,128)(2,1)S(1)} %get-tuple-element.66.refs_0_), custom_call_target="tpu_custom_call" | custom-call | flops 10000000 | bytes 100000 | tf_op jit(solution)/shard_map/project_grads/pallas_call | solution.py:245
  30.0 3.5 %project_grads.16 = (bf16[384,512]{1,0:T(8,128)(2,1)S(1)}, bf16[7168,512]{1,0:T(8,128)(2,1)S(1)}) custom-call(bf16[384,7168]{1,0:T(8,128)(2,1)S(1)} %join.2.rows_ref.refs_0_, bf16[7168,3584]{1,0:T(8,128)(2,1)} %basis_ref.31, bf16[7168,512]{1,0:T(8,128)(2,1)S(1)} %get-tuple-element.68.block_ref, bf16[384,2048]{1,0:T(8,128)(2,1)S(1)} %add.25.refs_0_), custom_call_target="tpu_custom_call" | custom-call | flops 10000000 | bytes 100000 | tf_op jit(solution)/shard_map/project_grads/pallas_call | solution.py:245
  33.4 2.0 %collective-permute-done.8.refs_1_ = bf16[384,512]{1,0:T(8,128)(2,1)S(1)} collective-permute-done((bf16[384,512]{1,0:T(8,128)(2,1)S(1)}, bf16[384,512]{1,0:T(8,128)(2,1)S(1)}, u32[]{:S(2)}, u32[]{:S(2)}) %collective-permute-start.8) | collective-permute-done | bytes 393248 | tf_op jit(solution)/shard_map/ppermute | solution.py:414
  36.1 1.6 collective-permute-start.9
  37.7 1.6 collective-permute-start.7
  39.3 3.5 %project_grads.17 = (bf16[384,512]{1,0:T(8,128)(2,1)S(1)}, bf16[7168,512]{1,0:T(8,128)(2,1)S(1)}) custom-call(bf16[384,7168]{1,0:T(8,128)(2,1)S(1)} %join.2.rows_ref.refs_0_, bf16[7168,3584]{1,0:T(8,128)(2,1)} %basis_ref.31, bf16[7168,512]{1,0:T(8,128)(2,1)S(1)} %get-tuple-element.70.block_ref, bf16[384,512]{1,0:T(8,128)(2,1)S(1)} %add.26.refs_0_), custom_call_target="tpu_custom_call" | custom-call | flops 10000000 | bytes 100000 | tf_op jit(solution)/shard_map/project_grads/pallas_call | solution.py:245
  42.8 1.1 collective-permute-done.10.refs_1_
  44.5 1.6 collective-permute-start.13
  46.1 3.5 %project_grads.18 = (bf16[384,512]{1,0:T(8,128)(2,1)S(1)}, bf16[7168,512]{1,0:T(8,128)(2,1)S(1)}) custom-call(bf16[384,7168]{1,0:T(8,128)(2,1)S(1)} %join.2.rows_ref.refs_0_, bf16[7168,3584]{1,0:T(8,128)(2,1)} %basis_ref.31, bf16[7168,512]{1,0:T(8,128)(2,1)S(1)} %get-tuple-element.72.block_ref, bf16[384,512]{1,0:T(8,128)(2,1)S(1)} %add.27.refs_0_), custom_call_target="tpu_custom_call" | custom-call | flops 10000000 | bytes 100000 | tf_op jit(solution)/shard_map/project_grads/pallas_call | solution.py:245
  50.2 1.8 collective-permute-start.12
  52.6 1.6 collective-permute-start.11
  54.2 3.5 %project_grads.19 = (bf16[384,512]{1,0:T(8,128)(2,1)S(1)}, bf16[7168,512]{1,0:T(8,128)(2,1)S(1)}) custom-call(bf16[384,7168]{1,0:T(8,128)(2,1)S(1)} %join.2.rows_ref.refs_0_, bf16[7168,3584]{1,0:T(8,128)(2,1)} %basis_ref.31, bf16[7168,512]{1,0:T(8,128)(2,1)S(1)} %get-tuple-element.74.block_ref, bf16[384,512]{1,0:T(8,128)(2,1)S(1)} %add.28.refs_0_), custom_call_target="tpu_custom_call" | custom-call | flops 10000000 | bytes 100000 | tf_op jit(solution)/shard_map/project_grads/pallas_call | solution.py:245
  58.3 1.7 collective-permute-start.22
  60.8 1.8 collective-permute-start.21
  62.6 3.5 %project_grads.20 = (bf16[384,512]{1,0:T(8,128)(2,1)S(1)}, bf16[7168,512]{1,0:T(8,128)(2,1)S(1)}) custom-call(bf16[384,7168]{1,0:T(8,128)(2,1)S(1)} %join.2.rows_ref.refs_0_, bf16[7168,3584]{1,0:T(8,128)(2,1)} %basis_ref.31, bf16[7168,512]{1,0:T(8,128)(2,1)S(1)} %get-tuple-element.76.block_ref, bf16[384,512]{1,0:T(8,128)(2,1)S(1)} %add.29.refs_0_), custom_call_target="tpu_custom_call" | custom-call | flops 10000000 | bytes 100000 | tf_op jit(solution)/shard_map/project_grads/pallas_call | solution.py:245
  66.9 1.8 split.1
  69.8 1.5 collective-permute-done.21.refs_1_
  71.8 1.6 collective-permute-start.25
  74.6 2.3 %collective-permute-start.24 = (bf16[384,512]{1,0:T(8,128)(2,1)S(1)}, bf16[384,512]{1,0:T(8,128)(2,1)S(1)}, u32[]{:S(2)}, u32[]{:S(2)}) collective-permute-start(bf16[384,512]{1,0:T(8,128)(2,1)S(1)} %add.30.refs_3_.refs_0_), channel_id=1, source_target_pairs={{4,8},{8,4},{20,24},{24,20},{0,16},{16,0},{12,28},{28,12},{5,9},{9... | collective-permute-start | bytes 1179656 | tf_op jit(solution)/shard_map/ppermute | solution.py:420
  77.4 1.8 collective-permute-start.23
  79.2 1.9 join.3.rows_ref.refs_0_
  81.1 3.5 %project_grads.21 = (bf16[384,512]{1,0:T(8,128)(2,1)S(1)}, bf16[7168,512]{1,0:T(8,128)(2,1)S(1)}) custom-call(bf16[384,7168]{1,0:T(8,128)(2,1)S(1)} %join.3.rows_ref.refs_0_, bf16[7168,3584]{1,0:T(8,128)(2,1)} %basis_ref.31, bf16[7168,512]{1,0:T(8,128)(2,1)S(1)} %get-tuple-element.85.block_ref, bf16[384,7168]{1,0:T(8,128)(2,1)S(1)} %join.3.rows_ref.refs_0_), custom_call_target="tpu_custom_call" | custom-call | flops 10000000 | bytes 100000 | tf_op jit(solution)/shard_map/project_grads/pallas_call | solution.py:245
  85.2 1.0 collective-permute-start.26
  86.8 1.7 collective-permute-start.29
  88.5 3.7 %collective-permute-done.23.refs_1_ = bf16[384,512]{1,0:T(8,128)(2,1)S(1)} collective-permute-done((bf16[384,512]{1,0:T(8,128)(2,1)S(1)}, bf16[384,512]{1,0:T(8,128)(2,1)S(1)}, u32[]{:S(2)}, u32[]{:S(2)}) %collective-permute-start.23) | collective-permute-done | bytes 393248 | tf_op jit(solution)/shard_map/ppermute | solution.py:414
  92.8 1.8 collective-permute-start.28
  94.6 3.5 %project_grads.22 = (bf16[384,512]{1,0:T(8,128)(2,1)S(1)}, bf16[7168,512]{1,0:T(8,128)(2,1)S(1)}) custom-call(bf16[384,7168]{1,0:T(8,128)(2,1)S(1)} %join.3.rows_ref.refs_0_, bf16[7168,3584]{1,0:T(8,128)(2,1)} %basis_ref.31, bf16[7168,512]{1,0:T(8,128)(2,1)S(1)} %get-tuple-element.86.block_ref, bf16[384,512]{1,0:T(8,128)(2,1)S(1)} %add.32.refs_0_), custom_call_target="tpu_custom_call" | custom-call | flops 10000000 | bytes 100000 | tf_op jit(solution)/shard_map/project_grads/pallas_call | solution.py:245
  98.7 1.7 collective-permute-start.27
  101.0 1.8 collective-permute-start.32
  102.8 3.5 %project_grads.23 = (bf16[384,512]{1,0:T(8,128)(2,1)S(1)}, bf16[7168,512]{1,0:T(8,128)(2,1)S(1)}) custom-call(bf16[384,7168]{1,0:T(8,128)(2,1)S(1)} %join.3.rows_ref.refs_0_, bf16[7168,3584]{1,0:T(8,128)(2,1)} %basis_ref.31, bf16[7168,512]{1,0:T(8,128)(2,1)S(1)} %get-tuple-element.89.block_ref, bf16[384,512]{1,0:T(8,128)(2,1)S(1)} %add.33.refs_0_), custom_call_target="tpu_custom_call" | custom-call | flops 10000000 | bytes 100000 | tf_op jit(solution)/shard_map/project_grads/pallas_call | solution.py:245
  106.9 1.7 collective-permute-start.31
  109.3 2.0 %collective-permute-start.30 = (bf16[384,512]{1,0:T(8,128)(2,1)S(1)}, bf16[384,512]{1,0:T(8,128)(2,1)S(1)}, u32[]{:S(2)}, u32[]{:S(2)}) collective-permute-start(bf16[384,512]{1,0:T(8,128)(2,1)S(1)} %add.34.refs_0_), channel_id=1, source_target_pairs={{4,8},{8,4},{20,24},{24,20},{0,16},{16,0},{12,28},{28,12},{5,9},{9... | collective-permute-start | bytes 1179656 | tf_op jit(solution)/shard_map/ppermute | solution.py:420
  111.2 3.5 %project_grads.24 = (bf16[384,512]{1,0:T(8,128)(2,1)S(1)}, bf16[7168,512]{1,0:T(8,128)(2,1)S(1)}) custom-call(bf16[384,7168]{1,0:T(8,128)(2,1)S(1)} %join.3.rows_ref.refs_0_, bf16[7168,3584]{1,0:T(8,128)(2,1)} %basis_ref.31, bf16[7168,512]{1,0:T(8,128)(2,1)S(1)} %get-tuple-element.91.block_ref, bf16[384,512]{1,0:T(8,128)(2,1)S(1)} %add.34.refs_0_), custom_call_target="tpu_custom_call" | custom-call | flops 10000000 | bytes 100000 | tf_op jit(solution)/shard_map/project_grads/pallas_call | solution.py:245
  115.3 1.7 collective-permute-start.37
  117.0 1.0 collective-permute-done.31.refs_1_
  118.7 2.2 %collective-permute-start.36 = (bf16[384,512]{1,0:T(8,128)(2,1)S(1)}, bf16[384,512]{1,0:T(8,128)(2,1)S(1)}, u32[]{:S(2)}, u32[]{:S(2)}) collective-permute-start(bf16[384,512]{1,0:T(8,128)(2,1)S(1)} %add.35.refs_0_), channel_id=1, source_target_pairs={{4,8},{8,4},{20,24},{24,20},{0,16},{16,0},{12,28},{28,12},{5,9},{9... | collective-permute-start | bytes 1179656 | tf_op jit(solution)/shard_map/ppermute | solution.py:420
  120.9 3.5 %project_grads.25 = (bf16[384,512]{1,0:T(8,128)(2,1)S(1)}, bf16[7168,512]{1,0:T(8,128)(2,1)S(1)}) custom-call(bf16[384,7168]{1,0:T(8,128)(2,1)S(1)} %join.3.rows_ref.refs_0_, bf16[7168,3584]{1,0:T(8,128)(2,1)} %basis_ref.31, bf16[7168,512]{1,0:T(8,128)(2,1)S(1)} %get-tuple-element.92.block_ref, bf16[384,512]{1,0:T(8,128)(2,1)S(1)} %add.35.refs_0_), custom_call_target="tpu_custom_call" | custom-call | flops 10000000 | bytes 100000 | tf_op jit(solution)/shard_map/project_grads/pallas_call | solution.py:245
  125.0 1.6 collective-permute-start.35
  126.6 1.0 square.24
  128.8 1.3 collective-permute-start.40
  130.1 3.5 %project_grads.26 = (bf16[384,512]{1,0:T(8,128)(2,1)S(1)}, bf16[7168,512]{1,0:T(8,128)(2,1)S(1)}) custom-call(bf16[384,7168]{1,0:T(8,128)(2,1)S(1)} %join.3.rows_ref.refs_0_, bf16[7168,3584]{1,0:T(8,128)(2,1)} %basis_ref.31, bf16[7168,512]{1,0:T(8,128)(2,1)S(1)} %get-tuple-element.97.block_ref, bf16[384,512]{1,0:T(8,128)(2,1)S(1)} %add.36.refs_0_), custom_call_target="tpu_custom_call" | custom-call | flops 10000000 | bytes 100000 | tf_op jit(solution)/shard_map/project_grads/pallas_call | solution.py:245
  134.4 1.6 collective-permute-start.39
  136.6 1.1 collective-permute-start.38
  137.7 3.4 %project_grads.27.refs_2_.refs_3_.refs_0_ = bf16[384,512]{1,0:T(8,128)(2,1)S(1)} custom-call(bf16[384,7168]{1,0:T(8,128)(2,1)S(1)} %join.3.rows_ref.refs_0_, bf16[7168,3584]{1,0:T(8,128)(2,1)} %basis_ref.31, bf16[7168,512]{1,0:T(8,128)(2,1)S(1)} %get-tuple-element.99.block_ref, bf16[384,512]{1,0:T(8,128)(2,1)S(1)} %add.37.refs_0_), custom_call_target="tpu_custom_call" | custom-call | flops 10000000 | bytes 100000 | tf_op jit(solution)/shard_map/project_grads/pallas_call | solution.py:245
  141.7 1.0 collective-permute-start.41
  142.7 3.7 %collective-permute-done.39.refs_1_.refs_7_ = bf16[384,512]{1,0:T(8,128)(2,1)S(1)} collective-permute-done((bf16[384,512]{1,0:T(8,128)(2,1)S(1)}, bf16[384,512]{1,0:T(8,128)(2,1)S(1)}, u32[]{:S(2)}, u32[]{:S(2)}) %collective-permute-start.39) | collective-permute-done | bytes 393248 | tf_op jit(solution)/shard_map/ppermute | solution.py:414
  148.0 1.3 collective-permute-done.38.refs_1_
  149.9 1.4 stack.22.act_ref.refs_4_
  151.4 4.0 %correct.5 = (bf16[2048,3584]{1,0:T(8,128)(2,1)}, bf16[16,128]{1,0:T(8,128)(2,1)S(1)}) custom-call(s32[3]{0:T(128)S(1)} %pad_add_fusion.refs_0_.flags_ref, bf16[2048,768]{1,0:T(8,128)(2,1)S(1)} %stack.22.act_ref.refs_4_, bf16[384,512]{1,0:T(8,128)(2,1)S(1)} %copy-done.1, bf16[384,512]{1,0:T(8,128)(2,1)S(1)} %copy-done.4, ...), custom_call_target="tpu_custom_call" | custom-call | flops 10000000 | bytes 100000 | tf_op jit(solution)/shard_map/correct/pallas_call | solution.py:351
  156.1 1.3 collective-permute-start.42
  157.4 1.4 collective-permute-start.46
  160.1 6.9 %correct.6 = (bf16[2048,3584]{1,0:T(8,128)(2,1)}, bf16[16,128]{1,0:T(8,128)(2,1)S(1)}) custom-call(s32[3]{0:T(128)S(1)} %pad_add_fusion.refs_0_.flags_ref, bf16[2048,768]{1,0:T(8,128)(2,1)S(1)} %stack.22.act_ref.refs_4_, bf16[384,512]{1,0:T(8,128)(2,1)S(1)} %square.16.refs_2_.refs_0_, ...), custom_call_target="tpu_custom_call", output_to_operand_aliasing={{0}: (10, {})} | custom-call | flops 10000000 | bytes 100000 | tf_op jit(solution)/shard_map/correct/pallas_call | solution.py:351
  167.7 1.5 collective-permute-start.44
  169.4 6.9 %correct.7 = (bf16[2048,3584]{1,0:T(8,128)(2,1)}, bf16[16,128]{1,0:T(8,128)(2,1)S(1)}) custom-call(s32[3]{0:T(128)S(1)} %pad_add_fusion.refs_0_.flags_ref, bf16[2048,768]{1,0:T(8,128)(2,1)S(1)} %stack.22.act_ref.refs_4_, bf16[384,512]{1,0:T(8,128)(2,1)S(1)} %square.18.refs_8_.refs_0_, ...), custom_call_target="tpu_custom_call", output_to_operand_aliasing={{0}: (10, {})} | custom-call | flops 10000000 | bytes 100000 | tf_op jit(solution)/shard_map/correct/pallas_call | solution.py:351
  176.4 1.5 collective-permute-done.45.refs_3_
  177.9 4.0 %correct.8 = (bf16[2048,3584]{1,0:T(8,128)(2,1)}, bf16[16,128]{1,0:T(8,128)(2,1)S(1)}) custom-call(s32[3]{0:T(128)S(1)} %pad_add_fusion.refs_0_.flags_ref, bf16[2048,768]{1,0:T(8,128)(2,1)S(1)} %stack.22.act_ref.refs_4_, bf16[384,512]{1,0:T(8,128)(2,1)S(1)} %square.20.refs_2_.refs_0_, ...), custom_call_target="tpu_custom_call", output_to_operand_aliasing={{0}: (6, {})} | custom-call | flops 10000000 | bytes 100000 | tf_op jit(solution)/shard_map/correct/pallas_call | solution.py:351
  181.9 1.4 collective-permute-done.44.refs_3_
  183.3 4.6 %correct.9 = (bf16[2048,3584]{1,0:T(8,128)(2,1)}, bf16[16,128]{1,0:T(8,128)(2,1)}) custom-call(s32[3]{0:T(128)S(1)} %pad_add_fusion.refs_0_.flags_ref, bf16[2048,768]{1,0:T(8,128)(2,1)S(1)} %stack.22.act_ref.refs_4_, bf16[384,512]{1,0:T(8,128)(2,1)S(1)} %square.21.refs_2_.refs_0_, ...), custom_call_target="tpu_custom_call", output_to_operand_aliasing={{0}: (6, {})} | custom-call | flops 10000000 | bytes 100000 | tf_op jit(solution)/shard_map/correct/pallas_call | solution.py:351
  (96 shorter events, 26.3 us)
Async XLA Ops:
  0.0 17.8 %collective-permute-start.4 = (bf16[192,7168]{1,0:T(8,128)(2,1)}, bf16[192,7168]{1,0:T(8,128)(2,1)S(1)}, u32[]{:S(2)}, u32[]{:S(2)}) collective-permute-start(bf16[192,7168]{1,0:T(8,128)(2,1)} %refs_0_.1), channel_id=1, source_target_pairs={{0,1},{1,0},{2,3},{3,2},{4,5},{5,4},{6,7},{7,6},{8,9},{9,8},{10,11... | collective-permute-start | bytes 8257544 | tf_op jit(solution)/shard_map/ppermute | solution.py:385
  0.5 66.4 %collective-permute-start.6 = (bf16[192,7168]{1,0:T(8,128)(2,1)}, bf16[192,7168]{1,0:T(8,128)(2,1)}, u32[]{:S(2)}, u32[]{:S(2)}) collective-permute-start(bf16[192,7168]{1,0:T(8,128)(2,1)} %refs_0_.1), channel_id=1, source_target_pairs={{0,2},{2,0},{1,3},{3,1},{4,6},{6,4},{5,7},{7,5},{8,10},{10,8},{9,1... | collective-permute-start | bytes 8257544 | tf_op jit(solution)/shard_map/ppermute | solution.py:441
  3.0 4.1 %copy-start.2 = (bf16[768,2048]{1,0:T(8,128)(2,1)S(1)}, bf16[768,2048]{1,0:T(8,128)(2,1)}, u32[]{:S(2)}) copy-start(bf16[768,2048]{1,0:T(8,128)(2,1)} %acts_ref.1) | copy-start | bytes 9437188
  17.0 6.4 %collective-permute-start = (bf16[384,512]{1,0:T(8,128)(2,1)S(1)}, bf16[384,512]{1,0:T(8,128)(2,1)S(1)}, u32[]{:S(2)}, u32[]{:S(2)}) collective-permute-start(bf16[384,512]{1,0:T(8,128)(2,1)S(1)} %get-tuple-element.61), channel_id=1, source_target_pairs={{0,1},{1,0},{2,3},{3,2},{4,5},{5,4},{6,7},{7,6},{8,9},{9,8},{10,11... | collective-permute-start | bytes 1179656 | tf_op jit(solution)/shard_map/ppermute | solution.py:448
  17.3 11.2 %collective-permute-start.1 = (bf16[384,512]{1,0:T(8,128)(2,1)S(1)}, bf16[384,512]{1,0:T(8,128)(2,1)S(1)}, u32[]{:S(2)}, u32[]{:S(2)}) collective-permute-start(bf16[384,512]{1,0:T(8,128)(2,1)S(1)} %get-tuple-element.62), channel_id=1, source_target_pairs={{0,1},{1,0},{2,3},{3,2},{4,5},{5,4},{6,7},{7,6},{8,9},{9,8},{10,11... | collective-permute-start | bytes 1179656 | tf_op jit(solution)/shard_map/ppermute | solution.py:448
  17.6 11.4 %collective-permute-start.2 = (bf16[384,512]{1,0:T(8,128)(2,1)S(1)}, bf16[384,512]{1,0:T(8,128)(2,1)S(1)}, u32[]{:S(2)}, u32[]{:S(2)}) collective-permute-start(bf16[384,512]{1,0:T(8,128)(2,1)S(1)} %get-tuple-element.63), channel_id=1, source_target_pairs={{0,1},{1,0},{2,3},{3,2},{4,5},{5,4},{6,7},{7,6},{8,9},{9,8},{10,11... | collective-permute-start | bytes 1179656 | tf_op jit(solution)/shard_map/ppermute | solution.py:448
  17.8 11.2 %collective-permute-start.3 = (bf16[384,512]{1,0:T(8,128)(2,1)S(1)}, bf16[384,512]{1,0:T(8,128)(2,1)S(1)}, u32[]{:S(2)}, u32[]{:S(2)}) collective-permute-start(bf16[384,512]{1,0:T(8,128)(2,1)S(1)} %get-tuple-element.64), channel_id=1, source_target_pairs={{0,1},{1,0},{2,3},{3,2},{4,5},{5,4},{6,7},{7,6},{8,9},{9,8},{10,11... | collective-permute-start | bytes 1179656 | tf_op jit(solution)/shard_map/ppermute | solution.py:448
  23.4 12.0 %collective-permute-start.8 = (bf16[384,512]{1,0:T(8,128)(2,1)S(1)}, bf16[384,512]{1,0:T(8,128)(2,1)S(1)}, u32[]{:S(2)}, u32[]{:S(2)}) collective-permute-start(bf16[384,512]{1,0:T(8,128)(2,1)S(1)} %get-tuple-element.66.refs_0_), channel_id=1, source_target_pairs={{0,4},{4,0},{8,12},{12,8},{1,5},{5,1},{9,13},{13,9},{2,6},{6,2},{1... | collective-permute-start | bytes 1179656 | tf_op jit(solution)/shard_map/ppermute | solution.py:414
  28.5 15.3 %collective-permute-start.10 = (bf16[384,512]{1,0:T(8,128)(2,1)S(1)}, bf16[384,512]{1,0:T(8,128)(2,1)S(1)}, u32[]{:S(2)}, u32[]{:S(2)}) collective-permute-start(bf16[384,512]{1,0:T(8,128)(2,1)S(1)} %get-tuple-element.67.refs_8_.refs_0_), channel_id=1, source_target_pairs={{0,4},{4,0},{8,12},{12,8},{1,5},{5,1},{9,13},{13,9},{2,6},{6,2},{1... | collective-permute-start | bytes 1179656 | tf_op jit(solution)/shard_map/ppermute | solution.py:414
  36.1 13.5 %collective-permute-start.9 = (bf16[384,512]{1,0:T(8,128)(2,1)S(1)}, bf16[384,512]{1,0:T(8,128)(2,1)S(1)}, u32[]{:S(2)}, u32[]{:S(2)}) collective-permute-start(bf16[384,512]{1,0:T(8,128)(2,1)S(1)} %add.26.refs_0_), channel_id=1, source_target_pairs={{4,8},{8,4},{20,24},{24,20},{0,16},{16,0},{12,28},{28,12},{5,9},{9... | collective-permute-start | bytes 1179656 | tf_op jit(solution)/shard_map/ppermute | solution.py:420
  37.7 14.3 %collective-permute-start.7 = (bf16[384,512]{1,0:T(8,128)(2,1)S(1)}, bf16[384,512]{1,0:T(8,128)(2,1)S(1)}, u32[]{:S(2)}, u32[]{:S(2)}) collective-permute-start(bf16[384,512]{1,0:T(8,128)(2,1)S(1)} %get-tuple-element.69.refs_2_.refs_0_), channel_id=1, source_target_pairs={{0,4},{4,0},{8,12},{12,8},{1,5},{5,1},{9,13},{13,9},{2,6},{6,2},{1... | collective-permute-start | bytes 1179656 | tf_op jit(solution)/shard_map/ppermute | solution.py:414
  44.5 13.2 %collective-permute-start.13 = (bf16[384,512]{1,0:T(8,128)(2,1)S(1)}, bf16[384,512]{1,0:T(8,128)(2,1)S(1)}, u32[]{:S(2)}, u32[]{:S(2)}) collective-permute-start(bf16[384,512]{1,0:T(8,128)(2,1)S(1)} %add.27.refs_0_), channel_id=1, source_target_pairs={{4,8},{8,4},{20,24},{24,20},{0,16},{16,0},{12,28},{28,12},{5,9},{9... | collective-permute-start | bytes 1179656 | tf_op jit(solution)/shard_map/ppermute | solution.py:420
  50.1 7.5 %copy-start = (bf16[384,512]{1,0:T(8,128)(2,1)}, bf16[384,512]{1,0:T(8,128)(2,1)S(1)}, u32[]{:S(2)}) copy-start(bf16[384,512]{1,0:T(8,128)(2,1)S(1)} %square.15.refs_2_.refs_0_) | copy-start | bytes 1179652
  50.2 10.0 %collective-permute-start.12 = (bf16[384,512]{1,0:T(8,128)(2,1)S(1)}, bf16[384,512]{1,0:T(8,128)(2,1)S(1)}, u32[]{:S(2)}, u32[]{:S(2)}) collective-permute-start(bf16[384,512]{1,0:T(8,128)(2,1)S(1)} %square.15.refs_2_.refs_0_), channel_id=1, source_target_pairs={{0,4},{4,0},{8,12},{12,8},{1,5},{5,1},{9,13},{13,9},{2,6},{6,2},{1... | collective-permute-start | bytes 1179656 | tf_op jit(solution)/shard_map/ppermute | solution.py:414
  52.6 13.5 %collective-permute-start.11 = (bf16[384,512]{1,0:T(8,128)(2,1)S(1)}, bf16[384,512]{1,0:T(8,128)(2,1)S(1)}, u32[]{:S(2)}, u32[]{:S(2)}) collective-permute-start(bf16[384,512]{1,0:T(8,128)(2,1)S(1)} %add.28.refs_0_), channel_id=1, source_target_pairs={{4,8},{8,4},{20,24},{24,20},{0,16},{16,0},{12,28},{28,12},{5,9},{9... | collective-permute-start | bytes 1179656 | tf_op jit(solution)/shard_map/ppermute | solution.py:420
  58.3 11.1 %collective-permute-start.22 = (bf16[384,512]{1,0:T(8,128)(2,1)S(1)}, bf16[384,512]{1,0:T(8,128)(2,1)S(1)}, u32[]{:S(2)}, u32[]{:S(2)}) collective-permute-start(bf16[384,512]{1,0:T(8,128)(2,1)S(1)} %square.16.refs_2_.refs_0_), channel_id=1, source_target_pairs={{0,4},{4,0},{8,12},{12,8},{1,5},{5,1},{9,13},{13,9},{2,6},{6,2},{1... | collective-permute-start | bytes 1179656 | tf_op jit(solution)/shard_map/ppermute | solution.py:414
  60.2 5.9 %copy-start.3 = (bf16[384,512]{1,0:T(8,128)(2,1)}, bf16[384,512]{1,0:T(8,128)(2,1)S(1)}, u32[]{:S(2)}) copy-start(bf16[384,512]{1,0:T(8,128)(2,1)S(1)} %collective-permute-done.12.refs_1_) | copy-start | bytes 1179652
  60.8 10.4 %collective-permute-start.21 = (bf16[384,512]{1,0:T(8,128)(2,1)S(1)}, bf16[384,512]{1,0:T(8,128)(2,1)S(1)}, u32[]{:S(2)}, u32[]{:S(2)}) collective-permute-start(bf16[384,512]{1,0:T(8,128)(2,1)S(1)} %add.29.refs_0_), channel_id=1, source_target_pairs={{4,8},{8,4},{20,24},{24,20},{0,16},{16,0},{12,28},{28,12},{5,9},{9... | collective-permute-start | bytes 1179656 | tf_op jit(solution)/shard_map/ppermute | solution.py:420
  68.7 2.6 %collective-permute-start.14 = (bf16[192,1024]{1,0:T(8,128)(2,1)S(1)}, bf16[192,1024]{1,0:T(8,128)(2,1)S(1)}, u32[]{:S(2)}, u32[]{:S(2)}) collective-permute-start(bf16[192,1024]{1,0:T(8,128)(2,1)S(1)} %get-tuple-element.78), channel_id=1, source_target_pairs={{0,1},{1,0},{2,3},{3,2},{4,5},{5,4},{6,7},{7,6},{8,9},{9,8},{10,11... | collective-permute-start | bytes 1179656 | tf_op jit(solution)/shard_map/ppermute | solution.py:467
  68.8 3.0 %collective-permute-start.15 = (bf16[192,1024]{1,0:T(8,128)(2,1)S(1)}, bf16[192,1024]{1,0:T(8,128)(2,1)S(1)}, u32[]{:S(2)}, u32[]{:S(2)}) collective-permute-start(bf16[192,1024]{1,0:T(8,128)(2,1)S(1)} %get-tuple-element.79), channel_id=1, source_target_pairs={{0,1},{1,0},{2,3},{3,2},{4,5},{5,4},{6,7},{7,6},{8,9},{9,8},{10,11... | collective-permute-start | bytes 1179656 | tf_op jit(solution)/shard_map/ppermute | solution.py:467
  69.3 2.6 %collective-permute-start.16 = (bf16[192,1024]{1,0:T(8,128)(2,1)S(1)}, bf16[192,1024]{1,0:T(8,128)(2,1)S(1)}, u32[]{:S(2)}, u32[]{:S(2)}) collective-permute-start(bf16[192,1024]{1,0:T(8,128)(2,1)S(1)} %get-tuple-element.80), channel_id=1, source_target_pairs={{0,1},{1,0},{2,3},{3,2},{4,5},{5,4},{6,7},{7,6},{8,9},{9,8},{10,11... | collective-permute-start | bytes 1179656 | tf_op jit(solution)/shard_map/ppermute | solution.py:467
  69.3 4.0 %collective-permute-start.17 = (bf16[192,1024]{1,0:T(8,128)(2,1)S(1)}, bf16[192,1024]{1,0:T(8,128)(2,1)S(1)}, u32[]{:S(2)}, u32[]{:S(2)}) collective-permute-start(bf16[192,1024]{1,0:T(8,128)(2,1)S(1)} %get-tuple-element.81), channel_id=1, source_target_pairs={{0,1},{1,0},{2,3},{3,2},{4,5},{5,4},{6,7},{7,6},{8,9},{9,8},{10,11... | collective-permute-start | bytes 1179656 | tf_op jit(solution)/shard_map/ppermute | solution.py:467
  71.2 3.4 %collective-permute-start.18 = (bf16[192,1024]{1,0:T(8,128)(2,1)S(1)}, bf16[192,1024]{1,0:T(8,128)(2,1)S(1)}, u32[]{:S(2)}, u32[]{:S(2)}) collective-permute-start(bf16[192,1024]{1,0:T(8,128)(2,1)S(1)} %get-tuple-element.82), channel_id=1, source_target_pairs={{0,1},{1,0},{2,3},{3,2},{4,5},{5,4},{6,7},{7,6},{8,9},{9,8},{10,11... | collective-permute-start | bytes 1179656 | tf_op jit(solution)/shard_map/ppermute | solution.py:467
  71.2 6.2 %collective-permute-start.19 = (bf16[192,1024]{1,0:T(8,128)(2,1)S(1)}, bf16[192,1024]{1,0:T(8,128)(2,1)S(1)}, u32[]{:S(2)}, u32[]{:S(2)}) collective-permute-start(bf16[192,1024]{1,0:T(8,128)(2,1)S(1)} %get-tuple-element.83), channel_id=1, source_target_pairs={{0,1},{1,0},{2,3},{3,2},{4,5},{5,4},{6,7},{7,6},{8,9},{9,8},{10,11... | collective-permute-start | bytes 1179656 | tf_op jit(solution)/shard_map/ppermute | solution.py:467
  71.7 7.5 %collective-permute-start.20 = (bf16[192,1024]{1,0:T(8,128)(2,1)S(1)}, bf16[192,1024]{1,0:T(8,128)(2,1)S(1)}, u32[]{:S(2)}, u32[]{:S(2)}) collective-permute-start(bf16[192,1024]{1,0:T(8,128)(2,1)S(1)} %get-tuple-element.84.refs_2_), channel_id=1, source_target_pairs={{0,1},{1,0},{2,3},{3,2},{4,5},{5,4},{6,7},{7,6},{8,9},{9,8},{10,11... | collective-permute-start | bytes 1179656 | tf_op jit(solution)/shard_map/ppermute | solution.py:467
  71.8 12.7 %collective-permute-start.25 = (bf16[384,512]{1,0:T(8,128)(2,1)S(1)}, bf16[384,512]{1,0:T(8,128)(2,1)S(1)}, u32[]{:S(2)}, u32[]{:S(2)}) collective-permute-start(bf16[384,512]{1,0:T(8,128)(2,1)S(1)} %square.17.refs_0_.refs_4_), channel_id=1, source_target_pairs={{0,4},{4,0},{8,12},{12,8},{1,5},{5,1},{9,13},{13,9},{2,6},{6,2},{1... | collective-permute-start | bytes 1179656 | tf_op jit(solution)/shard_map/ppermute | solution.py:414
  73.4 53.2 %collective-permute-start.5 = (bf16[384,2048]{1,0:T(8,128)(2,1)S(1)}, bf16[384,2048]{1,0:T(8,128)(2,1)S(1)}, u32[]{:S(2)}, u32[]{:S(2)}) collective-permute-start(bf16[384,2048]{1,0:T(8,128)(2,1)S(1)} %add.25.refs_0_), channel_id=1, source_target_pairs={{0,2},{2,0},{1,3},{3,1},{4,6},{6,4},{5,7},{7,5},{8,10},{10,8},{9,1... | collective-permute-start | bytes 4718600 | tf_op jit(solution)/shard_map/ppermute | solution.py:456
  74.6 11.6 %collective-permute-start.24 = (bf16[384,512]{1,0:T(8,128)(2,1)S(1)}, bf16[384,512]{1,0:T(8,128)(2,1)S(1)}, u32[]{:S(2)}, u32[]{:S(2)}) collective-permute-start(bf16[384,512]{1,0:T(8,128)(2,1)S(1)} %add.30.refs_3_.refs_0_), channel_id=1, source_target_pairs={{4,8},{8,4},{20,24},{24,20},{0,16},{16,0},{12,28},{28,12},{5,9},{9... | collective-permute-start | bytes 1179656 | tf_op jit(solution)/shard_map/ppermute | solution.py:420
  77.4 14.7 %collective-permute-start.23 = (bf16[384,512]{1,0:T(8,128)(2,1)S(1)}, bf16[384,512]{1,0:T(8,128)(2,1)S(1)}, u32[]{:S(2)}, u32[]{:S(2)}) collective-permute-start(bf16[384,512]{1,0:T(8,128)(2,1)S(1)} %square.18.refs_8_.refs_0_), channel_id=1, source_target_pairs={{0,4},{4,0},{8,12},{12,8},{1,5},{5,1},{9,13},{13,9},{2,6},{6,2},{1... | collective-permute-start | bytes 1179656 | tf_op jit(solution)/shard_map/ppermute | solution.py:414
  85.2 12.9 %collective-permute-start.26 = (bf16[384,512]{1,0:T(8,128)(2,1)S(1)}, bf16[384,512]{1,0:T(8,128)(2,1)S(1)}, u32[]{:S(2)}, u32[]{:S(2)}) collective-permute-start(bf16[384,512]{1,0:T(8,128)(2,1)S(1)} %add.31.refs_3_.refs_0_), channel_id=1, source_target_pairs={{4,8},{8,4},{20,24},{24,20},{0,16},{16,0},{12,28},{28,12},{5,9},{9... | collective-permute-start | bytes 1179656 | tf_op jit(solution)/shard_map/ppermute | solution.py:420
  86.8 13.6 %collective-permute-start.29 = (bf16[384,512]{1,0:T(8,128)(2,1)S(1)}, bf16[384,512]{1,0:T(8,128)(2,1)S(1)}, u32[]{:S(2)}, u32[]{:S(2)}) collective-permute-start(bf16[384,512]{1,0:T(8,128)(2,1)S(1)} %square.19.refs_2_.refs_4_), channel_id=1, source_target_pairs={{0,4},{4,0},{8,12},{12,8},{1,5},{5,1},{9,13},{13,9},{2,6},{6,2},{1... | collective-permute-start | bytes 1179656 | tf_op jit(solution)/shard_map/ppermute | solution.py:414
  92.8 13.5 %collective-permute-start.28 = (bf16[384,512]{1,0:T(8,128)(2,1)S(1)}, bf16[384,512]{1,0:T(8,128)(2,1)S(1)}, u32[]{:S(2)}, u32[]{:S(2)}) collective-permute-start(bf16[384,512]{1,0:T(8,128)(2,1)S(1)} %add.32.refs_0_), channel_id=1, source_target_pairs={{4,8},{8,4},{20,24},{24,20},{0,16},{16,0},{12,28},{28,12},{5,9},{9... | collective-permute-start | bytes 1179656 | tf_op jit(solution)/shard_map/ppermute | solution.py:420
  98.7 10.0 %collective-permute-start.27 = (bf16[384,512]{1,0:T(8,128)(2,1)S(1)}, bf16[384,512]{1,0:T(8,128)(2,1)S(1)}, u32[]{:S(2)}, u32[]{:S(2)}) collective-permute-start(bf16[384,512]{1,0:T(8,128)(2,1)S(1)} %square.20.refs_2_.refs_0_), channel_id=1, source_target_pairs={{0,4},{4,0},{8,12},{12,8},{1,5},{5,1},{9,13},{13,9},{2,6},{6,2},{1... | collective-permute-start | bytes 1179656 | tf_op jit(solution)/shard_map/ppermute | solution.py:414
  101.0 13.7 %collective-permute-start.32 = (bf16[384,512]{1,0:T(8,128)(2,1)S(1)}, bf16[384,512]{1,0:T(8,128)(2,1)S(1)}, u32[]{:S(2)}, u32[]{:S(2)}) collective-permute-start(bf16[384,512]{1,0:T(8,128)(2,1)S(1)} %add.33.refs_0_), channel_id=1, source_target_pairs={{4,8},{8,4},{20,24},{24,20},{0,16},{16,0},{12,28},{28,12},{5,9},{9... | collective-permute-start | bytes 1179656 | tf_op jit(solution)/shard_map/ppermute | solution.py:420
  106.9 11.2 %collective-permute-start.31 = (bf16[384,512]{1,0:T(8,128)(2,1)S(1)}, bf16[384,512]{1,0:T(8,128)(2,1)S(1)}, u32[]{:S(2)}, u32[]{:S(2)}) collective-permute-start(bf16[384,512]{1,0:T(8,128)(2,1)S(1)} %square.21.refs_2_.refs_0_), channel_id=1, source_target_pairs={{0,4},{4,0},{8,12},{12,8},{1,5},{5,1},{9,13},{13,9},{2,6},{6,2},{1... | collective-permute-start | bytes 1179656 | tf_op jit(solution)/shard_map/ppermute | solution.py:414
  109.3 15.1 %collective-permute-start.30 = (bf16[384,512]{1,0:T(8,128)(2,1)S(1)}, bf16[384,512]{1,0:T(8,128)(2,1)S(1)}, u32[]{:S(2)}, u32[]{:S(2)}) collective-permute-start(bf16[384,512]{1,0:T(8,128)(2,1)S(1)} %add.34.refs_0_), channel_id=1, source_target_pairs={{4,8},{8,4},{20,24},{24,20},{0,16},{16,0},{12,28},{28,12},{5,9},{9... | collective-permute-start | bytes 1179656 | tf_op jit(solution)/shard_map/ppermute | solution.py:420
  115.3 12.8 %collective-permute-start.37 = (bf16[384,512]{1,0:T(8,128)(2,1)S(1)}, bf16[384,512]{1,0:T(8,128)(2,1)S(1)}, u32[]{:S(2)}, u32[]{:S(2)}) collective-permute-start(bf16[384,512]{1,0:T(8,128)(2,1)S(1)} %square.22.refs_2_), channel_id=1, source_target_pairs={{0,4},{4,0},{8,12},{12,8},{1,5},{5,1},{9,13},{13,9},{2,6},{6,2},{1... | collective-permute-start | bytes 1179656 | tf_op jit(solution)/shard_map/ppermute | solution.py:414
  118.7 14.9 %collective-permute-start.36 = (bf16[384,512]{1,0:T(8,128)(2,1)S(1)}, bf16[384,512]{1,0:T(8,128)(2,1)S(1)}, u32[]{:S(2)}, u32[]{:S(2)}) collective-permute-start(bf16[384,512]{1,0:T(8,128)(2,1)S(1)} %add.35.refs_0_), channel_id=1, source_target_pairs={{4,8},{8,4},{20,24},{24,20},{0,16},{16,0},{12,28},{28,12},{5,9},{9... | collective-permute-start | bytes 1179656 | tf_op jit(solution)/shard_map/ppermute | solution.py:420
  125.0 11.0 %collective-permute-start.35 = (bf16[384,512]{1,0:T(8,128)(2,1)S(1)}, bf16[384,512]{1,0:T(8,128)(2,1)S(1)}, u32[]{:S(2)}, u32[]{:S(2)}) collective-permute-start(bf16[384,512]{1,0:T(8,128)(2,1)S(1)} %square.23.refs_2_), channel_id=1, source_target_pairs={{0,4},{4,0},{8,12},{12,8},{1,5},{5,1},{9,13},{13,9},{2,6},{6,2},{1... | collective-permute-start | bytes 1179656 | tf_op jit(solution)/shard_map/ppermute | solution.py:414
  127.6 22.3 %collective-permute-start.33 = (bf16[384,1024]{1,0:T(8,128)(2,1)S(1)}, bf16[384,1024]{1,0:T(8,128)(2,1)S(1)}, u32[]{:S(2)}, u32[]{:S(2)}) collective-permute-start(bf16[384,1024]{1,0:T(8,128)(2,1)S(1)} %get-tuple-element.95.refs_0_), channel_id=1, source_target_pairs={{0,1},{1,0},{2,3},{3,2},{4,5},{5,4},{6,7},{7,6},{8,9},{9,8},{10,11... | collective-permute-start | bytes 2359304 | tf_op jit(solution)/shard_map/ppermute | solution.py:481
  127.7 22.3 %collective-permute-start.34 = (bf16[384,1024]{1,0:T(8,128)(2,1)S(1)}, bf16[384,1024]{1,0:T(8,128)(2,1)S(1)}, u32[]{:S(2)}, u32[]{:S(2)}) collective-permute-start(bf16[384,1024]{1,0:T(8,128)(2,1)S(1)} %get-tuple-element.96.refs_2_.refs_1_), channel_id=1, source_target_pairs={{0,1},{1,0},{2,3},{3,2},{4,5},{5,4},{6,7},{7,6},{8,9},{9,8},{10,11... | collective-permute-start | bytes 2359304 | tf_op jit(solution)/shard_map/ppermute | solution.py:481
  128.8 12.3 %collective-permute-start.40 = (bf16[384,512]{1,0:T(8,128)(2,1)S(1)}, bf16[384,512]{1,0:T(8,128)(2,1)S(1)}, u32[]{:S(2)}, u32[]{:S(2)}) collective-permute-start(bf16[384,512]{1,0:T(8,128)(2,1)S(1)} %add.36.refs_0_), channel_id=1, source_target_pairs={{4,8},{8,4},{20,24},{24,20},{0,16},{16,0},{12,28},{28,12},{5,9},{9... | collective-permute-start | bytes 1179656 | tf_op jit(solution)/shard_map/ppermute | solution.py:420
  134.4 12.1 %collective-permute-start.39 = (bf16[384,512]{1,0:T(8,128)(2,1)S(1)}, bf16[384,512]{1,0:T(8,128)(2,1)S(1)}, u32[]{:S(2)}, u32[]{:S(2)}) collective-permute-start(bf16[384,512]{1,0:T(8,128)(2,1)S(1)} %square.25.refs_2_.refs_6_), channel_id=1, source_target_pairs={{0,4},{4,0},{8,12},{12,8},{1,5},{5,1},{9,13},{13,9},{2,6},{6,2},{1... | collective-permute-start | bytes 1179656 | tf_op jit(solution)/shard_map/ppermute | solution.py:414
  136.6 12.7 %collective-permute-start.38 = (bf16[384,512]{1,0:T(8,128)(2,1)S(1)}, bf16[384,512]{1,0:T(8,128)(2,1)S(1)}, u32[]{:S(2)}, u32[]{:S(2)}) collective-permute-start(bf16[384,512]{1,0:T(8,128)(2,1)S(1)} %add.37.refs_0_), channel_id=1, source_target_pairs={{4,8},{8,4},{20,24},{24,20},{0,16},{16,0},{12,28},{28,12},{5,9},{9... | collective-permute-start | bytes 1179656 | tf_op jit(solution)/shard_map/ppermute | solution.py:420
  141.1 10.3 %copy-start.1 = (bf16[384,512]{1,0:T(8,128)(2,1)S(1)}, bf16[384,512]{1,0:T(8,128)(2,1)}, u32[]{:S(2)}) copy-start(bf16[384,512]{1,0:T(8,128)(2,1)} %copy-done) | copy-start | bytes 1179652
  141.1 10.3 %copy-start.4 = (bf16[384,512]{1,0:T(8,128)(2,1)S(1)}, bf16[384,512]{1,0:T(8,128)(2,1)}, u32[]{:S(2)}) copy-start(bf16[384,512]{1,0:T(8,128)(2,1)} %copy-done.3) | copy-start | bytes 1179652
  141.7 13.7 %collective-permute-start.41 = (bf16[384,512]{1,0:T(8,128)(2,1)S(1)}, bf16[384,512]{1,0:T(8,128)(2,1)S(1)}, u32[]{:S(2)}, u32[]{:S(2)}) collective-permute-start(bf16[384,512]{1,0:T(8,128)(2,1)S(1)} %square.26.refs_2_), channel_id=1, source_target_pairs={{0,4},{4,0},{8,12},{12,8},{1,5},{5,1},{9,13},{13,9},{2,6},{6,2},{1... | collective-permute-start | bytes 1179656 | tf_op jit(solution)/shard_map/ppermute | solution.py:414
  147.1 11.7 %collective-permute-start.43 = (bf16[384,512]{1,0:T(8,128)(2,1)S(1)}, bf16[384,512]{1,0:T(8,128)(2,1)S(1)}, u32[]{:S(2)}, u32[]{:S(2)}) collective-permute-start(bf16[384,512]{1,0:T(8,128)(2,1)S(1)} %add.38.refs_2_.refs_0_), channel_id=1, source_target_pairs={{4,8},{8,4},{20,24},{24,20},{0,16},{16,0},{12,28},{28,12},{5,9},{9... | collective-permute-start | bytes 1179656 | tf_op jit(solution)/shard_map/ppermute | solution.py:420
  156.1 11.0 %collective-permute-start.42 = (bf16[384,512]{1,0:T(8,128)(2,1)S(1)}, bf16[384,512]{1,0:T(8,128)(2,1)S(1)}, u32[]{:S(2)}, u32[]{:S(2)}) collective-permute-start(bf16[384,512]{1,0:T(8,128)(2,1)S(1)} %add.39.refs_2_.refs_0_), channel_id=1, source_target_pairs={{4,8},{8,4},{20,24},{24,20},{0,16},{16,0},{12,28},{28,12},{5,9},{9... | collective-permute-start | bytes 1179656 | tf_op jit(solution)/shard_map/ppermute | solution.py:420
  157.4 12.1 %collective-permute-start.46 = (bf16[384,512]{1,0:T(8,128)(2,1)S(1)}, bf16[384,512]{1,0:T(8,128)(2,1)S(1)}, u32[]{:S(2)}, u32[]{:S(2)}) collective-permute-start(bf16[384,512]{1,0:T(8,128)(2,1)S(1)} %square.27.refs_4_.refs_6_), channel_id=1, source_target_pairs={{0,4},{4,0},{8,12},{12,8},{1,5},{5,1},{9,13},{13,9},{2,6},{6,2},{1... | collective-permute-start | bytes 1179656 | tf_op jit(solution)/shard_map/ppermute | solution.py:414
  159.5 18.4 %collective-permute-start.45 = (bf16[384,512]{1,0:T(8,128)(2,1)S(1)}, bf16[384,512]{1,0:T(8,128)(2,1)S(1)}, u32[]{:S(2)}, u32[]{:S(2)}) collective-permute-start(bf16[384,512]{1,0:T(8,128)(2,1)S(1)} %square.28.refs_9_.refs_2_), channel_id=1, source_target_pairs={{0,4},{4,0},{8,12},{12,8},{1,5},{5,1},{9,13},{13,9},{2,6},{6,2},{1... | collective-permute-start | bytes 1179656 | tf_op jit(solution)/shard_map/ppermute | solution.py:414
  167.7 15.6 %collective-permute-start.44 = (bf16[384,512]{1,0:T(8,128)(2,1)S(1)}, bf16[384,512]{1,0:T(8,128)(2,1)S(1)}, u32[]{:S(2)}, u32[]{:S(2)}) collective-permute-start(bf16[384,512]{1,0:T(8,128)(2,1)S(1)} %square.29.refs_9_.refs_2_), channel_id=1, source_target_pairs={{0,4},{4,0},{8,12},{12,8},{1,5},{5,1},{9,13},{13,9},{2,6},{6,2},{1... | collective-permute-start | bytes 1179656 | tf_op jit(solution)/shard_map/ppermute | solution.py:414

commit v3 on v2

--- a/solution.py
+++ b/solution.py
@@ -314,7 +314,7 @@
     flat = [a for piece in pieces for a in piece]
     width = chunk * len(pieces)
     extra = list(after) if result is None else [result, *after]
-    rows = height // (4 * len(pieces))
+    rows = height // (2 * len(pieces))
 
     def body(flags_ref, act_ref, *refs):
         ins = refs[:len(flat)]
@@ -442,21 +442,21 @@
     columns = act_basis.shape[1]
     block = fetch(grad_basis, chunk, last)
     last = (block,)
+    rows = join([pltpu.with_memory_space_constraint(grads, pltpu.HBM)], [near], last)
+    last = (rows,)
+    project_next(rows)
+    send(0)
     act_terms = list(project_acts(flags, acts, act_basis, 0, columns, [], last))
     keep, give = act_terms[:len(act_terms) // 2], act_terms[len(act_terms) // 2:]
     last = (keep[-1],)
     taken = [lax.ppermute(piece, "gc", CORES) for piece in give]
-    rows = join([pltpu.with_memory_space_constraint(grads, pltpu.HBM)], [near], last)
-    last = (rows,)
-    project_next(rows)
-    send(0)
     project_next(rows)
     send(1)
-    (act,) = small(add_pieces_body, [(keep[0].shape[0], columns)], [*keep, *taken], "add")
-    act_far = lax.ppermute(act, "gc", CHIPS)
     project_next(rows)
     send(2)
     add(0)
+    (act,) = small(add_pieces_body, [(keep[0].shape[0], columns)], [*keep, *taken], "add")
+    act_far = lax.ppermute(act, "gc", CHIPS)
     project_next(rows)
     for k in (1, 2, 3):
         add(k)

time: 188 us -> 186 us (0.989)
  Pallas kernels: 115 us -> 113 us
    ppermute x14, starting transfers between devices: 22.2 us -> 18.7 us  [add(): others.append(lax.ppermute(sums[-1], ('layers', 'gr'), INNER))]
  transfers between devices with their start and end apart: 47 -> 47, of which waited for: 12 -> 10; matrix products, arithmetic and copies ran while one was open for 0% -> 0% of each run, Pallas kernels for 58% -> 58%
where the time goes in v3:
time: 186 us; the launch traced here: 185 us
  Pallas kernels  113 us (61%)
  starting transfers between devices  53.2 us (29%)
  waiting for transfers between devices  18.5 us (10%)
    pallas_call x14, Pallas kernels, project(): pl.pallas_call(body, in_specs=[VMEM, ANYWHERE, VMEM] + [ANYWHERE] * len(a...  48.4 us
    ppermute x17, starting transfers between devices, send(): received.append(lax.ppermute(payload, 'gr', OUTER))  26.7 us
    pallas_call x5, Pallas kernels, correct(): pl.pallas_call(body, in_specs=[pl.BlockSpec(memory_space=pltpu.SMEM)] + [...  24.8 us
    pallas_call x31, Pallas kernels, whole(): pl.pallas_call(run, in_specs=[pl.BlockSpec(memory_space=pltpu.SMEM)] + [V...  20.9 us
    ppermute x14, starting transfers between devices, add(): others.append(lax.ppermute(sums[-1], ('layers', 'gr'), INNER))  18.7 us
    ppermute x17, waiting for transfers between devices, send(): received.append(lax.ppermute(payload, 'gr', OUTER))  14.3 us
    pallas_call x1, Pallas kernels, project_acts(): pl.pallas_call(body, grid_spec=pltpu.PrefetchScalarGridSpec(num_scalar_pr...  9.88 us
    ppermute x14, waiting for transfers between devices, add(): others.append(lax.ppermute(sums[-1], ('layers', 'gr'), INNER))  3.79 us
  transfers between devices with their start and end apart: 47, of which 10 were waited for; matrix products, arithmetic and copies ran while one was open for 0% of the time, Pallas kernels for 58%

profile of v3, /device:TPU:0, one launch (start us, length us, event | category | flops | bytes accessed | tf_op | source)
XLA Modules:
  0.0 185.4 jit_solution(14599361249520010305)
XLA Ops:
  0.5 2.5 %collective-permute-start.7 = (bf16[192,7168]{1,0:T(8,128)(2,1)}, bf16[192,7168]{1,0:T(8,128)(2,1)}, u32[]{:S(2)}, u32[]{:S(2)}) collective-permute-start(bf16[192,7168]{1,0:T(8,128)(2,1)} %refs_0_.1), channel_id=1, source_target_pairs={{0,2},{2,0},{1,3},{3,1},{4,6},{6,4},{5,7},{7,5},{8,10},{10,8},{9,1... | collective-permute-start | bytes 8257544 | tf_op jit(solution)/shard_map/ppermute | solution.py:441
  3.0 3.2 %fetch.1.refs_2_.block_ref = bf16[7168,512]{1,0:T(8,128)(2,1)S(1)} custom-call(bf16[7168,3584]{1,0:T(8,128)(2,1)} %basis_ref.31, s32[3]{0:T(128)S(1)} %pad_add_fusion.refs_0_.flags_ref), custom_call_target="tpu_custom_call" | custom-call | flops 10000000 | bytes 100000 | tf_op jit(solution)/shard_map/fetch/pallas_call | solution.py:212
  6.3 1.8 join.2.rows_ref.refs_0_
  8.1 3.5 %project_grads.14 = (bf16[384,512]{1,0:T(8,128)(2,1)S(1)}, bf16[7168,512]{1,0:T(8,128)(2,1)S(1)}) custom-call(bf16[384,7168]{1,0:T(8,128)(2,1)S(1)} %join.2.rows_ref.refs_0_, bf16[7168,3584]{1,0:T(8,128)(2,1)} %basis_ref.31, bf16[7168,512]{1,0:T(8,128)(2,1)S(1)} %fetch.1.refs_2_.block_ref, bf16[384,7168]{1,0:T(8,128)(2,1)S(1)} %join.2.rows_ref.refs_0_), custom_call_target="tpu_custom_call" | custom-call | flops 10000000 | bytes 100000 | tf_op jit(solution)/shard_map/project_grads/pallas_call | solution.py:245
  11.5 2.1 %collective-permute-start.5 = (bf16[384,512]{1,0:T(8,128)(2,1)S(1)}, bf16[384,512]{1,0:T(8,128)(2,1)S(1)}, u32[]{:S(2)}, u32[]{:S(2)}) collective-permute-start(bf16[384,512]{1,0:T(8,128)(2,1)S(1)} %get-tuple-element.57.refs_0_), channel_id=1, source_target_pairs={{0,4},{4,0},{8,12},{12,8},{1,5},{5,1},{9,13},{13,9},{2,6},{6,2},{1... | collective-permute-start | bytes 1179656 | tf_op jit(solution)/shard_map/ppermute | solution.py:414
  13.7 9.9 %project_acts.1 = (bf16[384,512]{1,0:T(8,128)(2,1)S(1)}, bf16[384,512]{1,0:T(8,128)(2,1)S(1)}, bf16[384,512]{1,0:T(8,128)(2,1)S(1)}, bf16[384,512]{1,0:T(8,128)(...) custom-call(s32[3]{0:T(128)S(1)} %pad_add_fusion.refs_0_.flags_ref, ...), custom_call_target="tpu_custom_call" | custom-call | flops 10000000 | bytes 100000 | tf_op jit(solution)/shard_map/project_acts/pallas_call | solution.py:285
  24.7 3.5 %project_grads.15 = (bf16[384,512]{1,0:T(8,128)(2,1)S(1)}, bf16[7168,512]{1,0:T(8,128)(2,1)S(1)}) custom-call(bf16[384,7168]{1,0:T(8,128)(2,1)S(1)} %join.2.rows_ref.refs_0_, bf16[7168,3584]{1,0:T(8,128)(2,1)} %basis_ref.31, bf16[7168,512]{1,0:T(8,128)(2,1)S(1)} %get-tuple-element.66.block_ref, bf16[384,512]{1,0:T(8,128)(2,1)S(1)} %get-tuple-element.61.refs_0_.refs_3_), custom_call_target="tpu_custom_call" | custom-call | flops 10000000 | bytes 100000 | tf_op jit(solution)/shard_map/project_grads/pallas_call | solution.py:245
  28.8 3.5 %project_grads.16 = (bf16[384,512]{1,0:T(8,128)(2,1)S(1)}, bf16[7168,512]{1,0:T(8,128)(2,1)S(1)}) custom-call(bf16[384,7168]{1,0:T(8,128)(2,1)S(1)} %join.2.rows_ref.refs_0_, bf16[7168,3584]{1,0:T(8,128)(2,1)} %basis_ref.31, bf16[7168,512]{1,0:T(8,128)(2,1)S(1)} %get-tuple-element.67.block_ref, bf16[384,512]{1,0:T(8,128)(2,1)S(1)} %get-tuple-element.68.refs_0_), custom_call_target="tpu_custom_call" | custom-call | flops 10000000 | bytes 100000 | tf_op jit(solution)/shard_map/project_grads/pallas_call | solution.py:245
  32.9 1.6 collective-permute-start.9
  34.5 1.6 collective-permute-start.8
  36.1 0.9 add.26.refs_0_
  37.1 3.5 %project_grads.17 = (bf16[384,512]{1,0:T(8,128)(2,1)S(1)}, bf16[7168,512]{1,0:T(8,128)(2,1)S(1)}) custom-call(bf16[384,7168]{1,0:T(8,128)(2,1)S(1)} %join.2.rows_ref.refs_0_, bf16[7168,3584]{1,0:T(8,128)(2,1)} %basis_ref.31, bf16[7168,512]{1,0:T(8,128)(2,1)S(1)} %get-tuple-element.70.block_ref, bf16[384,2048]{1,0:T(8,128)(2,1)S(1)} %add.26.refs_0_), custom_call_target="tpu_custom_call" | custom-call | flops 10000000 | bytes 100000 | tf_op jit(solution)/shard_map/project_grads/pallas_call | solution.py:245
  41.2 1.6 collective-permute-start.13
  42.8 3.5 %project_grads.18 = (bf16[384,512]{1,0:T(8,128)(2,1)S(1)}, bf16[7168,512]{1,0:T(8,128)(2,1)S(1)}) custom-call(bf16[384,7168]{1,0:T(8,128)(2,1)S(1)} %join.2.rows_ref.refs_0_, bf16[7168,3584]{1,0:T(8,128)(2,1)} %basis_ref.31, bf16[7168,512]{1,0:T(8,128)(2,1)S(1)} %get-tuple-element.72.block_ref, bf16[384,512]{1,0:T(8,128)(2,1)S(1)} %add.27.refs_0_), custom_call_target="tpu_custom_call" | custom-call | flops 10000000 | bytes 100000 | tf_op jit(solution)/shard_map/project_grads/pallas_call | solution.py:245
  46.8 1.6 collective-permute-start.12
  49.1 1.4 collective-permute-start.11
  50.5 3.5 %project_grads.19 = (bf16[384,512]{1,0:T(8,128)(2,1)S(1)}, bf16[7168,512]{1,0:T(8,128)(2,1)S(1)}) custom-call(bf16[384,7168]{1,0:T(8,128)(2,1)S(1)} %join.2.rows_ref.refs_0_, bf16[7168,3584]{1,0:T(8,128)(2,1)} %basis_ref.31, bf16[7168,512]{1,0:T(8,128)(2,1)S(1)} %get-tuple-element.74.block_ref, bf16[384,512]{1,0:T(8,128)(2,1)S(1)} %add.28.refs_0_), custom_call_target="tpu_custom_call" | custom-call | flops 10000000 | bytes 100000 | tf_op jit(solution)/shard_map/project_grads/pallas_call | solution.py:245
  54.6 1.8 collective-permute-start.22
  56.4 1.6 collective-permute-done.12.refs_1_
  58.9 3.5 %project_grads.20 = (bf16[384,512]{1,0:T(8,128)(2,1)S(1)}, bf16[7168,512]{1,0:T(8,128)(2,1)S(1)}) custom-call(bf16[384,7168]{1,0:T(8,128)(2,1)S(1)} %join.2.rows_ref.refs_0_, bf16[7168,3584]{1,0:T(8,128)(2,1)} %basis_ref.31, bf16[7168,512]{1,0:T(8,128)(2,1)S(1)} %get-tuple-element.76.block_ref, bf16[384,512]{1,0:T(8,128)(2,1)S(1)} %add.29.refs_0_), custom_call_target="tpu_custom_call" | custom-call | flops 10000000 | bytes 100000 | tf_op jit(solution)/shard_map/project_grads/pallas_call | solution.py:245
  63.6 1.8 split.1
  66.5 2.6 %collective-permute-done.21.refs_1_ = bf16[384,512]{1,0:T(8,128)(2,1)S(1)} collective-permute-done((bf16[384,512]{1,0:T(8,128)(2,1)S(1)}, bf16[384,512]{1,0:T(8,128)(2,1)S(1)}, u32[]{:S(2)}, u32[]{:S(2)}) %collective-permute-start.21) | collective-permute-done | bytes 393248 | tf_op jit(solution)/shard_map/ppermute | solution.py:420
  69.7 1.4 collective-permute-start.25
  71.1 1.5 collective-permute-start.6
  73.3 1.6 collective-permute-start.24
  75.5 1.8 collective-permute-start.23
  77.2 1.9 %join.3.rows_ref.refs_0_ = bf16[384,7168]{1,0:T(8,128)(2,1)S(1)} custom-call(bf16[192,7168]{1,0:T(8,128)(2,1)} %collective-permute-done.7.array_ref.refs_0_, bf16[192,1024]{1,0:T(8,128)(2,1)S(1)} %collective-permute-done.14.refs_1_, bf16[192,1024]{1,0:T(8,128)(2,1)S(1)} %collective-permute-done.15.refs_2_, ...), custom_call_target="tpu_custom_call" | custom-call | flops 10000000 | bytes 100000 | tf_op jit(solution)/shard_map/join/pallas_call | solution.py:167
  79.1 3.5 %project_grads.21 = (bf16[384,512]{1,0:T(8,128)(2,1)S(1)}, bf16[7168,512]{1,0:T(8,128)(2,1)S(1)}) custom-call(bf16[384,7168]{1,0:T(8,128)(2,1)S(1)} %join.3.rows_ref.refs_0_, bf16[7168,3584]{1,0:T(8,128)(2,1)} %basis_ref.31, bf16[7168,512]{1,0:T(8,128)(2,1)S(1)} %get-tuple-element.85.block_ref, bf16[384,7168]{1,0:T(8,128)(2,1)S(1)} %join.3.rows_ref.refs_0_), custom_call_target="tpu_custom_call" | custom-call | flops 10000000 | bytes 100000 | tf_op jit(solution)/shard_map/project_grads/pallas_call | solution.py:245
  83.2 1.6 collective-permute-start.26
  85.4 1.0 collective-permute-start.29
  86.4 3.6 %collective-permute-done.23.refs_1_ = bf16[384,512]{1,0:T(8,128)(2,1)S(1)} collective-permute-done((bf16[384,512]{1,0:T(8,128)(2,1)S(1)}, bf16[384,512]{1,0:T(8,128)(2,1)S(1)}, u32[]{:S(2)}, u32[]{:S(2)}) %collective-permute-start.23) | collective-permute-done | bytes 393248 | tf_op jit(solution)/shard_map/ppermute | solution.py:414
  90.7 1.6 collective-permute-start.28
  92.3 3.5 %project_grads.22 = (bf16[384,512]{1,0:T(8,128)(2,1)S(1)}, bf16[7168,512]{1,0:T(8,128)(2,1)S(1)}) custom-call(bf16[384,7168]{1,0:T(8,128)(2,1)S(1)} %join.3.rows_ref.refs_0_, bf16[7168,3584]{1,0:T(8,128)(2,1)} %basis_ref.31, bf16[7168,512]{1,0:T(8,128)(2,1)S(1)} %get-tuple-element.86.block_ref, bf16[384,512]{1,0:T(8,128)(2,1)S(1)} %add.32.refs_0_), custom_call_target="tpu_custom_call" | custom-call | flops 10000000 | bytes 100000 | tf_op jit(solution)/shard_map/project_grads/pallas_call | solution.py:245
  96.4 1.8 collective-permute-start.27
  98.8 1.6 collective-permute-start.32
  100.4 3.5 %project_grads.23 = (bf16[384,512]{1,0:T(8,128)(2,1)S(1)}, bf16[7168,512]{1,0:T(8,128)(2,1)S(1)}) custom-call(bf16[384,7168]{1,0:T(8,128)(2,1)S(1)} %join.3.rows_ref.refs_0_, bf16[7168,3584]{1,0:T(8,128)(2,1)} %basis_ref.31, bf16[7168,512]{1,0:T(8,128)(2,1)S(1)} %get-tuple-element.89.block_ref, bf16[384,512]{1,0:T(8,128)(2,1)S(1)} %add.33.refs_0_), custom_call_target="tpu_custom_call" | custom-call | flops 10000000 | bytes 100000 | tf_op jit(solution)/shard_map/project_grads/pallas_call | solution.py:245
  104.5 2.0 %collective-permute-start.31 = (bf16[384,512]{1,0:T(8,128)(2,1)S(1)}, bf16[384,512]{1,0:T(8,128)(2,1)S(1)}, u32[]{:S(2)}, u32[]{:S(2)}) collective-permute-start(bf16[384,512]{1,0:T(8,128)(2,1)S(1)} %square.21.refs_2_.refs_0_), channel_id=1, source_target_pairs={{0,4},{4,0},{8,12},{12,8},{1,5},{5,1},{9,13},{13,9},{2,6},{6,2},{1... | collective-permute-start | bytes 1179656 | tf_op jit(solution)/shard_map/ppermute | solution.py:414
  107.1 1.7 collective-permute-start.30
  108.8 3.5 %project_grads.24 = (bf16[384,512]{1,0:T(8,128)(2,1)S(1)}, bf16[7168,512]{1,0:T(8,128)(2,1)S(1)}) custom-call(bf16[384,7168]{1,0:T(8,128)(2,1)S(1)} %join.3.rows_ref.refs_0_, bf16[7168,3584]{1,0:T(8,128)(2,1)} %basis_ref.31, bf16[7168,512]{1,0:T(8,128)(2,1)S(1)} %get-tuple-element.91.block_ref, bf16[384,512]{1,0:T(8,128)(2,1)S(1)} %add.34.refs_0_), custom_call_target="tpu_custom_call" | custom-call | flops 10000000 | bytes 100000 | tf_op jit(solution)/shard_map/project_grads/pallas_call | solution.py:245
  112.9 2.0 %collective-permute-start.37 = (bf16[384,512]{1,0:T(8,128)(2,1)S(1)}, bf16[384,512]{1,0:T(8,128)(2,1)S(1)}, u32[]{:S(2)}, u32[]{:S(2)}) collective-permute-start(bf16[384,512]{1,0:T(8,128)(2,1)S(1)} %square.22.refs_2_), channel_id=1, source_target_pairs={{0,4},{4,0},{8,12},{12,8},{1,5},{5,1},{9,13},{13,9},{2,6},{6,2},{1... | collective-permute-start | bytes 1179656 | tf_op jit(solution)/shard_map/ppermute | solution.py:414
  114.9 0.9 collective-permute-done.31.refs_1_
  116.4 1.2 collective-permute-start.36
  117.7 3.5 %project_grads.25 = (bf16[384,512]{1,0:T(8,128)(2,1)S(1)}, bf16[7168,512]{1,0:T(8,128)(2,1)S(1)}) custom-call(bf16[384,7168]{1,0:T(8,128)(2,1)S(1)} %join.3.rows_ref.refs_0_, bf16[7168,3584]{1,0:T(8,128)(2,1)} %basis_ref.31, bf16[7168,512]{1,0:T(8,128)(2,1)S(1)} %get-tuple-element.92.block_ref, bf16[384,512]{1,0:T(8,128)(2,1)S(1)} %add.35.refs_0_), custom_call_target="tpu_custom_call" | custom-call | flops 10000000 | bytes 100000 | tf_op jit(solution)/shard_map/project_grads/pallas_call | solution.py:245
  121.7 2.2 %collective-permute-start.35 = (bf16[384,512]{1,0:T(8,128)(2,1)S(1)}, bf16[384,512]{1,0:T(8,128)(2,1)S(1)}, u32[]{:S(2)}, u32[]{:S(2)}) collective-permute-start(bf16[384,512]{1,0:T(8,128)(2,1)S(1)} %square.23.refs_2_), channel_id=1, source_target_pairs={{0,4},{4,0},{8,12},{12,8},{1,5},{5,1},{9,13},{13,9},{2,6},{6,2},{1... | collective-permute-start | bytes 1179656 | tf_op jit(solution)/shard_map/ppermute | solution.py:414
  123.9 1.0 square.24
  126.1 1.6 collective-permute-start.40
  127.7 3.5 %project_grads.26 = (bf16[384,512]{1,0:T(8,128)(2,1)S(1)}, bf16[7168,512]{1,0:T(8,128)(2,1)S(1)}) custom-call(bf16[384,7168]{1,0:T(8,128)(2,1)S(1)} %join.3.rows_ref.refs_0_, bf16[7168,3584]{1,0:T(8,128)(2,1)} %basis_ref.31, bf16[7168,512]{1,0:T(8,128)(2,1)S(1)} %get-tuple-element.97.block_ref, bf16[384,512]{1,0:T(8,128)(2,1)S(1)} %add.36.refs_0_), custom_call_target="tpu_custom_call" | custom-call | flops 10000000 | bytes 100000 | tf_op jit(solution)/shard_map/project_grads/pallas_call | solution.py:245
  131.2 0.8 square.25.refs_2_.refs_6_
  132.0 1.6 collective-permute-start.39
  134.9 3.4 %project_grads.27.refs_2_.refs_3_.refs_0_ = bf16[384,512]{1,0:T(8,128)(2,1)S(1)} custom-call(bf16[384,7168]{1,0:T(8,128)(2,1)S(1)} %join.3.rows_ref.refs_0_, bf16[7168,3584]{1,0:T(8,128)(2,1)} %basis_ref.31, bf16[7168,512]{1,0:T(8,128)(2,1)S(1)} %get-tuple-element.99.block_ref, bf16[384,512]{1,0:T(8,128)(2,1)S(1)} %add.37.refs_0_), custom_call_target="tpu_custom_call" | custom-call | flops 10000000 | bytes 100000 | tf_op jit(solution)/shard_map/project_grads/pallas_call | solution.py:245
  138.9 1.5 collective-permute-start.41
  140.4 3.6 %collective-permute-done.39.refs_1_.refs_7_ = bf16[384,512]{1,0:T(8,128)(2,1)S(1)} collective-permute-done((bf16[384,512]{1,0:T(8,128)(2,1)S(1)}, bf16[384,512]{1,0:T(8,128)(2,1)S(1)}, u32[]{:S(2)}, u32[]{:S(2)}) %collective-permute-start.39) | collective-permute-done | bytes 393248 | tf_op jit(solution)/shard_map/ppermute | solution.py:414
  145.2 1.1 collective-permute-done.38.refs_1_
  147.0 1.4 stack.22.act_ref.refs_4_
  148.4 3.9 %correct.5 = (bf16[2048,3584]{1,0:T(8,128)(2,1)}, bf16[16,128]{1,0:T(8,128)(2,1)S(1)}) custom-call(s32[3]{0:T(128)S(1)} %pad_add_fusion.refs_0_.flags_ref, bf16[2048,768]{1,0:T(8,128)(2,1)S(1)} %stack.22.act_ref.refs_4_, bf16[384,512]{1,0:T(8,128)(2,1)S(1)} %copy-done.1, bf16[384,512]{1,0:T(8,128)(2,1)S(1)} %copy-done.4, ...), custom_call_target="tpu_custom_call" | custom-call | flops 10000000 | bytes 100000 | tf_op jit(solution)/shard_map/correct/pallas_call | solution.py:351
  152.9 1.9 %collective-permute-start.42 = (bf16[384,512]{1,0:T(8,128)(2,1)S(1)}, bf16[384,512]{1,0:T(8,128)(2,1)S(1)}, u32[]{:S(2)}, u32[]{:S(2)}) collective-permute-start(bf16[384,512]{1,0:T(8,128)(2,1)S(1)} %add.39.refs_2_.refs_0_), channel_id=1, source_target_pairs={{4,8},{8,4},{20,24},{24,20},{0,16},{16,0},{12,28},{28,12},{5,9},{9... | collective-permute-start | bytes 1179656 | tf_op jit(solution)/shard_map/ppermute | solution.py:420
  154.8 1.5 collective-permute-start.46
  157.6 6.3 %correct.6 = (bf16[2048,3584]{1,0:T(8,128)(2,1)}, bf16[16,128]{1,0:T(8,128)(2,1)S(1)}) custom-call(s32[3]{0:T(128)S(1)} %pad_add_fusion.refs_0_.flags_ref, bf16[2048,768]{1,0:T(8,128)(2,1)S(1)} %stack.22.act_ref.refs_4_, bf16[384,512]{1,0:T(8,128)(2,1)S(1)} %square.16.refs_2_.refs_0_, ...), custom_call_target="tpu_custom_call", output_to_operand_aliasing={{0}: (10, {})} | custom-call | flops 10000000 | bytes 100000 | tf_op jit(solution)/shard_map/correct/pallas_call | solution.py:351
  164.5 1.5 collective-permute-start.44
  166.9 6.3 %correct.7 = (bf16[2048,3584]{1,0:T(8,128)(2,1)}, bf16[16,128]{1,0:T(8,128)(2,1)S(1)}) custom-call(s32[3]{0:T(128)S(1)} %pad_add_fusion.refs_0_.flags_ref, bf16[2048,768]{1,0:T(8,128)(2,1)S(1)} %stack.22.act_ref.refs_4_, bf16[384,512]{1,0:T(8,128)(2,1)S(1)} %square.18.refs_8_.refs_0_, ...), custom_call_target="tpu_custom_call", output_to_operand_aliasing={{0}: (10, {})} | custom-call | flops 10000000 | bytes 100000 | tf_op jit(solution)/shard_map/correct/pallas_call | solution.py:351
  173.2 2.1 %collective-permute-done.45.refs_3_ = bf16[384,512]{1,0:T(8,128)(2,1)S(1)} collective-permute-done((bf16[384,512]{1,0:T(8,128)(2,1)S(1)}, bf16[384,512]{1,0:T(8,128)(2,1)S(1)}, u32[]{:S(2)}, u32[]{:S(2)}) %collective-permute-start.45) | collective-permute-done | bytes 393248 | tf_op jit(solution)/shard_map/ppermute | solution.py:414
  175.3 3.9 %correct.8 = (bf16[2048,3584]{1,0:T(8,128)(2,1)}, bf16[16,128]{1,0:T(8,128)(2,1)S(1)}) custom-call(s32[3]{0:T(128)S(1)} %pad_add_fusion.refs_0_.flags_ref, bf16[2048,768]{1,0:T(8,128)(2,1)S(1)} %stack.22.act_ref.refs_4_, bf16[384,512]{1,0:T(8,128)(2,1)S(1)} %square.20.refs_2_.refs_0_, ...), custom_call_target="tpu_custom_call", output_to_operand_aliasing={{0}: (6, {})} | custom-call | flops 10000000 | bytes 100000 | tf_op jit(solution)/shard_map/correct/pallas_call | solution.py:351
  179.2 1.6 collective-permute-done.44.refs_3_
  180.8 4.5 %correct.9 = (bf16[2048,3584]{1,0:T(8,128)(2,1)}, bf16[16,128]{1,0:T(8,128)(2,1)}) custom-call(s32[3]{0:T(128)S(1)} %pad_add_fusion.refs_0_.flags_ref, bf16[2048,768]{1,0:T(8,128)(2,1)S(1)} %stack.22.act_ref.refs_4_, bf16[384,512]{1,0:T(8,128)(2,1)S(1)} %square.21.refs_2_.refs_0_, ...), custom_call_target="tpu_custom_call", output_to_operand_aliasing={{0}: (6, {})} | custom-call | flops 10000000 | bytes 100000 | tf_op jit(solution)/shard_map/correct/pallas_call | solution.py:351
  (96 shorter events, 24.7 us)
Async XLA Ops:
  0.0 6.2 %collective-permute-start = (bf16[192,7168]{1,0:T(8,128)(2,1)}, bf16[192,7168]{1,0:T(8,128)(2,1)S(1)}, u32[]{:S(2)}, u32[]{:S(2)}) collective-permute-start(bf16[192,7168]{1,0:T(8,128)(2,1)} %refs_0_.1), channel_id=1, source_target_pairs={{0,1},{1,0},{2,3},{3,2},{4,5},{5,4},{6,7},{7,6},{8,9},{9,8},{10,11... | collective-permute-start | bytes 8257544 | tf_op jit(solution)/shard_map/ppermute | solution.py:385
  0.5 63.1 %collective-permute-start.7 = (bf16[192,7168]{1,0:T(8,128)(2,1)}, bf16[192,7168]{1,0:T(8,128)(2,1)}, u32[]{:S(2)}, u32[]{:S(2)}) collective-permute-start(bf16[192,7168]{1,0:T(8,128)(2,1)} %refs_0_.1), channel_id=1, source_target_pairs={{0,2},{2,0},{1,3},{3,1},{4,6},{6,4},{5,7},{7,5},{8,10},{10,8},{9,1... | collective-permute-start | bytes 8257544 | tf_op jit(solution)/shard_map/ppermute | solution.py:441
  8.1 5.6 %copy-start.2 = (bf16[768,2048]{1,0:T(8,128)(2,1)S(1)}, bf16[768,2048]{1,0:T(8,128)(2,1)}, u32[]{:S(2)}) copy-start(bf16[768,2048]{1,0:T(8,128)(2,1)} %acts_ref.1) | copy-start | bytes 9437188
  11.5 12.7 %collective-permute-start.5 = (bf16[384,512]{1,0:T(8,128)(2,1)S(1)}, bf16[384,512]{1,0:T(8,128)(2,1)S(1)}, u32[]{:S(2)}, u32[]{:S(2)}) collective-permute-start(bf16[384,512]{1,0:T(8,128)(2,1)S(1)} %get-tuple-element.57.refs_0_), channel_id=1, source_target_pairs={{0,4},{4,0},{8,12},{12,8},{1,5},{5,1},{9,13},{13,9},{2,6},{6,2},{1... | collective-permute-start | bytes 1179656 | tf_op jit(solution)/shard_map/ppermute | solution.py:414
  23.6 4.6 %collective-permute-start.1 = (bf16[384,512]{1,0:T(8,128)(2,1)S(1)}, bf16[384,512]{1,0:T(8,128)(2,1)S(1)}, u32[]{:S(2)}, u32[]{:S(2)}) collective-permute-start(bf16[384,512]{1,0:T(8,128)(2,1)S(1)} %get-tuple-element.62), channel_id=1, source_target_pairs={{0,1},{1,0},{2,3},{3,2},{4,5},{5,4},{6,7},{7,6},{8,9},{9,8},{10,11... | collective-permute-start | bytes 1179656 | tf_op jit(solution)/shard_map/ppermute | solution.py:452
  23.7 9.2 %collective-permute-start.2 = (bf16[384,512]{1,0:T(8,128)(2,1)S(1)}, bf16[384,512]{1,0:T(8,128)(2,1)S(1)}, u32[]{:S(2)}, u32[]{:S(2)}) collective-permute-start(bf16[384,512]{1,0:T(8,128)(2,1)S(1)} %get-tuple-element.63), channel_id=1, source_target_pairs={{0,1},{1,0},{2,3},{3,2},{4,5},{5,4},{6,7},{7,6},{8,9},{9,8},{10,11... | collective-permute-start | bytes 1179656 | tf_op jit(solution)/shard_map/ppermute | solution.py:452
  24.2 10.3 %collective-permute-start.3 = (bf16[384,512]{1,0:T(8,128)(2,1)S(1)}, bf16[384,512]{1,0:T(8,128)(2,1)S(1)}, u32[]{:S(2)}, u32[]{:S(2)}) collective-permute-start(bf16[384,512]{1,0:T(8,128)(2,1)S(1)} %get-tuple-element.64), channel_id=1, source_target_pairs={{0,1},{1,0},{2,3},{3,2},{4,5},{5,4},{6,7},{7,6},{8,9},{9,8},{10,11... | collective-permute-start | bytes 1179656 | tf_op jit(solution)/shard_map/ppermute | solution.py:452
  24.2 11.9 %collective-permute-start.4 = (bf16[384,512]{1,0:T(8,128)(2,1)S(1)}, bf16[384,512]{1,0:T(8,128)(2,1)S(1)}, u32[]{:S(2)}, u32[]{:S(2)}) collective-permute-start(bf16[384,512]{1,0:T(8,128)(2,1)S(1)} %get-tuple-element.65), channel_id=1, source_target_pairs={{0,1},{1,0},{2,3},{3,2},{4,5},{5,4},{6,7},{7,6},{8,9},{9,8},{10,11... | collective-permute-start | bytes 1179656 | tf_op jit(solution)/shard_map/ppermute | solution.py:452
  28.2 12.4 %collective-permute-start.10 = (bf16[384,512]{1,0:T(8,128)(2,1)S(1)}, bf16[384,512]{1,0:T(8,128)(2,1)S(1)}, u32[]{:S(2)}, u32[]{:S(2)}) collective-permute-start(bf16[384,512]{1,0:T(8,128)(2,1)S(1)} %get-tuple-element.68.refs_0_), channel_id=1, source_target_pairs={{0,4},{4,0},{8,12},{12,8},{1,5},{5,1},{9,13},{13,9},{2,6},{6,2},{1... | collective-permute-start | bytes 1179656 | tf_op jit(solution)/shard_map/ppermute | solution.py:414
  32.9 13.3 %collective-permute-start.9 = (bf16[384,512]{1,0:T(8,128)(2,1)S(1)}, bf16[384,512]{1,0:T(8,128)(2,1)S(1)}, u32[]{:S(2)}, u32[]{:S(2)}) collective-permute-start(bf16[384,512]{1,0:T(8,128)(2,1)S(1)} %add.25.refs_8_.refs_0_), channel_id=1, source_target_pairs={{4,8},{8,4},{20,24},{24,20},{0,16},{16,0},{12,28},{28,12},{5,9},{9... | collective-permute-start | bytes 1179656 | tf_op jit(solution)/shard_map/ppermute | solution.py:420
  34.5 14.0 %collective-permute-start.8 = (bf16[384,512]{1,0:T(8,128)(2,1)S(1)}, bf16[384,512]{1,0:T(8,128)(2,1)S(1)}, u32[]{:S(2)}, u32[]{:S(2)}) collective-permute-start(bf16[384,512]{1,0:T(8,128)(2,1)S(1)} %get-tuple-element.69.refs_2_.refs_0_), channel_id=1, source_target_pairs={{0,4},{4,0},{8,12},{12,8},{1,5},{5,1},{9,13},{13,9},{2,6},{6,2},{1... | collective-permute-start | bytes 1179656 | tf_op jit(solution)/shard_map/ppermute | solution.py:414
  41.2 12.8 %collective-permute-start.13 = (bf16[384,512]{1,0:T(8,128)(2,1)S(1)}, bf16[384,512]{1,0:T(8,128)(2,1)S(1)}, u32[]{:S(2)}, u32[]{:S(2)}) collective-permute-start(bf16[384,512]{1,0:T(8,128)(2,1)S(1)} %add.27.refs_0_), channel_id=1, source_target_pairs={{4,8},{8,4},{20,24},{24,20},{0,16},{16,0},{12,28},{28,12},{5,9},{9... | collective-permute-start | bytes 1179656 | tf_op jit(solution)/shard_map/ppermute | solution.py:420
  46.8 7.2 %copy-start = (bf16[384,512]{1,0:T(8,128)(2,1)}, bf16[384,512]{1,0:T(8,128)(2,1)S(1)}, u32[]{:S(2)}) copy-start(bf16[384,512]{1,0:T(8,128)(2,1)S(1)} %square.15.refs_2_.refs_0_) | copy-start | bytes 1179652
  46.8 11.2 %collective-permute-start.12 = (bf16[384,512]{1,0:T(8,128)(2,1)S(1)}, bf16[384,512]{1,0:T(8,128)(2,1)S(1)}, u32[]{:S(2)}, u32[]{:S(2)}) collective-permute-start(bf16[384,512]{1,0:T(8,128)(2,1)S(1)} %square.15.refs_2_.refs_0_), channel_id=1, source_target_pairs={{0,4},{4,0},{8,12},{12,8},{1,5},{5,1},{9,13},{13,9},{2,6},{6,2},{1... | collective-permute-start | bytes 1179656 | tf_op jit(solution)/shard_map/ppermute | solution.py:414
  49.1 13.3 %collective-permute-start.11 = (bf16[384,512]{1,0:T(8,128)(2,1)S(1)}, bf16[384,512]{1,0:T(8,128)(2,1)S(1)}, u32[]{:S(2)}, u32[]{:S(2)}) collective-permute-start(bf16[384,512]{1,0:T(8,128)(2,1)S(1)} %add.28.refs_0_), channel_id=1, source_target_pairs={{4,8},{8,4},{20,24},{24,20},{0,16},{16,0},{12,28},{28,12},{5,9},{9... | collective-permute-start | bytes 1179656 | tf_op jit(solution)/shard_map/ppermute | solution.py:420
  54.6 11.4 %collective-permute-start.22 = (bf16[384,512]{1,0:T(8,128)(2,1)S(1)}, bf16[384,512]{1,0:T(8,128)(2,1)S(1)}, u32[]{:S(2)}, u32[]{:S(2)}) collective-permute-start(bf16[384,512]{1,0:T(8,128)(2,1)S(1)} %square.16.refs_2_.refs_0_), channel_id=1, source_target_pairs={{0,4},{4,0},{8,12},{12,8},{1,5},{5,1},{9,13},{13,9},{2,6},{6,2},{1... | collective-permute-start | bytes 1179656 | tf_op jit(solution)/shard_map/ppermute | solution.py:414
  58.0 4.4 %copy-start.3 = (bf16[384,512]{1,0:T(8,128)(2,1)}, bf16[384,512]{1,0:T(8,128)(2,1)S(1)}, u32[]{:S(2)}) copy-start(bf16[384,512]{1,0:T(8,128)(2,1)S(1)} %collective-permute-done.12.refs_1_) | copy-start | bytes 1179652
  58.6 10.5 %collective-permute-start.21 = (bf16[384,512]{1,0:T(8,128)(2,1)S(1)}, bf16[384,512]{1,0:T(8,128)(2,1)S(1)}, u32[]{:S(2)}, u32[]{:S(2)}) collective-permute-start(bf16[384,512]{1,0:T(8,128)(2,1)S(1)} %add.29.refs_0_), channel_id=1, source_target_pairs={{4,8},{8,4},{20,24},{24,20},{0,16},{16,0},{12,28},{28,12},{5,9},{9... | collective-permute-start | bytes 1179656 | tf_op jit(solution)/shard_map/ppermute | solution.py:420
  65.4 3.7 %collective-permute-start.14 = (bf16[192,1024]{1,0:T(8,128)(2,1)S(1)}, bf16[192,1024]{1,0:T(8,128)(2,1)S(1)}, u32[]{:S(2)}, u32[]{:S(2)}) collective-permute-start(bf16[192,1024]{1,0:T(8,128)(2,1)S(1)} %get-tuple-element.78), channel_id=1, source_target_pairs={{0,1},{1,0},{2,3},{3,2},{4,5},{5,4},{6,7},{7,6},{8,9},{9,8},{10,11... | collective-permute-start | bytes 1179656 | tf_op jit(solution)/shard_map/ppermute | solution.py:467
  65.5 4.2 %collective-permute-start.15 = (bf16[192,1024]{1,0:T(8,128)(2,1)S(1)}, bf16[192,1024]{1,0:T(8,128)(2,1)S(1)}, u32[]{:S(2)}, u32[]{:S(2)}) collective-permute-start(bf16[192,1024]{1,0:T(8,128)(2,1)S(1)} %get-tuple-element.79), channel_id=1, source_target_pairs={{0,1},{1,0},{2,3},{3,2},{4,5},{5,4},{6,7},{7,6},{8,9},{9,8},{10,11... | collective-permute-start | bytes 1179656 | tf_op jit(solution)/shard_map/ppermute | solution.py:467
  66.0 3.8 %collective-permute-start.16 = (bf16[192,1024]{1,0:T(8,128)(2,1)S(1)}, bf16[192,1024]{1,0:T(8,128)(2,1)S(1)}, u32[]{:S(2)}, u32[]{:S(2)}) collective-permute-start(bf16[192,1024]{1,0:T(8,128)(2,1)S(1)} %get-tuple-element.80), channel_id=1, source_target_pairs={{0,1},{1,0},{2,3},{3,2},{4,5},{5,4},{6,7},{7,6},{8,9},{9,8},{10,11... | collective-permute-start | bytes 1179656 | tf_op jit(solution)/shard_map/ppermute | solution.py:467
  66.0 5.1 %collective-permute-start.17 = (bf16[192,1024]{1,0:T(8,128)(2,1)S(1)}, bf16[192,1024]{1,0:T(8,128)(2,1)S(1)}, u32[]{:S(2)}, u32[]{:S(2)}) collective-permute-start(bf16[192,1024]{1,0:T(8,128)(2,1)S(1)} %get-tuple-element.81), channel_id=1, source_target_pairs={{0,1},{1,0},{2,3},{3,2},{4,5},{5,4},{6,7},{7,6},{8,9},{9,8},{10,11... | collective-permute-start | bytes 1179656 | tf_op jit(solution)/shard_map/ppermute | solution.py:467
  69.1 4.1 %collective-permute-start.18 = (bf16[192,1024]{1,0:T(8,128)(2,1)S(1)}, bf16[192,1024]{1,0:T(8,128)(2,1)S(1)}, u32[]{:S(2)}, u32[]{:S(2)}) collective-permute-start(bf16[192,1024]{1,0:T(8,128)(2,1)S(1)} %get-tuple-element.82), channel_id=1, source_target_pairs={{0,1},{1,0},{2,3},{3,2},{4,5},{5,4},{6,7},{7,6},{8,9},{9,8},{10,11... | collective-permute-start | bytes 1179656 | tf_op jit(solution)/shard_map/ppermute | solution.py:467
  69.1 6.3 %collective-permute-start.19 = (bf16[192,1024]{1,0:T(8,128)(2,1)S(1)}, bf16[192,1024]{1,0:T(8,128)(2,1)S(1)}, u32[]{:S(2)}, u32[]{:S(2)}) collective-permute-start(bf16[192,1024]{1,0:T(8,128)(2,1)S(1)} %get-tuple-element.83), channel_id=1, source_target_pairs={{0,1},{1,0},{2,3},{3,2},{4,5},{5,4},{6,7},{7,6},{8,9},{9,8},{10,11... | collective-permute-start | bytes 1179656 | tf_op jit(solution)/shard_map/ppermute | solution.py:467
  69.6 7.6 %collective-permute-start.20 = (bf16[192,1024]{1,0:T(8,128)(2,1)S(1)}, bf16[192,1024]{1,0:T(8,128)(2,1)S(1)}, u32[]{:S(2)}, u32[]{:S(2)}) collective-permute-start(bf16[192,1024]{1,0:T(8,128)(2,1)S(1)} %get-tuple-element.84.refs_2_), channel_id=1, source_target_pairs={{0,1},{1,0},{2,3},{3,2},{4,5},{5,4},{6,7},{7,6},{8,9},{9,8},{10,11... | collective-permute-start | bytes 1179656 | tf_op jit(solution)/shard_map/ppermute | solution.py:467
  69.7 12.9 %collective-permute-start.25 = (bf16[384,512]{1,0:T(8,128)(2,1)S(1)}, bf16[384,512]{1,0:T(8,128)(2,1)S(1)}, u32[]{:S(2)}, u32[]{:S(2)}) collective-permute-start(bf16[384,512]{1,0:T(8,128)(2,1)S(1)} %square.17.refs_0_.refs_4_), channel_id=1, source_target_pairs={{0,4},{4,0},{8,12},{12,8},{1,5},{5,1},{9,13},{13,9},{2,6},{6,2},{1... | collective-permute-start | bytes 1179656 | tf_op jit(solution)/shard_map/ppermute | solution.py:414
  71.1 52.8 %collective-permute-start.6 = (bf16[384,2048]{1,0:T(8,128)(2,1)S(1)}, bf16[384,2048]{1,0:T(8,128)(2,1)S(1)}, u32[]{:S(2)}, u32[]{:S(2)}) collective-permute-start(bf16[384,2048]{1,0:T(8,128)(2,1)S(1)} %add.26.refs_0_), channel_id=1, source_target_pairs={{0,2},{2,0},{1,3},{3,1},{4,6},{6,4},{5,7},{7,5},{8,10},{10,8},{9,1... | collective-permute-start | bytes 4718600 | tf_op jit(solution)/shard_map/ppermute | solution.py:459
  73.3 11.6 %collective-permute-start.24 = (bf16[384,512]{1,0:T(8,128)(2,1)S(1)}, bf16[384,512]{1,0:T(8,128)(2,1)S(1)}, u32[]{:S(2)}, u32[]{:S(2)}) collective-permute-start(bf16[384,512]{1,0:T(8,128)(2,1)S(1)} %add.30.refs_3_.refs_0_), channel_id=1, source_target_pairs={{4,8},{8,4},{20,24},{24,20},{0,16},{16,0},{12,28},{28,12},{5,9},{9... | collective-permute-start | bytes 1179656 | tf_op jit(solution)/shard_map/ppermute | solution.py:420
  75.5 14.6 %collective-permute-start.23 = (bf16[384,512]{1,0:T(8,128)(2,1)S(1)}, bf16[384,512]{1,0:T(8,128)(2,1)S(1)}, u32[]{:S(2)}, u32[]{:S(2)}) collective-permute-start(bf16[384,512]{1,0:T(8,128)(2,1)S(1)} %square.18.refs_8_.refs_0_), channel_id=1, source_target_pairs={{0,4},{4,0},{8,12},{12,8},{1,5},{5,1},{9,13},{13,9},{2,6},{6,2},{1... | collective-permute-start | bytes 1179656 | tf_op jit(solution)/shard_map/ppermute | solution.py:414
  83.2 12.6 %collective-permute-start.26 = (bf16[384,512]{1,0:T(8,128)(2,1)S(1)}, bf16[384,512]{1,0:T(8,128)(2,1)S(1)}, u32[]{:S(2)}, u32[]{:S(2)}) collective-permute-start(bf16[384,512]{1,0:T(8,128)(2,1)S(1)} %add.31.refs_3_.refs_0_), channel_id=1, source_target_pairs={{4,8},{8,4},{20,24},{24,20},{0,16},{16,0},{12,28},{28,12},{5,9},{9... | collective-permute-start | bytes 1179656 | tf_op jit(solution)/shard_map/ppermute | solution.py:420
  85.4 12.7 %collective-permute-start.29 = (bf16[384,512]{1,0:T(8,128)(2,1)S(1)}, bf16[384,512]{1,0:T(8,128)(2,1)S(1)}, u32[]{:S(2)}, u32[]{:S(2)}) collective-permute-start(bf16[384,512]{1,0:T(8,128)(2,1)S(1)} %square.19.refs_2_.refs_4_), channel_id=1, source_target_pairs={{0,4},{4,0},{8,12},{12,8},{1,5},{5,1},{9,13},{13,9},{2,6},{6,2},{1... | collective-permute-start | bytes 1179656 | tf_op jit(solution)/shard_map/ppermute | solution.py:414
  90.7 13.2 %collective-permute-start.28 = (bf16[384,512]{1,0:T(8,128)(2,1)S(1)}, bf16[384,512]{1,0:T(8,128)(2,1)S(1)}, u32[]{:S(2)}, u32[]{:S(2)}) collective-permute-start(bf16[384,512]{1,0:T(8,128)(2,1)S(1)} %add.32.refs_0_), channel_id=1, source_target_pairs={{4,8},{8,4},{20,24},{24,20},{0,16},{16,0},{12,28},{28,12},{5,9},{9... | collective-permute-start | bytes 1179656 | tf_op jit(solution)/shard_map/ppermute | solution.py:420
  96.4 10.1 %collective-permute-start.27 = (bf16[384,512]{1,0:T(8,128)(2,1)S(1)}, bf16[384,512]{1,0:T(8,128)(2,1)S(1)}, u32[]{:S(2)}, u32[]{:S(2)}) collective-permute-start(bf16[384,512]{1,0:T(8,128)(2,1)S(1)} %square.20.refs_2_.refs_0_), channel_id=1, source_target_pairs={{0,4},{4,0},{8,12},{12,8},{1,5},{5,1},{9,13},{13,9},{2,6},{6,2},{1... | collective-permute-start | bytes 1179656 | tf_op jit(solution)/shard_map/ppermute | solution.py:414
  98.8 13.5 %collective-permute-start.32 = (bf16[384,512]{1,0:T(8,128)(2,1)S(1)}, bf16[384,512]{1,0:T(8,128)(2,1)S(1)}, u32[]{:S(2)}, u32[]{:S(2)}) collective-permute-start(bf16[384,512]{1,0:T(8,128)(2,1)S(1)} %add.33.refs_0_), channel_id=1, source_target_pairs={{4,8},{8,4},{20,24},{24,20},{0,16},{16,0},{12,28},{28,12},{5,9},{9... | collective-permute-start | bytes 1179656 | tf_op jit(solution)/shard_map/ppermute | solution.py:420
  104.5 11.4 %collective-permute-start.31 = (bf16[384,512]{1,0:T(8,128)(2,1)S(1)}, bf16[384,512]{1,0:T(8,128)(2,1)S(1)}, u32[]{:S(2)}, u32[]{:S(2)}) collective-permute-start(bf16[384,512]{1,0:T(8,128)(2,1)S(1)} %square.21.refs_2_.refs_0_), channel_id=1, source_target_pairs={{0,4},{4,0},{8,12},{12,8},{1,5},{5,1},{9,13},{13,9},{2,6},{6,2},{1... | collective-permute-start | bytes 1179656 | tf_op jit(solution)/shard_map/ppermute | solution.py:414
  107.1 14.0 %collective-permute-start.30 = (bf16[384,512]{1,0:T(8,128)(2,1)S(1)}, bf16[384,512]{1,0:T(8,128)(2,1)S(1)}, u32[]{:S(2)}, u32[]{:S(2)}) collective-permute-start(bf16[384,512]{1,0:T(8,128)(2,1)S(1)} %add.34.refs_0_), channel_id=1, source_target_pairs={{4,8},{8,4},{20,24},{24,20},{0,16},{16,0},{12,28},{28,12},{5,9},{9... | collective-permute-start | bytes 1179656 | tf_op jit(solution)/shard_map/ppermute | solution.py:420
  112.9 12.6 %collective-permute-start.37 = (bf16[384,512]{1,0:T(8,128)(2,1)S(1)}, bf16[384,512]{1,0:T(8,128)(2,1)S(1)}, u32[]{:S(2)}, u32[]{:S(2)}) collective-permute-start(bf16[384,512]{1,0:T(8,128)(2,1)S(1)} %square.22.refs_2_), channel_id=1, source_target_pairs={{0,4},{4,0},{8,12},{12,8},{1,5},{5,1},{9,13},{13,9},{2,6},{6,2},{1... | collective-permute-start | bytes 1179656 | tf_op jit(solution)/shard_map/ppermute | solution.py:414
  116.4 14.7 %collective-permute-start.36 = (bf16[384,512]{1,0:T(8,128)(2,1)S(1)}, bf16[384,512]{1,0:T(8,128)(2,1)S(1)}, u32[]{:S(2)}, u32[]{:S(2)}) collective-permute-start(bf16[384,512]{1,0:T(8,128)(2,1)S(1)} %add.35.refs_0_), channel_id=1, source_target_pairs={{4,8},{8,4},{20,24},{24,20},{0,16},{16,0},{12,28},{28,12},{5,9},{9... | collective-permute-start | bytes 1179656 | tf_op jit(solution)/shard_map/ppermute | solution.py:420
  121.7 11.9 %collective-permute-start.35 = (bf16[384,512]{1,0:T(8,128)(2,1)S(1)}, bf16[384,512]{1,0:T(8,128)(2,1)S(1)}, u32[]{:S(2)}, u32[]{:S(2)}) collective-permute-start(bf16[384,512]{1,0:T(8,128)(2,1)S(1)} %square.23.refs_2_), channel_id=1, source_target_pairs={{0,4},{4,0},{8,12},{12,8},{1,5},{5,1},{9,13},{13,9},{2,6},{6,2},{1... | collective-permute-start | bytes 1179656 | tf_op jit(solution)/shard_map/ppermute | solution.py:414
  124.9 22.1 %collective-permute-start.33 = (bf16[384,1024]{1,0:T(8,128)(2,1)S(1)}, bf16[384,1024]{1,0:T(8,128)(2,1)S(1)}, u32[]{:S(2)}, u32[]{:S(2)}) collective-permute-start(bf16[384,1024]{1,0:T(8,128)(2,1)S(1)} %get-tuple-element.95.refs_0_), channel_id=1, source_target_pairs={{0,1},{1,0},{2,3},{3,2},{4,5},{5,4},{6,7},{7,6},{8,9},{9,8},{10,11... | collective-permute-start | bytes 2359304 | tf_op jit(solution)/shard_map/ppermute | solution.py:481
  125.0 22.0 %collective-permute-start.34 = (bf16[384,1024]{1,0:T(8,128)(2,1)S(1)}, bf16[384,1024]{1,0:T(8,128)(2,1)S(1)}, u32[]{:S(2)}, u32[]{:S(2)}) collective-permute-start(bf16[384,1024]{1,0:T(8,128)(2,1)S(1)} %get-tuple-element.96.refs_2_.refs_1_), channel_id=1, source_target_pairs={{0,1},{1,0},{2,3},{3,2},{4,5},{5,4},{6,7},{7,6},{8,9},{9,8},{10,11... | collective-permute-start | bytes 2359304 | tf_op jit(solution)/shard_map/ppermute | solution.py:481
  126.1 12.2 %collective-permute-start.40 = (bf16[384,512]{1,0:T(8,128)(2,1)S(1)}, bf16[384,512]{1,0:T(8,128)(2,1)S(1)}, u32[]{:S(2)}, u32[]{:S(2)}) collective-permute-start(bf16[384,512]{1,0:T(8,128)(2,1)S(1)} %add.36.refs_0_), channel_id=1, source_target_pairs={{4,8},{8,4},{20,24},{24,20},{0,16},{16,0},{12,28},{28,12},{5,9},{9... | collective-permute-start | bytes 1179656 | tf_op jit(solution)/shard_map/ppermute | solution.py:420
  132.0 12.1 %collective-permute-start.39 = (bf16[384,512]{1,0:T(8,128)(2,1)S(1)}, bf16[384,512]{1,0:T(8,128)(2,1)S(1)}, u32[]{:S(2)}, u32[]{:S(2)}) collective-permute-start(bf16[384,512]{1,0:T(8,128)(2,1)S(1)} %square.25.refs_2_.refs_6_), channel_id=1, source_target_pairs={{0,4},{4,0},{8,12},{12,8},{1,5},{5,1},{9,13},{13,9},{2,6},{6,2},{1... | collective-permute-start | bytes 1179656 | tf_op jit(solution)/shard_map/ppermute | solution.py:414
  134.2 12.1 %collective-permute-start.38 = (bf16[384,512]{1,0:T(8,128)(2,1)S(1)}, bf16[384,512]{1,0:T(8,128)(2,1)S(1)}, u32[]{:S(2)}, u32[]{:S(2)}) collective-permute-start(bf16[384,512]{1,0:T(8,128)(2,1)S(1)} %add.37.refs_0_), channel_id=1, source_target_pairs={{4,8},{8,4},{20,24},{24,20},{0,16},{16,0},{12,28},{28,12},{5,9},{9... | collective-permute-start | bytes 1179656 | tf_op jit(solution)/shard_map/ppermute | solution.py:420
  138.3 10.1 %copy-start.1 = (bf16[384,512]{1,0:T(8,128)(2,1)S(1)}, bf16[384,512]{1,0:T(8,128)(2,1)}, u32[]{:S(2)}) copy-start(bf16[384,512]{1,0:T(8,128)(2,1)} %copy-done) | copy-start | bytes 1179652
  138.3 10.1 %copy-start.4 = (bf16[384,512]{1,0:T(8,128)(2,1)S(1)}, bf16[384,512]{1,0:T(8,128)(2,1)}, u32[]{:S(2)}) copy-start(bf16[384,512]{1,0:T(8,128)(2,1)} %copy-done.3) | copy-start | bytes 1179652
  138.9 13.4 %collective-permute-start.41 = (bf16[384,512]{1,0:T(8,128)(2,1)S(1)}, bf16[384,512]{1,0:T(8,128)(2,1)S(1)}, u32[]{:S(2)}, u32[]{:S(2)}) collective-permute-start(bf16[384,512]{1,0:T(8,128)(2,1)S(1)} %square.26.refs_2_), channel_id=1, source_target_pairs={{0,4},{4,0},{8,12},{12,8},{1,5},{5,1},{9,13},{13,9},{2,6},{6,2},{1... | collective-permute-start | bytes 1179656 | tf_op jit(solution)/shard_map/ppermute | solution.py:414
  144.7 11.6 %collective-permute-start.43 = (bf16[384,512]{1,0:T(8,128)(2,1)S(1)}, bf16[384,512]{1,0:T(8,128)(2,1)S(1)}, u32[]{:S(2)}, u32[]{:S(2)}) collective-permute-start(bf16[384,512]{1,0:T(8,128)(2,1)S(1)} %add.38.refs_2_.refs_0_), channel_id=1, source_target_pairs={{4,8},{8,4},{20,24},{24,20},{0,16},{16,0},{12,28},{28,12},{5,9},{9... | collective-permute-start | bytes 1179656 | tf_op jit(solution)/shard_map/ppermute | solution.py:420
  152.9 10.9 %collective-permute-start.42 = (bf16[384,512]{1,0:T(8,128)(2,1)S(1)}, bf16[384,512]{1,0:T(8,128)(2,1)S(1)}, u32[]{:S(2)}, u32[]{:S(2)}) collective-permute-start(bf16[384,512]{1,0:T(8,128)(2,1)S(1)} %add.39.refs_2_.refs_0_), channel_id=1, source_target_pairs={{4,8},{8,4},{20,24},{24,20},{0,16},{16,0},{12,28},{28,12},{5,9},{9... | collective-permute-start | bytes 1179656 | tf_op jit(solution)/shard_map/ppermute | solution.py:420
  154.8 12.1 %collective-permute-start.46 = (bf16[384,512]{1,0:T(8,128)(2,1)S(1)}, bf16[384,512]{1,0:T(8,128)(2,1)S(1)}, u32[]{:S(2)}, u32[]{:S(2)}) collective-permute-start(bf16[384,512]{1,0:T(8,128)(2,1)S(1)} %square.27.refs_4_.refs_6_), channel_id=1, source_target_pairs={{0,4},{4,0},{8,12},{12,8},{1,5},{5,1},{9,13},{13,9},{2,6},{6,2},{1... | collective-permute-start | bytes 1179656 | tf_op jit(solution)/shard_map/ppermute | solution.py:414
  156.9 18.4 %collective-permute-start.45 = (bf16[384,512]{1,0:T(8,128)(2,1)S(1)}, bf16[384,512]{1,0:T(8,128)(2,1)S(1)}, u32[]{:S(2)}, u32[]{:S(2)}) collective-permute-start(bf16[384,512]{1,0:T(8,128)(2,1)S(1)} %square.28.refs_9_.refs_2_), channel_id=1, source_target_pairs={{0,4},{4,0},{8,12},{12,8},{1,5},{5,1},{9,13},{13,9},{2,6},{6,2},{1... | collective-permute-start | bytes 1179656 | tf_op jit(solution)/shard_map/ppermute | solution.py:414
  164.5 16.2 %collective-permute-start.44 = (bf16[384,512]{1,0:T(8,128)(2,1)S(1)}, bf16[384,512]{1,0:T(8,128)(2,1)S(1)}, u32[]{:S(2)}, u32[]{:S(2)}) collective-permute-start(bf16[384,512]{1,0:T(8,128)(2,1)S(1)} %square.29.refs_9_.refs_2_), channel_id=1, source_target_pairs={{0,4},{4,0},{8,12},{12,8},{1,5},{5,1},{9,13},{13,9},{2,6},{6,2},{1... | collective-permute-start | bytes 1179656 | tf_op jit(solution)/shard_map/ppermute | solution.py:414

commit v4 on v3

--- a/solution.py
+++ b/solution.py
@@ -479,9 +479,9 @@
         if k == 9:
             own = small(square_pieces_body, [(act.shape[0], columns // 2)] * 2, [act, act_far], "square")
             other = [lax.ppermute(piece, "gc", CORES) for piece in own]
+    (act_sq,) = small(stack_body, [(columns, 2 * act.shape[0])], [*own, *other], "stack")
     add(12)
     send(14)
-    (act_sq,) = small(stack_body, [(columns, 2 * act.shape[0])], [*own, *other], "stack")
     correct_next(1)
     add(13)
     send(15)

time: 186 us -> 185 us (level)
  transfers between devices with their start and end apart: 47 -> 47, of which waited for: 10 -> 12; matrix products, arithmetic and copies ran while one was open for 0% -> 0% of each run, Pallas kernels for 58% -> 59%
where the time goes in v4:
time: 185 us
  Pallas kernels  113 us (61%)
  starting transfers between devices  54 us (29%)
  waiting for transfers between devices  17.4 us (9%)
    pallas_call x14, Pallas kernels, project(): pl.pallas_call(body, in_specs=[VMEM, ANYWHERE, VMEM] + [ANYWHERE] * len(a...  48.4 us
    ppermute x17, starting transfers between devices, send(): received.append(lax.ppermute(payload, 'gr', OUTER))  26.7 us
    pallas_call x5, Pallas kernels, correct(): pl.pallas_call(body, in_specs=[pl.BlockSpec(memory_space=pltpu.SMEM)] + [...  24.8 us
    pallas_call x31, Pallas kernels, whole(): pl.pallas_call(run, in_specs=[pl.BlockSpec(memory_space=pltpu.SMEM)] + [V...  21 us
    ppermute x14, starting transfers between devices, add(): others.append(lax.ppermute(sums[-1], ('layers', 'gr'), INNER))  19.6 us
    ppermute x17, waiting for transfers between devices, send(): received.append(lax.ppermute(payload, 'gr', OUTER))  13.8 us
    pallas_call x1, Pallas kernels, project_acts(): pl.pallas_call(body, grid_spec=pltpu.PrefetchScalarGridSpec(num_scalar_pr...  9.88 us
  transfers between devices with their start and end apart: 47, of which 12 were waited for; matrix products, arithmetic and copies ran while one was open for 0% of the time, Pallas kernels for 59%

profile of v4, /device:TPU:0, one launch (start us, length us, event | category | flops | bytes accessed | tf_op | source)
XLA Modules:
  0.0 185.1 jit_solution(7412737621437218100)
XLA Ops:
  0.5 2.5 %collective-permute-start.7 = (bf16[192,7168]{1,0:T(8,128)(2,1)}, bf16[192,7168]{1,0:T(8,128)(2,1)}, u32[]{:S(2)}, u32[]{:S(2)}) collective-permute-start(bf16[192,7168]{1,0:T(8,128)(2,1)} %refs_0_.1), channel_id=1, source_target_pairs={{0,2},{2,0},{1,3},{3,1},{4,6},{6,4},{5,7},{7,5},{8,10},{10,8},{9,1... | collective-permute-start | bytes 8257544 | tf_op jit(solution)/shard_map/ppermute | solution.py:441
  3.0 3.2 %fetch.1.refs_2_.block_ref = bf16[7168,512]{1,0:T(8,128)(2,1)S(1)} custom-call(bf16[7168,3584]{1,0:T(8,128)(2,1)} %basis_ref.31, s32[3]{0:T(128)S(1)} %pad_add_fusion.refs_0_.flags_ref), custom_call_target="tpu_custom_call" | custom-call | flops 10000000 | bytes 100000 | tf_op jit(solution)/shard_map/fetch/pallas_call | solution.py:212
  6.3 1.8 join.2.rows_ref.refs_0_
  8.1 3.5 %project_grads.14 = (bf16[384,512]{1,0:T(8,128)(2,1)S(1)}, bf16[7168,512]{1,0:T(8,128)(2,1)S(1)}) custom-call(bf16[384,7168]{1,0:T(8,128)(2,1)S(1)} %join.2.rows_ref.refs_0_, bf16[7168,3584]{1,0:T(8,128)(2,1)} %basis_ref.31, bf16[7168,512]{1,0:T(8,128)(2,1)S(1)} %fetch.1.refs_2_.block_ref, bf16[384,7168]{1,0:T(8,128)(2,1)S(1)} %join.2.rows_ref.refs_0_), custom_call_target="tpu_custom_call" | custom-call | flops 10000000 | bytes 100000 | tf_op jit(solution)/shard_map/project_grads/pallas_call | solution.py:245
  11.5 2.1 %collective-permute-start.5 = (bf16[384,512]{1,0:T(8,128)(2,1)S(1)}, bf16[384,512]{1,0:T(8,128)(2,1)S(1)}, u32[]{:S(2)}, u32[]{:S(2)}) collective-permute-start(bf16[384,512]{1,0:T(8,128)(2,1)S(1)} %get-tuple-element.57.refs_0_), channel_id=1, source_target_pairs={{0,4},{4,0},{8,12},{12,8},{1,5},{5,1},{9,13},{13,9},{2,6},{6,2},{1... | collective-permute-start | bytes 1179656 | tf_op jit(solution)/shard_map/ppermute | solution.py:414
  13.7 9.9 %project_acts.1 = (bf16[384,512]{1,0:T(8,128)(2,1)S(1)}, bf16[384,512]{1,0:T(8,128)(2,1)S(1)}, bf16[384,512]{1,0:T(8,128)(2,1)S(1)}, bf16[384,512]{1,0:T(8,128)(...) custom-call(s32[3]{0:T(128)S(1)} %pad_add_fusion.refs_0_.flags_ref, ...), custom_call_target="tpu_custom_call" | custom-call | flops 10000000 | bytes 100000 | tf_op jit(solution)/shard_map/project_acts/pallas_call | solution.py:285
  24.7 3.5 %project_grads.15 = (bf16[384,512]{1,0:T(8,128)(2,1)S(1)}, bf16[7168,512]{1,0:T(8,128)(2,1)S(1)}) custom-call(bf16[384,7168]{1,0:T(8,128)(2,1)S(1)} %join.2.rows_ref.refs_0_, bf16[7168,3584]{1,0:T(8,128)(2,1)} %basis_ref.31, bf16[7168,512]{1,0:T(8,128)(2,1)S(1)} %get-tuple-element.66.block_ref, bf16[384,512]{1,0:T(8,128)(2,1)S(1)} %get-tuple-element.61.refs_0_.refs_3_), custom_call_target="tpu_custom_call" | custom-call | flops 10000000 | bytes 100000 | tf_op jit(solution)/shard_map/project_grads/pallas_call | solution.py:245
  28.8 3.5 %project_grads.16 = (bf16[384,512]{1,0:T(8,128)(2,1)S(1)}, bf16[7168,512]{1,0:T(8,128)(2,1)S(1)}) custom-call(bf16[384,7168]{1,0:T(8,128)(2,1)S(1)} %join.2.rows_ref.refs_0_, bf16[7168,3584]{1,0:T(8,128)(2,1)} %basis_ref.31, bf16[7168,512]{1,0:T(8,128)(2,1)S(1)} %get-tuple-element.67.block_ref, bf16[384,512]{1,0:T(8,128)(2,1)S(1)} %get-tuple-element.68.refs_0_), custom_call_target="tpu_custom_call" | custom-call | flops 10000000 | bytes 100000 | tf_op jit(solution)/shard_map/project_grads/pallas_call | solution.py:245
  32.9 1.6 collective-permute-start.9
  34.5 1.6 collective-permute-start.8
  37.1 3.5 %project_grads.17 = (bf16[384,512]{1,0:T(8,128)(2,1)S(1)}, bf16[7168,512]{1,0:T(8,128)(2,1)S(1)}) custom-call(bf16[384,7168]{1,0:T(8,128)(2,1)S(1)} %join.2.rows_ref.refs_0_, bf16[7168,3584]{1,0:T(8,128)(2,1)} %basis_ref.31, bf16[7168,512]{1,0:T(8,128)(2,1)S(1)} %get-tuple-element.70.block_ref, bf16[384,2048]{1,0:T(8,128)(2,1)S(1)} %add.26.refs_0_), custom_call_target="tpu_custom_call" | custom-call | flops 10000000 | bytes 100000 | tf_op jit(solution)/shard_map/project_grads/pallas_call | solution.py:245
  41.2 1.6 collective-permute-start.13
  42.8 3.5 %project_grads.18 = (bf16[384,512]{1,0:T(8,128)(2,1)S(1)}, bf16[7168,512]{1,0:T(8,128)(2,1)S(1)}) custom-call(bf16[384,7168]{1,0:T(8,128)(2,1)S(1)} %join.2.rows_ref.refs_0_, bf16[7168,3584]{1,0:T(8,128)(2,1)} %basis_ref.31, bf16[7168,512]{1,0:T(8,128)(2,1)S(1)} %get-tuple-element.72.block_ref, bf16[384,512]{1,0:T(8,128)(2,1)S(1)} %add.27.refs_0_), custom_call_target="tpu_custom_call" | custom-call | flops 10000000 | bytes 100000 | tf_op jit(solution)/shard_map/project_grads/pallas_call | solution.py:245
  46.8 1.6 collective-permute-start.12
  49.1 1.4 collective-permute-start.11
  50.5 3.5 %project_grads.19 = (bf16[384,512]{1,0:T(8,128)(2,1)S(1)}, bf16[7168,512]{1,0:T(8,128)(2,1)S(1)}) custom-call(bf16[384,7168]{1,0:T(8,128)(2,1)S(1)} %join.2.rows_ref.refs_0_, bf16[7168,3584]{1,0:T(8,128)(2,1)} %basis_ref.31, bf16[7168,512]{1,0:T(8,128)(2,1)S(1)} %get-tuple-element.74.block_ref, bf16[384,512]{1,0:T(8,128)(2,1)S(1)} %add.28.refs_0_), custom_call_target="tpu_custom_call" | custom-call | flops 10000000 | bytes 100000 | tf_op jit(solution)/shard_map/project_grads/pallas_call | solution.py:245
  54.6 1.8 collective-permute-start.22
  56.4 1.6 collective-permute-done.12.refs_1_
  58.9 3.5 %project_grads.20 = (bf16[384,512]{1,0:T(8,128)(2,1)S(1)}, bf16[7168,512]{1,0:T(8,128)(2,1)S(1)}) custom-call(bf16[384,7168]{1,0:T(8,128)(2,1)S(1)} %join.2.rows_ref.refs_0_, bf16[7168,3584]{1,0:T(8,128)(2,1)} %basis_ref.31, bf16[7168,512]{1,0:T(8,128)(2,1)S(1)} %get-tuple-element.76.block_ref, bf16[384,512]{1,0:T(8,128)(2,1)S(1)} %add.29.refs_0_), custom_call_target="tpu_custom_call" | custom-call | flops 10000000 | bytes 100000 | tf_op jit(solution)/shard_map/project_grads/pallas_call | solution.py:245
  63.6 1.8 split.1
  66.5 2.6 %collective-permute-done.21.refs_1_ = bf16[384,512]{1,0:T(8,128)(2,1)S(1)} collective-permute-done((bf16[384,512]{1,0:T(8,128)(2,1)S(1)}, bf16[384,512]{1,0:T(8,128)(2,1)S(1)}, u32[]{:S(2)}, u32[]{:S(2)}) %collective-permute-start.21) | collective-permute-done | bytes 393248 | tf_op jit(solution)/shard_map/ppermute | solution.py:420
  69.7 1.4 collective-permute-start.25
  71.1 1.5 collective-permute-start.6
  73.3 1.6 collective-permute-start.24
  75.5 1.8 collective-permute-start.23
  77.3 1.9 %join.3.rows_ref.refs_0_ = bf16[384,7168]{1,0:T(8,128)(2,1)S(1)} custom-call(bf16[192,7168]{1,0:T(8,128)(2,1)} %collective-permute-done.7.array_ref.refs_0_, bf16[192,1024]{1,0:T(8,128)(2,1)S(1)} %collective-permute-done.14.refs_1_, bf16[192,1024]{1,0:T(8,128)(2,1)S(1)} %collective-permute-done.15.refs_2_, ...), custom_call_target="tpu_custom_call" | custom-call | flops 10000000 | bytes 100000 | tf_op jit(solution)/shard_map/join/pallas_call | solution.py:167
  79.1 3.5 %project_grads.21 = (bf16[384,512]{1,0:T(8,128)(2,1)S(1)}, bf16[7168,512]{1,0:T(8,128)(2,1)S(1)}) custom-call(bf16[384,7168]{1,0:T(8,128)(2,1)S(1)} %join.3.rows_ref.refs_0_, bf16[7168,3584]{1,0:T(8,128)(2,1)} %basis_ref.31, bf16[7168,512]{1,0:T(8,128)(2,1)S(1)} %get-tuple-element.85.block_ref, bf16[384,7168]{1,0:T(8,128)(2,1)S(1)} %join.3.rows_ref.refs_0_), custom_call_target="tpu_custom_call" | custom-call | flops 10000000 | bytes 100000 | tf_op jit(solution)/shard_map/project_grads/pallas_call | solution.py:245
  83.2 1.6 collective-permute-start.26
  85.4 1.0 collective-permute-start.29
  86.4 3.6 %collective-permute-done.23.refs_1_ = bf16[384,512]{1,0:T(8,128)(2,1)S(1)} collective-permute-done((bf16[384,512]{1,0:T(8,128)(2,1)S(1)}, bf16[384,512]{1,0:T(8,128)(2,1)S(1)}, u32[]{:S(2)}, u32[]{:S(2)}) %collective-permute-start.23) | collective-permute-done | bytes 393248 | tf_op jit(solution)/shard_map/ppermute | solution.py:414
  90.7 1.6 collective-permute-start.28
  92.3 3.5 %project_grads.22 = (bf16[384,512]{1,0:T(8,128)(2,1)S(1)}, bf16[7168,512]{1,0:T(8,128)(2,1)S(1)}) custom-call(bf16[384,7168]{1,0:T(8,128)(2,1)S(1)} %join.3.rows_ref.refs_0_, bf16[7168,3584]{1,0:T(8,128)(2,1)} %basis_ref.31, bf16[7168,512]{1,0:T(8,128)(2,1)S(1)} %get-tuple-element.86.block_ref, bf16[384,512]{1,0:T(8,128)(2,1)S(1)} %add.32.refs_0_), custom_call_target="tpu_custom_call" | custom-call | flops 10000000 | bytes 100000 | tf_op jit(solution)/shard_map/project_grads/pallas_call | solution.py:245
  96.4 1.8 collective-permute-start.27
  98.8 1.6 collective-permute-start.32
  100.4 3.5 %project_grads.23 = (bf16[384,512]{1,0:T(8,128)(2,1)S(1)}, bf16[7168,512]{1,0:T(8,128)(2,1)S(1)}) custom-call(bf16[384,7168]{1,0:T(8,128)(2,1)S(1)} %join.3.rows_ref.refs_0_, bf16[7168,3584]{1,0:T(8,128)(2,1)} %basis_ref.31, bf16[7168,512]{1,0:T(8,128)(2,1)S(1)} %get-tuple-element.89.block_ref, bf16[384,512]{1,0:T(8,128)(2,1)S(1)} %add.33.refs_0_), custom_call_target="tpu_custom_call" | custom-call | flops 10000000 | bytes 100000 | tf_op jit(solution)/shard_map/project_grads/pallas_call | solution.py:245
  104.5 2.0 %collective-permute-start.31 = (bf16[384,512]{1,0:T(8,128)(2,1)S(1)}, bf16[384,512]{1,0:T(8,128)(2,1)S(1)}, u32[]{:S(2)}, u32[]{:S(2)}) collective-permute-start(bf16[384,512]{1,0:T(8,128)(2,1)S(1)} %square.21.refs_2_.refs_0_), channel_id=1, source_target_pairs={{0,4},{4,0},{8,12},{12,8},{1,5},{5,1},{9,13},{13,9},{2,6},{6,2},{1... | collective-permute-start | bytes 1179656 | tf_op jit(solution)/shard_map/ppermute | solution.py:414
  107.1 1.7 collective-permute-start.30
  108.8 3.5 %project_grads.24 = (bf16[384,512]{1,0:T(8,128)(2,1)S(1)}, bf16[7168,512]{1,0:T(8,128)(2,1)S(1)}) custom-call(bf16[384,7168]{1,0:T(8,128)(2,1)S(1)} %join.3.rows_ref.refs_0_, bf16[7168,3584]{1,0:T(8,128)(2,1)} %basis_ref.31, bf16[7168,512]{1,0:T(8,128)(2,1)S(1)} %get-tuple-element.91.block_ref, bf16[384,512]{1,0:T(8,128)(2,1)S(1)} %add.34.refs_0_), custom_call_target="tpu_custom_call" | custom-call | flops 10000000 | bytes 100000 | tf_op jit(solution)/shard_map/project_grads/pallas_call | solution.py:245
  112.9 2.0 %collective-permute-start.35 = (bf16[384,512]{1,0:T(8,128)(2,1)S(1)}, bf16[384,512]{1,0:T(8,128)(2,1)S(1)}, u32[]{:S(2)}, u32[]{:S(2)}) collective-permute-start(bf16[384,512]{1,0:T(8,128)(2,1)S(1)} %square.22.refs_2_), channel_id=1, source_target_pairs={{0,4},{4,0},{8,12},{12,8},{1,5},{5,1},{9,13},{13,9},{2,6},{6,2},{1... | collective-permute-start | bytes 1179656 | tf_op jit(solution)/shard_map/ppermute | solution.py:414
  114.9 0.9 collective-permute-done.31.refs_1_
  116.4 1.2 collective-permute-start.38
  117.7 3.5 %project_grads.25 = (bf16[384,512]{1,0:T(8,128)(2,1)S(1)}, bf16[7168,512]{1,0:T(8,128)(2,1)S(1)}) custom-call(bf16[384,7168]{1,0:T(8,128)(2,1)S(1)} %join.3.rows_ref.refs_0_, bf16[7168,3584]{1,0:T(8,128)(2,1)} %basis_ref.31, bf16[7168,512]{1,0:T(8,128)(2,1)S(1)} %get-tuple-element.92.block_ref, bf16[384,512]{1,0:T(8,128)(2,1)S(1)} %add.35.refs_0_), custom_call_target="tpu_custom_call" | custom-call | flops 10000000 | bytes 100000 | tf_op jit(solution)/shard_map/project_grads/pallas_call | solution.py:245
  121.7 1.0 square.24
  123.4 2.1 %collective-permute-start.37 = (bf16[384,512]{1,0:T(8,128)(2,1)S(1)}, bf16[384,512]{1,0:T(8,128)(2,1)S(1)}, u32[]{:S(2)}, u32[]{:S(2)}) collective-permute-start(bf16[384,512]{1,0:T(8,128)(2,1)S(1)} %square.23.refs_2_), channel_id=1, source_target_pairs={{0,4},{4,0},{8,12},{12,8},{1,5},{5,1},{9,13},{13,9},{2,6},{6,2},{1... | collective-permute-start | bytes 1179656 | tf_op jit(solution)/shard_map/ppermute | solution.py:414
  126.1 1.6 collective-permute-start.36
  127.7 3.5 %project_grads.26 = (bf16[384,512]{1,0:T(8,128)(2,1)S(1)}, bf16[7168,512]{1,0:T(8,128)(2,1)S(1)}) custom-call(bf16[384,7168]{1,0:T(8,128)(2,1)S(1)} %join.3.rows_ref.refs_0_, bf16[7168,3584]{1,0:T(8,128)(2,1)} %basis_ref.31, bf16[7168,512]{1,0:T(8,128)(2,1)S(1)} %get-tuple-element.97.block_ref, bf16[384,512]{1,0:T(8,128)(2,1)S(1)} %add.36.refs_0_), custom_call_target="tpu_custom_call" | custom-call | flops 10000000 | bytes 100000 | tf_op jit(solution)/shard_map/project_grads/pallas_call | solution.py:245
  132.0 1.6 collective-permute-start.41
  133.6 1.8 collective-permute-done.37.refs_1_.refs_3_
  136.0 1.6 collective-permute-start.40
  137.6 3.4 %project_grads.27.refs_2_.refs_3_.refs_0_ = bf16[384,512]{1,0:T(8,128)(2,1)S(1)} custom-call(bf16[384,7168]{1,0:T(8,128)(2,1)S(1)} %join.3.rows_ref.refs_0_, bf16[7168,3584]{1,0:T(8,128)(2,1)} %basis_ref.31, bf16[7168,512]{1,0:T(8,128)(2,1)S(1)} %get-tuple-element.98.block_ref, bf16[384,512]{1,0:T(8,128)(2,1)S(1)} %add.37.refs_0_), custom_call_target="tpu_custom_call" | custom-call | flops 10000000 | bytes 100000 | tf_op jit(solution)/shard_map/project_grads/pallas_call | solution.py:245
  141.6 1.6 collective-permute-start.39
  143.2 1.4 stack.22.refs_2_.act_ref
  146.8 3.9 %correct.5 = (bf16[2048,3584]{1,0:T(8,128)(2,1)}, bf16[16,128]{1,0:T(8,128)(2,1)S(1)}) custom-call(s32[3]{0:T(128)S(1)} %pad_add_fusion.refs_0_.flags_ref, bf16[2048,768]{1,0:T(8,128)(2,1)S(1)} %stack.22.refs_2_.act_ref, bf16[384,512]{1,0:T(8,128)(2,1)S(1)} %copy-done.1, bf16[384,512]{1,0:T(8,128)(2,1)S(1)} %copy-done.4, ...), custom_call_target="tpu_custom_call" | custom-call | flops 10000000 | bytes 100000 | tf_op jit(solution)/shard_map/correct/pallas_call | solution.py:351
  150.7 1.0 collective-permute-done.39.refs_1_.refs_3_
  152.3 1.6 collective-permute-start.42
  153.9 1.4 collective-permute-start.46
  156.4 1.1 collective-permute-start.45
  157.6 6.3 %correct.6 = (bf16[2048,3584]{1,0:T(8,128)(2,1)}, bf16[16,128]{1,0:T(8,128)(2,1)S(1)}) custom-call(s32[3]{0:T(128)S(1)} %pad_add_fusion.refs_0_.flags_ref, bf16[2048,768]{1,0:T(8,128)(2,1)S(1)} %stack.22.refs_2_.act_ref, bf16[384,512]{1,0:T(8,128)(2,1)S(1)} %square.16.refs_2_.refs_0_, ...), custom_call_target="tpu_custom_call", output_to_operand_aliasing={{0}: (10, {})} | custom-call | flops 10000000 | bytes 100000 | tf_op jit(solution)/shard_map/correct/pallas_call | solution.py:351
  164.6 1.0 collective-permute-start.44
  165.9 6.3 %correct.7 = (bf16[2048,3584]{1,0:T(8,128)(2,1)}, bf16[16,128]{1,0:T(8,128)(2,1)S(1)}) custom-call(s32[3]{0:T(128)S(1)} %pad_add_fusion.refs_0_.flags_ref, bf16[2048,768]{1,0:T(8,128)(2,1)S(1)} %stack.22.refs_2_.act_ref, bf16[384,512]{1,0:T(8,128)(2,1)S(1)} %square.18.refs_8_.refs_0_, ...), custom_call_target="tpu_custom_call", output_to_operand_aliasing={{0}: (10, {})} | custom-call | flops 10000000 | bytes 100000 | tf_op jit(solution)/shard_map/correct/pallas_call | solution.py:351
  172.2 2.1 %collective-permute-done.45.refs_3_ = bf16[384,512]{1,0:T(8,128)(2,1)S(1)} collective-permute-done((bf16[384,512]{1,0:T(8,128)(2,1)S(1)}, bf16[384,512]{1,0:T(8,128)(2,1)S(1)}, u32[]{:S(2)}, u32[]{:S(2)}) %collective-permute-start.45) | collective-permute-done | bytes 393248 | tf_op jit(solution)/shard_map/ppermute | solution.py:414
  174.3 3.9 %correct.8 = (bf16[2048,3584]{1,0:T(8,128)(2,1)}, bf16[16,128]{1,0:T(8,128)(2,1)S(1)}) custom-call(s32[3]{0:T(128)S(1)} %pad_add_fusion.refs_0_.flags_ref, bf16[2048,768]{1,0:T(8,128)(2,1)S(1)} %stack.22.refs_2_.act_ref, bf16[384,512]{1,0:T(8,128)(2,1)S(1)} %square.20.refs_2_.refs_0_, ...), custom_call_target="tpu_custom_call", output_to_operand_aliasing={{0}: (6, {})} | custom-call | flops 10000000 | bytes 100000 | tf_op jit(solution)/shard_map/correct/pallas_call | solution.py:351
  178.2 2.3 %collective-permute-done.44.refs_3_ = bf16[384,512]{1,0:T(8,128)(2,1)S(1)} collective-permute-done((bf16[384,512]{1,0:T(8,128)(2,1)S(1)}, bf16[384,512]{1,0:T(8,128)(2,1)S(1)}, u32[]{:S(2)}, u32[]{:S(2)}) %collective-permute-start.44) | collective-permute-done | bytes 393248 | tf_op jit(solution)/shard_map/ppermute | solution.py:414
  180.5 4.5 %correct.9 = (bf16[2048,3584]{1,0:T(8,128)(2,1)}, bf16[16,128]{1,0:T(8,128)(2,1)}) custom-call(s32[3]{0:T(128)S(1)} %pad_add_fusion.refs_0_.flags_ref, bf16[2048,768]{1,0:T(8,128)(2,1)S(1)} %stack.22.refs_2_.act_ref, bf16[384,512]{1,0:T(8,128)(2,1)S(1)} %square.21.refs_2_.refs_0_, ...), custom_call_target="tpu_custom_call", output_to_operand_aliasing={{0}: (6, {})} | custom-call | flops 10000000 | bytes 100000 | tf_op jit(solution)/shard_map/correct/pallas_call | solution.py:351
  (96 shorter events, 25.4 us)
Async XLA Ops:
  0.0 6.2 %collective-permute-start = (bf16[192,7168]{1,0:T(8,128)(2,1)}, bf16[192,7168]{1,0:T(8,128)(2,1)S(1)}, u32[]{:S(2)}, u32[]{:S(2)}) collective-permute-start(bf16[192,7168]{1,0:T(8,128)(2,1)} %refs_0_.1), channel_id=1, source_target_pairs={{0,1},{1,0},{2,3},{3,2},{4,5},{5,4},{6,7},{7,6},{8,9},{9,8},{10,11... | collective-permute-start | bytes 8257544 | tf_op jit(solution)/shard_map/ppermute | solution.py:385
  0.5 63.1 %collective-permute-start.7 = (bf16[192,7168]{1,0:T(8,128)(2,1)}, bf16[192,7168]{1,0:T(8,128)(2,1)}, u32[]{:S(2)}, u32[]{:S(2)}) collective-permute-start(bf16[192,7168]{1,0:T(8,128)(2,1)} %refs_0_.1), channel_id=1, source_target_pairs={{0,2},{2,0},{1,3},{3,1},{4,6},{6,4},{5,7},{7,5},{8,10},{10,8},{9,1... | collective-permute-start | bytes 8257544 | tf_op jit(solution)/shard_map/ppermute | solution.py:441
  8.1 5.6 %copy-start.2 = (bf16[768,2048]{1,0:T(8,128)(2,1)S(1)}, bf16[768,2048]{1,0:T(8,128)(2,1)}, u32[]{:S(2)}) copy-start(bf16[768,2048]{1,0:T(8,128)(2,1)} %acts_ref.1) | copy-start | bytes 9437188
  11.5 12.7 %collective-permute-start.5 = (bf16[384,512]{1,0:T(8,128)(2,1)S(1)}, bf16[384,512]{1,0:T(8,128)(2,1)S(1)}, u32[]{:S(2)}, u32[]{:S(2)}) collective-permute-start(bf16[384,512]{1,0:T(8,128)(2,1)S(1)} %get-tuple-element.57.refs_0_), channel_id=1, source_target_pairs={{0,4},{4,0},{8,12},{12,8},{1,5},{5,1},{9,13},{13,9},{2,6},{6,2},{1... | collective-permute-start | bytes 1179656 | tf_op jit(solution)/shard_map/ppermute | solution.py:414
  23.6 4.6 %collective-permute-start.1 = (bf16[384,512]{1,0:T(8,128)(2,1)S(1)}, bf16[384,512]{1,0:T(8,128)(2,1)S(1)}, u32[]{:S(2)}, u32[]{:S(2)}) collective-permute-start(bf16[384,512]{1,0:T(8,128)(2,1)S(1)} %get-tuple-element.62), channel_id=1, source_target_pairs={{0,1},{1,0},{2,3},{3,2},{4,5},{5,4},{6,7},{7,6},{8,9},{9,8},{10,11... | collective-permute-start | bytes 1179656 | tf_op jit(solution)/shard_map/ppermute | solution.py:452
  23.7 9.2 %collective-permute-start.2 = (bf16[384,512]{1,0:T(8,128)(2,1)S(1)}, bf16[384,512]{1,0:T(8,128)(2,1)S(1)}, u32[]{:S(2)}, u32[]{:S(2)}) collective-permute-start(bf16[384,512]{1,0:T(8,128)(2,1)S(1)} %get-tuple-element.63), channel_id=1, source_target_pairs={{0,1},{1,0},{2,3},{3,2},{4,5},{5,4},{6,7},{7,6},{8,9},{9,8},{10,11... | collective-permute-start | bytes 1179656 | tf_op jit(solution)/shard_map/ppermute | solution.py:452
  24.2 10.3 %collective-permute-start.3 = (bf16[384,512]{1,0:T(8,128)(2,1)S(1)}, bf16[384,512]{1,0:T(8,128)(2,1)S(1)}, u32[]{:S(2)}, u32[]{:S(2)}) collective-permute-start(bf16[384,512]{1,0:T(8,128)(2,1)S(1)} %get-tuple-element.64), channel_id=1, source_target_pairs={{0,1},{1,0},{2,3},{3,2},{4,5},{5,4},{6,7},{7,6},{8,9},{9,8},{10,11... | collective-permute-start | bytes 1179656 | tf_op jit(solution)/shard_map/ppermute | solution.py:452
  24.2 11.9 %collective-permute-start.4 = (bf16[384,512]{1,0:T(8,128)(2,1)S(1)}, bf16[384,512]{1,0:T(8,128)(2,1)S(1)}, u32[]{:S(2)}, u32[]{:S(2)}) collective-permute-start(bf16[384,512]{1,0:T(8,128)(2,1)S(1)} %get-tuple-element.65), channel_id=1, source_target_pairs={{0,1},{1,0},{2,3},{3,2},{4,5},{5,4},{6,7},{7,6},{8,9},{9,8},{10,11... | collective-permute-start | bytes 1179656 | tf_op jit(solution)/shard_map/ppermute | solution.py:452
  28.2 12.4 %collective-permute-start.10 = (bf16[384,512]{1,0:T(8,128)(2,1)S(1)}, bf16[384,512]{1,0:T(8,128)(2,1)S(1)}, u32[]{:S(2)}, u32[]{:S(2)}) collective-permute-start(bf16[384,512]{1,0:T(8,128)(2,1)S(1)} %get-tuple-element.68.refs_0_), channel_id=1, source_target_pairs={{0,4},{4,0},{8,12},{12,8},{1,5},{5,1},{9,13},{13,9},{2,6},{6,2},{1... | collective-permute-start | bytes 1179656 | tf_op jit(solution)/shard_map/ppermute | solution.py:414
  32.9 13.3 %collective-permute-start.9 = (bf16[384,512]{1,0:T(8,128)(2,1)S(1)}, bf16[384,512]{1,0:T(8,128)(2,1)S(1)}, u32[]{:S(2)}, u32[]{:S(2)}) collective-permute-start(bf16[384,512]{1,0:T(8,128)(2,1)S(1)} %add.25.refs_8_.refs_0_), channel_id=1, source_target_pairs={{4,8},{8,4},{20,24},{24,20},{0,16},{16,0},{12,28},{28,12},{5,9},{9... | collective-permute-start | bytes 1179656 | tf_op jit(solution)/shard_map/ppermute | solution.py:420
  34.5 14.0 %collective-permute-start.8 = (bf16[384,512]{1,0:T(8,128)(2,1)S(1)}, bf16[384,512]{1,0:T(8,128)(2,1)S(1)}, u32[]{:S(2)}, u32[]{:S(2)}) collective-permute-start(bf16[384,512]{1,0:T(8,128)(2,1)S(1)} %get-tuple-element.69.refs_2_.refs_0_), channel_id=1, source_target_pairs={{0,4},{4,0},{8,12},{12,8},{1,5},{5,1},{9,13},{13,9},{2,6},{6,2},{1... | collective-permute-start | bytes 1179656 | tf_op jit(solution)/shard_map/ppermute | solution.py:414
  41.2 12.8 %collective-permute-start.13 = (bf16[384,512]{1,0:T(8,128)(2,1)S(1)}, bf16[384,512]{1,0:T(8,128)(2,1)S(1)}, u32[]{:S(2)}, u32[]{:S(2)}) collective-permute-start(bf16[384,512]{1,0:T(8,128)(2,1)S(1)} %add.27.refs_0_), channel_id=1, source_target_pairs={{4,8},{8,4},{20,24},{24,20},{0,16},{16,0},{12,28},{28,12},{5,9},{9... | collective-permute-start | bytes 1179656 | tf_op jit(solution)/shard_map/ppermute | solution.py:420
  46.8 7.2 %copy-start = (bf16[384,512]{1,0:T(8,128)(2,1)}, bf16[384,512]{1,0:T(8,128)(2,1)S(1)}, u32[]{:S(2)}) copy-start(bf16[384,512]{1,0:T(8,128)(2,1)S(1)} %square.15.refs_2_.refs_0_) | copy-start | bytes 1179652
  46.8 11.2 %collective-permute-start.12 = (bf16[384,512]{1,0:T(8,128)(2,1)S(1)}, bf16[384,512]{1,0:T(8,128)(2,1)S(1)}, u32[]{:S(2)}, u32[]{:S(2)}) collective-permute-start(bf16[384,512]{1,0:T(8,128)(2,1)S(1)} %square.15.refs_2_.refs_0_), channel_id=1, source_target_pairs={{0,4},{4,0},{8,12},{12,8},{1,5},{5,1},{9,13},{13,9},{2,6},{6,2},{1... | collective-permute-start | bytes 1179656 | tf_op jit(solution)/shard_map/ppermute | solution.py:414
  49.1 13.3 %collective-permute-start.11 = (bf16[384,512]{1,0:T(8,128)(2,1)S(1)}, bf16[384,512]{1,0:T(8,128)(2,1)S(1)}, u32[]{:S(2)}, u32[]{:S(2)}) collective-permute-start(bf16[384,512]{1,0:T(8,128)(2,1)S(1)} %add.28.refs_0_), channel_id=1, source_target_pairs={{4,8},{8,4},{20,24},{24,20},{0,16},{16,0},{12,28},{28,12},{5,9},{9... | collective-permute-start | bytes 1179656 | tf_op jit(solution)/shard_map/ppermute | solution.py:420
  54.6 11.4 %collective-permute-start.22 = (bf16[384,512]{1,0:T(8,128)(2,1)S(1)}, bf16[384,512]{1,0:T(8,128)(2,1)S(1)}, u32[]{:S(2)}, u32[]{:S(2)}) collective-permute-start(bf16[384,512]{1,0:T(8,128)(2,1)S(1)} %square.16.refs_2_.refs_0_), channel_id=1, source_target_pairs={{0,4},{4,0},{8,12},{12,8},{1,5},{5,1},{9,13},{13,9},{2,6},{6,2},{1... | collective-permute-start | bytes 1179656 | tf_op jit(solution)/shard_map/ppermute | solution.py:414
  58.0 4.4 %copy-start.3 = (bf16[384,512]{1,0:T(8,128)(2,1)}, bf16[384,512]{1,0:T(8,128)(2,1)S(1)}, u32[]{:S(2)}) copy-start(bf16[384,512]{1,0:T(8,128)(2,1)S(1)} %collective-permute-done.12.refs_1_) | copy-start | bytes 1179652
  58.6 10.5 %collective-permute-start.21 = (bf16[384,512]{1,0:T(8,128)(2,1)S(1)}, bf16[384,512]{1,0:T(8,128)(2,1)S(1)}, u32[]{:S(2)}, u32[]{:S(2)}) collective-permute-start(bf16[384,512]{1,0:T(8,128)(2,1)S(1)} %add.29.refs_0_), channel_id=1, source_target_pairs={{4,8},{8,4},{20,24},{24,20},{0,16},{16,0},{12,28},{28,12},{5,9},{9... | collective-permute-start | bytes 1179656 | tf_op jit(solution)/shard_map/ppermute | solution.py:420
  65.4 3.7 %collective-permute-start.14 = (bf16[192,1024]{1,0:T(8,128)(2,1)S(1)}, bf16[192,1024]{1,0:T(8,128)(2,1)S(1)}, u32[]{:S(2)}, u32[]{:S(2)}) collective-permute-start(bf16[192,1024]{1,0:T(8,128)(2,1)S(1)} %get-tuple-element.78), channel_id=1, source_target_pairs={{0,1},{1,0},{2,3},{3,2},{4,5},{5,4},{6,7},{7,6},{8,9},{9,8},{10,11... | collective-permute-start | bytes 1179656 | tf_op jit(solution)/shard_map/ppermute | solution.py:467
  65.5 4.2 %collective-permute-start.15 = (bf16[192,1024]{1,0:T(8,128)(2,1)S(1)}, bf16[192,1024]{1,0:T(8,128)(2,1)S(1)}, u32[]{:S(2)}, u32[]{:S(2)}) collective-permute-start(bf16[192,1024]{1,0:T(8,128)(2,1)S(1)} %get-tuple-element.79), channel_id=1, source_target_pairs={{0,1},{1,0},{2,3},{3,2},{4,5},{5,4},{6,7},{7,6},{8,9},{9,8},{10,11... | collective-permute-start | bytes 1179656 | tf_op jit(solution)/shard_map/ppermute | solution.py:467
  66.0 3.8 %collective-permute-start.16 = (bf16[192,1024]{1,0:T(8,128)(2,1)S(1)}, bf16[192,1024]{1,0:T(8,128)(2,1)S(1)}, u32[]{:S(2)}, u32[]{:S(2)}) collective-permute-start(bf16[192,1024]{1,0:T(8,128)(2,1)S(1)} %get-tuple-element.80), channel_id=1, source_target_pairs={{0,1},{1,0},{2,3},{3,2},{4,5},{5,4},{6,7},{7,6},{8,9},{9,8},{10,11... | collective-permute-start | bytes 1179656 | tf_op jit(solution)/shard_map/ppermute | solution.py:467
  66.0 5.1 %collective-permute-start.17 = (bf16[192,1024]{1,0:T(8,128)(2,1)S(1)}, bf16[192,1024]{1,0:T(8,128)(2,1)S(1)}, u32[]{:S(2)}, u32[]{:S(2)}) collective-permute-start(bf16[192,1024]{1,0:T(8,128)(2,1)S(1)} %get-tuple-element.81), channel_id=1, source_target_pairs={{0,1},{1,0},{2,3},{3,2},{4,5},{5,4},{6,7},{7,6},{8,9},{9,8},{10,11... | collective-permute-start | bytes 1179656 | tf_op jit(solution)/shard_map/ppermute | solution.py:467
  69.1 4.1 %collective-permute-start.18 = (bf16[192,1024]{1,0:T(8,128)(2,1)S(1)}, bf16[192,1024]{1,0:T(8,128)(2,1)S(1)}, u32[]{:S(2)}, u32[]{:S(2)}) collective-permute-start(bf16[192,1024]{1,0:T(8,128)(2,1)S(1)} %get-tuple-element.82), channel_id=1, source_target_pairs={{0,1},{1,0},{2,3},{3,2},{4,5},{5,4},{6,7},{7,6},{8,9},{9,8},{10,11... | collective-permute-start | bytes 1179656 | tf_op jit(solution)/shard_map/ppermute | solution.py:467
  69.1 6.3 %collective-permute-start.19 = (bf16[192,1024]{1,0:T(8,128)(2,1)S(1)}, bf16[192,1024]{1,0:T(8,128)(2,1)S(1)}, u32[]{:S(2)}, u32[]{:S(2)}) collective-permute-start(bf16[192,1024]{1,0:T(8,128)(2,1)S(1)} %get-tuple-element.83), channel_id=1, source_target_pairs={{0,1},{1,0},{2,3},{3,2},{4,5},{5,4},{6,7},{7,6},{8,9},{9,8},{10,11... | collective-permute-start | bytes 1179656 | tf_op jit(solution)/shard_map/ppermute | solution.py:467
  69.6 7.6 %collective-permute-start.20 = (bf16[192,1024]{1,0:T(8,128)(2,1)S(1)}, bf16[192,1024]{1,0:T(8,128)(2,1)S(1)}, u32[]{:S(2)}, u32[]{:S(2)}) collective-permute-start(bf16[192,1024]{1,0:T(8,128)(2,1)S(1)} %get-tuple-element.84.refs_2_), channel_id=1, source_target_pairs={{0,1},{1,0},{2,3},{3,2},{4,5},{5,4},{6,7},{7,6},{8,9},{9,8},{10,11... | collective-permute-start | bytes 1179656 | tf_op jit(solution)/shard_map/ppermute | solution.py:467
  69.7 12.9 %collective-permute-start.25 = (bf16[384,512]{1,0:T(8,128)(2,1)S(1)}, bf16[384,512]{1,0:T(8,128)(2,1)S(1)}, u32[]{:S(2)}, u32[]{:S(2)}) collective-permute-start(bf16[384,512]{1,0:T(8,128)(2,1)S(1)} %square.17.refs_0_.refs_4_), channel_id=1, source_target_pairs={{0,4},{4,0},{8,12},{12,8},{1,5},{5,1},{9,13},{13,9},{2,6},{6,2},{1... | collective-permute-start | bytes 1179656 | tf_op jit(solution)/shard_map/ppermute | solution.py:414
  71.1 50.6 %collective-permute-start.6 = (bf16[384,2048]{1,0:T(8,128)(2,1)S(1)}, bf16[384,2048]{1,0:T(8,128)(2,1)S(1)}, u32[]{:S(2)}, u32[]{:S(2)}) collective-permute-start(bf16[384,2048]{1,0:T(8,128)(2,1)S(1)} %add.26.refs_0_), channel_id=1, source_target_pairs={{0,2},{2,0},{1,3},{3,1},{4,6},{6,4},{5,7},{7,5},{8,10},{10,8},{9,1... | collective-permute-start | bytes 4718600 | tf_op jit(solution)/shard_map/ppermute | solution.py:459
  73.3 11.6 %collective-permute-start.24 = (bf16[384,512]{1,0:T(8,128)(2,1)S(1)}, bf16[384,512]{1,0:T(8,128)(2,1)S(1)}, u32[]{:S(2)}, u32[]{:S(2)}) collective-permute-start(bf16[384,512]{1,0:T(8,128)(2,1)S(1)} %add.30.refs_3_.refs_0_), channel_id=1, source_target_pairs={{4,8},{8,4},{20,24},{24,20},{0,16},{16,0},{12,28},{28,12},{5,9},{9... | collective-permute-start | bytes 1179656 | tf_op jit(solution)/shard_map/ppermute | solution.py:420
  75.5 14.6 %collective-permute-start.23 = (bf16[384,512]{1,0:T(8,128)(2,1)S(1)}, bf16[384,512]{1,0:T(8,128)(2,1)S(1)}, u32[]{:S(2)}, u32[]{:S(2)}) collective-permute-start(bf16[384,512]{1,0:T(8,128)(2,1)S(1)} %square.18.refs_8_.refs_0_), channel_id=1, source_target_pairs={{0,4},{4,0},{8,12},{12,8},{1,5},{5,1},{9,13},{13,9},{2,6},{6,2},{1... | collective-permute-start | bytes 1179656 | tf_op jit(solution)/shard_map/ppermute | solution.py:414
  83.2 12.5 %collective-permute-start.26 = (bf16[384,512]{1,0:T(8,128)(2,1)S(1)}, bf16[384,512]{1,0:T(8,128)(2,1)S(1)}, u32[]{:S(2)}, u32[]{:S(2)}) collective-permute-start(bf16[384,512]{1,0:T(8,128)(2,1)S(1)} %add.31.refs_3_.refs_0_), channel_id=1, source_target_pairs={{4,8},{8,4},{20,24},{24,20},{0,16},{16,0},{12,28},{28,12},{5,9},{9... | collective-permute-start | bytes 1179656 | tf_op jit(solution)/shard_map/ppermute | solution.py:420
  85.4 12.7 %collective-permute-start.29 = (bf16[384,512]{1,0:T(8,128)(2,1)S(1)}, bf16[384,512]{1,0:T(8,128)(2,1)S(1)}, u32[]{:S(2)}, u32[]{:S(2)}) collective-permute-start(bf16[384,512]{1,0:T(8,128)(2,1)S(1)} %square.19.refs_2_.refs_4_), channel_id=1, source_target_pairs={{0,4},{4,0},{8,12},{12,8},{1,5},{5,1},{9,13},{13,9},{2,6},{6,2},{1... | collective-permute-start | bytes 1179656 | tf_op jit(solution)/shard_map/ppermute | solution.py:414
  90.7 13.2 %collective-permute-start.28 = (bf16[384,512]{1,0:T(8,128)(2,1)S(1)}, bf16[384,512]{1,0:T(8,128)(2,1)S(1)}, u32[]{:S(2)}, u32[]{:S(2)}) collective-permute-start(bf16[384,512]{1,0:T(8,128)(2,1)S(1)} %add.32.refs_0_), channel_id=1, source_target_pairs={{4,8},{8,4},{20,24},{24,20},{0,16},{16,0},{12,28},{28,12},{5,9},{9... | collective-permute-start | bytes 1179656 | tf_op jit(solution)/shard_map/ppermute | solution.py:420
  96.4 10.1 %collective-permute-start.27 = (bf16[384,512]{1,0:T(8,128)(2,1)S(1)}, bf16[384,512]{1,0:T(8,128)(2,1)S(1)}, u32[]{:S(2)}, u32[]{:S(2)}) collective-permute-start(bf16[384,512]{1,0:T(8,128)(2,1)S(1)} %square.20.refs_2_.refs_0_), channel_id=1, source_target_pairs={{0,4},{4,0},{8,12},{12,8},{1,5},{5,1},{9,13},{13,9},{2,6},{6,2},{1... | collective-permute-start | bytes 1179656 | tf_op jit(solution)/shard_map/ppermute | solution.py:414
  98.8 13.5 %collective-permute-start.32 = (bf16[384,512]{1,0:T(8,128)(2,1)S(1)}, bf16[384,512]{1,0:T(8,128)(2,1)S(1)}, u32[]{:S(2)}, u32[]{:S(2)}) collective-permute-start(bf16[384,512]{1,0:T(8,128)(2,1)S(1)} %add.33.refs_0_), channel_id=1, source_target_pairs={{4,8},{8,4},{20,24},{24,20},{0,16},{16,0},{12,28},{28,12},{5,9},{9... | collective-permute-start | bytes 1179656 | tf_op jit(solution)/shard_map/ppermute | solution.py:420
  104.5 11.3 %collective-permute-start.31 = (bf16[384,512]{1,0:T(8,128)(2,1)S(1)}, bf16[384,512]{1,0:T(8,128)(2,1)S(1)}, u32[]{:S(2)}, u32[]{:S(2)}) collective-permute-start(bf16[384,512]{1,0:T(8,128)(2,1)S(1)} %square.21.refs_2_.refs_0_), channel_id=1, source_target_pairs={{0,4},{4,0},{8,12},{12,8},{1,5},{5,1},{9,13},{13,9},{2,6},{6,2},{1... | collective-permute-start | bytes 1179656 | tf_op jit(solution)/shard_map/ppermute | solution.py:414
  107.1 14.0 %collective-permute-start.30 = (bf16[384,512]{1,0:T(8,128)(2,1)S(1)}, bf16[384,512]{1,0:T(8,128)(2,1)S(1)}, u32[]{:S(2)}, u32[]{:S(2)}) collective-permute-start(bf16[384,512]{1,0:T(8,128)(2,1)S(1)} %add.34.refs_0_), channel_id=1, source_target_pairs={{4,8},{8,4},{20,24},{24,20},{0,16},{16,0},{12,28},{28,12},{5,9},{9... | collective-permute-start | bytes 1179656 | tf_op jit(solution)/shard_map/ppermute | solution.py:420
  112.9 12.6 %collective-permute-start.35 = (bf16[384,512]{1,0:T(8,128)(2,1)S(1)}, bf16[384,512]{1,0:T(8,128)(2,1)S(1)}, u32[]{:S(2)}, u32[]{:S(2)}) collective-permute-start(bf16[384,512]{1,0:T(8,128)(2,1)S(1)} %square.22.refs_2_), channel_id=1, source_target_pairs={{0,4},{4,0},{8,12},{12,8},{1,5},{5,1},{9,13},{13,9},{2,6},{6,2},{1... | collective-permute-start | bytes 1179656 | tf_op jit(solution)/shard_map/ppermute | solution.py:414
  116.4 14.7 %collective-permute-start.38 = (bf16[384,512]{1,0:T(8,128)(2,1)S(1)}, bf16[384,512]{1,0:T(8,128)(2,1)S(1)}, u32[]{:S(2)}, u32[]{:S(2)}) collective-permute-start(bf16[384,512]{1,0:T(8,128)(2,1)S(1)} %add.35.refs_0_), channel_id=1, source_target_pairs={{4,8},{8,4},{20,24},{24,20},{0,16},{16,0},{12,28},{28,12},{5,9},{9... | collective-permute-start | bytes 1179656 | tf_op jit(solution)/shard_map/ppermute | solution.py:420
  122.8 20.4 %collective-permute-start.33 = (bf16[384,1024]{1,0:T(8,128)(2,1)S(1)}, bf16[384,1024]{1,0:T(8,128)(2,1)S(1)}, u32[]{:S(2)}, u32[]{:S(2)}) collective-permute-start(bf16[384,1024]{1,0:T(8,128)(2,1)S(1)} %get-tuple-element.95.refs_0_), channel_id=1, source_target_pairs={{0,1},{1,0},{2,3},{3,2},{4,5},{5,4},{6,7},{7,6},{8,9},{9,8},{10,11... | collective-permute-start | bytes 2359304 | tf_op jit(solution)/shard_map/ppermute | solution.py:481
  122.9 20.3 %collective-permute-start.34 = (bf16[384,1024]{1,0:T(8,128)(2,1)S(1)}, bf16[384,1024]{1,0:T(8,128)(2,1)S(1)}, u32[]{:S(2)}, u32[]{:S(2)}) collective-permute-start(bf16[384,1024]{1,0:T(8,128)(2,1)S(1)} %get-tuple-element.96.refs_2_.refs_1_), channel_id=1, source_target_pairs={{0,1},{1,0},{2,3},{3,2},{4,5},{5,4},{6,7},{7,6},{8,9},{9,8},{10,11... | collective-permute-start | bytes 2359304 | tf_op jit(solution)/shard_map/ppermute | solution.py:481
  123.4 12.0 %collective-permute-start.37 = (bf16[384,512]{1,0:T(8,128)(2,1)S(1)}, bf16[384,512]{1,0:T(8,128)(2,1)S(1)}, u32[]{:S(2)}, u32[]{:S(2)}) collective-permute-start(bf16[384,512]{1,0:T(8,128)(2,1)S(1)} %square.23.refs_2_), channel_id=1, source_target_pairs={{0,4},{4,0},{8,12},{12,8},{1,5},{5,1},{9,13},{13,9},{2,6},{6,2},{1... | collective-permute-start | bytes 1179656 | tf_op jit(solution)/shard_map/ppermute | solution.py:414
  126.1 14.9 %collective-permute-start.36 = (bf16[384,512]{1,0:T(8,128)(2,1)S(1)}, bf16[384,512]{1,0:T(8,128)(2,1)S(1)}, u32[]{:S(2)}, u32[]{:S(2)}) collective-permute-start(bf16[384,512]{1,0:T(8,128)(2,1)S(1)} %add.36.refs_0_), channel_id=1, source_target_pairs={{4,8},{8,4},{20,24},{24,20},{0,16},{16,0},{12,28},{28,12},{5,9},{9... | collective-permute-start | bytes 1179656 | tf_op jit(solution)/shard_map/ppermute | solution.py:420
  132.0 12.7 %collective-permute-start.41 = (bf16[384,512]{1,0:T(8,128)(2,1)S(1)}, bf16[384,512]{1,0:T(8,128)(2,1)S(1)}, u32[]{:S(2)}, u32[]{:S(2)}) collective-permute-start(bf16[384,512]{1,0:T(8,128)(2,1)S(1)} %square.25.refs_2_.refs_6_), channel_id=1, source_target_pairs={{0,4},{4,0},{8,12},{12,8},{1,5},{5,1},{9,13},{13,9},{2,6},{6,2},{1... | collective-permute-start | bytes 1179656 | tf_op jit(solution)/shard_map/ppermute | solution.py:414
  136.0 10.1 %collective-permute-start.40 = (bf16[384,512]{1,0:T(8,128)(2,1)S(1)}, bf16[384,512]{1,0:T(8,128)(2,1)S(1)}, u32[]{:S(2)}, u32[]{:S(2)}) collective-permute-start(bf16[384,512]{1,0:T(8,128)(2,1)S(1)} %add.37.refs_0_), channel_id=1, source_target_pairs={{4,8},{8,4},{20,24},{24,20},{0,16},{16,0},{12,28},{28,12},{5,9},{9... | collective-permute-start | bytes 1179656 | tf_op jit(solution)/shard_map/ppermute | solution.py:420
  141.0 5.8 %copy-start.1 = (bf16[384,512]{1,0:T(8,128)(2,1)S(1)}, bf16[384,512]{1,0:T(8,128)(2,1)}, u32[]{:S(2)}) copy-start(bf16[384,512]{1,0:T(8,128)(2,1)} %copy-done) | copy-start | bytes 1179652
  141.0 5.8 %copy-start.4 = (bf16[384,512]{1,0:T(8,128)(2,1)S(1)}, bf16[384,512]{1,0:T(8,128)(2,1)}, u32[]{:S(2)}) copy-start(bf16[384,512]{1,0:T(8,128)(2,1)} %copy-done.3) | copy-start | bytes 1179652
  141.6 10.1 %collective-permute-start.39 = (bf16[384,512]{1,0:T(8,128)(2,1)S(1)}, bf16[384,512]{1,0:T(8,128)(2,1)S(1)}, u32[]{:S(2)}, u32[]{:S(2)}) collective-permute-start(bf16[384,512]{1,0:T(8,128)(2,1)S(1)} %square.26.refs_4_.refs_2_), channel_id=1, source_target_pairs={{0,4},{4,0},{8,12},{12,8},{1,5},{5,1},{9,13},{13,9},{2,6},{6,2},{1... | collective-permute-start | bytes 1179656 | tf_op jit(solution)/shard_map/ppermute | solution.py:414
  145.3 10.5 %collective-permute-start.43 = (bf16[384,512]{1,0:T(8,128)(2,1)S(1)}, bf16[384,512]{1,0:T(8,128)(2,1)S(1)}, u32[]{:S(2)}, u32[]{:S(2)}) collective-permute-start(bf16[384,512]{1,0:T(8,128)(2,1)S(1)} %add.38.refs_2_.refs_0_), channel_id=1, source_target_pairs={{4,8},{8,4},{20,24},{24,20},{0,16},{16,0},{12,28},{28,12},{5,9},{9... | collective-permute-start | bytes 1179656 | tf_op jit(solution)/shard_map/ppermute | solution.py:420
  152.3 11.6 %collective-permute-start.42 = (bf16[384,512]{1,0:T(8,128)(2,1)S(1)}, bf16[384,512]{1,0:T(8,128)(2,1)S(1)}, u32[]{:S(2)}, u32[]{:S(2)}) collective-permute-start(bf16[384,512]{1,0:T(8,128)(2,1)S(1)} %add.39.refs_2_.refs_0_), channel_id=1, source_target_pairs={{4,8},{8,4},{20,24},{24,20},{0,16},{16,0},{12,28},{28,12},{5,9},{9... | collective-permute-start | bytes 1179656 | tf_op jit(solution)/shard_map/ppermute | solution.py:420
  153.9 12.1 %collective-permute-start.46 = (bf16[384,512]{1,0:T(8,128)(2,1)S(1)}, bf16[384,512]{1,0:T(8,128)(2,1)S(1)}, u32[]{:S(2)}, u32[]{:S(2)}) collective-permute-start(bf16[384,512]{1,0:T(8,128)(2,1)S(1)} %square.27.refs_4_.refs_6_), channel_id=1, source_target_pairs={{0,4},{4,0},{8,12},{12,8},{1,5},{5,1},{9,13},{13,9},{2,6},{6,2},{1... | collective-permute-start | bytes 1179656 | tf_op jit(solution)/shard_map/ppermute | solution.py:414
  156.4 17.9 %collective-permute-start.45 = (bf16[384,512]{1,0:T(8,128)(2,1)S(1)}, bf16[384,512]{1,0:T(8,128)(2,1)S(1)}, u32[]{:S(2)}, u32[]{:S(2)}) collective-permute-start(bf16[384,512]{1,0:T(8,128)(2,1)S(1)} %square.28.refs_9_.refs_2_), channel_id=1, source_target_pairs={{0,4},{4,0},{8,12},{12,8},{1,5},{5,1},{9,13},{13,9},{2,6},{6,2},{1... | collective-permute-start | bytes 1179656 | tf_op jit(solution)/shard_map/ppermute | solution.py:414
  164.6 15.9 %collective-permute-start.44 = (bf16[384,512]{1,0:T(8,128)(2,1)S(1)}, bf16[384,512]{1,0:T(8,128)(2,1)S(1)}, u32[]{:S(2)}, u32[]{:S(2)}) collective-permute-start(bf16[384,512]{1,0:T(8,128)(2,1)S(1)} %square.29.refs_9_.refs_2_), channel_id=1, source_target_pairs={{0,4},{4,0},{8,12},{12,8},{1,5},{5,1},{9,13},{13,9},{2,6},{6,2},{1... | collective-permute-start | bytes 1179656 | tf_op jit(solution)/shard_map/ppermute | solution.py:414
